TPU v7x, 1024 devices: a whole 8x8x8 slice. The times are simulated.
1024 devices in a mesh: dp: 16 (over x, y_lo), expert: 64 (over z, y_hi, core).
Axes of the slice: x: 8, y: 8 (y_hi: 4, y_lo: 2; y = y_hi * 2 + y_lo), z: 8, core: 2. Of those that a mesh axis runs over, the one named last changes fastest.
Arguments:
- tokens: bfloat16 [2, 4096, 7168], P(None, 'expert', 'dp'), may hold values from -6 to 6
- out_grad: bfloat16 [2, 4096, 7168], P(None, 'expert', 'dp'), may hold values from -6 to 6
- expert_ids: int32 [2, 4096, 1], P(None, 'expert'), may hold values from 0 to 15; in each aligned block of 64 rows (0 to 63, 64 to 127, ..., all dimensions but the last counted through in order) at most 8 rows name the same one
- gate_weights: float32 [2, 4096, 1], P(None, 'expert'), may hold values from 0.1 to 1
- w_up: bfloat16 [7168, 32768], P('dp', 'expert'), may hold values from -0.0625 to 0.0625
- w_down: bfloat16 [32768, 7168], P('expert', 'dp'), may hold values from -0.125 to 0.125
Outputs:
- mixed: bfloat16 [2, 4096, 7168], P(None, 'expert', 'dp')
- token_grad: bfloat16 [2, 4096, 7168], P(None, 'expert', 'dp')
- grad_up: bfloat16 [7168, 32768], P('dp', 'expert')
- grad_down: bfloat16 [32768, 7168], P('expert', 'dp')
Inputs may be any that keep to these rules, and one draw needn't show every extreme that they name: `expert_ids`: within each micro-batch, the 64 tokens of one index of the expert axis (aligned blocks of 64 rows) name no expert more than 8 times; some expert is named exactly 8 times in some block.
All inputs are finite; a program needn't handle non-finite values.
Results may differ from a plain program's by a relative error of at most 0.03.
Values may be sent and summed in bfloat16 or wider, within the bound.
No kernel may reach another device: no remote copies, remote signals or barrier semaphores. Data moves between devices by JAX's collectives and lax.ppermute only.
A program may use at most 64 MiB of HBM per device.

v0:
```python
import jax
import jax.numpy as jnp
from jax import lax
from jax.sharding import PartitionSpec as P

FF = 2048


def silu_grad(preact):
    logistic = jax.nn.sigmoid(preact)
    return logistic * (1.0 + preact * (1.0 - logistic))


def forward_step(summed, stored):
    return (jax.nn.silu(summed).astype(jnp.bfloat16), summed)


def backward_step(summed, stored):
    return ((summed * silu_grad(stored)).astype(jnp.bfloat16), stored)


def reduce_then(partial_term, stored, stepper):
    portion = lax.psum_scatter(
        partial_term.astype(jnp.bfloat16), "dp", scatter_dimension=0, tiled=True
    ).astype(jnp.float32)
    share_value, kept_value = stepper(portion, stored)
    return (lax.all_gather(share_value, "dp", axis=0, tiled=True), kept_value)


def on_device(tokens, out_grad, expert_ids, gate_weights, w_up, w_down):
    micro_count, token_count, features = tokens.shape
    hidden_cols = w_up.shape[1]
    columns = lax.axis_size("expert")
    groups_per = FF // hidden_cols
    experts = columns // groups_per
    capacity = 2 * token_count // experts
    slot_count = experts * capacity
    expert_range = jnp.arange(experts, dtype=jnp.int32)
    slot_range = jnp.arange(slot_count, dtype=jnp.int32)
    grad_in = jnp.zeros((features, hidden_cols), jnp.float32)
    grad_out = jnp.zeros((hidden_cols, features), jnp.float32)
    contract_last = (((1,), (1,)), ((), ()))
    contract_first = (((0,), (0,)), ((), ()))
    mixed_list = []
    token_list = []
    for micro_index in range(micro_count):
        routing = expert_ids[micro_index, :, 0]
        choose = (routing[:, None] == expert_range[None, :]).astype(jnp.int32)
        position = jnp.sum((jnp.cumsum(choose, axis=0) - 1) * choose, axis=1)
        slot_table = (routing * capacity + position)[:, None] == slot_range[None, :]
        table_low = slot_table.astype(jnp.bfloat16)
        scaled = (gate_weights[micro_index] * out_grad[micro_index].astype(jnp.float32)).astype(
            jnp.bfloat16
        )
        packed_in = jnp.dot(
            table_low.T, tokens[micro_index], preferred_element_type=jnp.float32
        ).astype(jnp.bfloat16)
        packed_grad = jnp.dot(table_low.T, scaled, preferred_element_type=jnp.float32).astype(
            jnp.bfloat16
        )
        outgoing_in = jnp.repeat(
            packed_in.reshape(experts, capacity * features), groups_per, axis=0
        )
        outgoing_grad = jnp.repeat(
            packed_grad.reshape(experts, capacity * features), groups_per, axis=0
        )
        arrived_in, arrived_grad = (
            lax.all_to_all(outgoing_in, "expert", split_axis=0, concat_axis=0, tiled=True),
            lax.all_to_all(outgoing_grad, "expert", split_axis=0, concat_axis=0, tiled=True),
        )
        rows_in = arrived_in.reshape(columns * capacity, features)
        rows_grad = arrived_grad.reshape(columns * capacity, features)
        partial_pre = jnp.dot(rows_in, w_up, preferred_element_type=jnp.float32)
        hidden, stored = reduce_then(partial_pre, None, forward_step)
        mixed_part = jnp.dot(hidden, w_down, preferred_element_type=jnp.float32).astype(
            jnp.bfloat16
        )
        back_term = lax.dot_general(
            rows_grad, w_down, contract_last, preferred_element_type=jnp.float32
        )
        preact_grad, unused = reduce_then(back_term, stored, backward_step)
        token_part = lax.dot_general(
            preact_grad, w_up, contract_last, preferred_element_type=jnp.float32
        ).astype(jnp.bfloat16)
        grad_in = grad_in + lax.dot_general(
            rows_in, preact_grad, contract_first, preferred_element_type=jnp.float32
        )
        grad_out = grad_out + lax.dot_general(
            hidden, rows_grad, contract_first, preferred_element_type=jnp.float32
        )
        came_mixed, came_token = (
            lax.all_to_all(
                mixed_part.reshape(columns, capacity * features),
                "expert",
                split_axis=0,
                concat_axis=0,
                tiled=True,
            ),
            lax.all_to_all(
                token_part.reshape(columns, capacity * features),
                "expert",
                split_axis=0,
                concat_axis=0,
                tiled=True,
            ),
        )
        summed_mixed = jnp.sum(
            came_mixed.astype(jnp.float32).reshape(experts, groups_per, capacity * features), axis=1
        ).reshape(slot_count, features)
        summed_token = jnp.sum(
            came_token.astype(jnp.float32).reshape(experts, groups_per, capacity * features), axis=1
        ).reshape(slot_count, features)
        table_high = slot_table.astype(jnp.float32)
        token_mixed = jnp.dot(
            table_high,
            summed_mixed,
            precision=lax.Precision.HIGHEST,
            preferred_element_type=jnp.float32,
        )
        token_back = jnp.dot(
            table_high,
            summed_token,
            precision=lax.Precision.HIGHEST,
            preferred_element_type=jnp.float32,
        )
        mixed_list.append((gate_weights[micro_index] * token_mixed).astype(jnp.bfloat16))
        token_list.append(token_back.astype(jnp.bfloat16))
    return (
        jnp.stack(mixed_list),
        jnp.stack(token_list),
        grad_in.astype(jnp.bfloat16),
        grad_out.astype(jnp.bfloat16),
    )


def solution(mesh):
    in_specs = (
        P(None, "expert", "dp"),
        P(None, "expert", "dp"),
        P(None, "expert", None),
        P(None, "expert", None),
        P("dp", "expert"),
        P("expert", "dp"),
    )
    out_specs = (
        P(None, "expert", "dp"),
        P(None, "expert", "dp"),
        P("dp", "expert"),
        P("expert", "dp"),
    )
    return jax.shard_map(
        on_device, mesh=mesh, in_specs=in_specs, out_specs=out_specs, check_vma=False
    )
```

profile of v0, /device:TPU:1, one launch (start us, length us, event | category | flops | bytes accessed | tf_op | source)
XLA Modules:
  0.0 562.6 jit_solution(8991009960789358181)
XLA Ops:
  10.7 3.4 reduce.12
  15.0 24.6 %all-to-all-start.2 = ((bf16[64,2,1792]{2,1,0:T(2,128)(2,1)}), bf16[64,2,1792]{2,1,0:T(2,128)(2,1)S(1)}, u32[]{:S(2)}, u32[]{:S(2)}) async-start(bf16[64,2,1792]{2,1,0:T(2,128)(2,1)} %reshape.146), calls=%async_computation.3 | async-start | bytes 917504 | tf_op jit(solution)/shard_map/all_to_all | solution.py:68
  40.6 3.4 reduce.13
  44.9 13.7 %all-to-all-done.2 = bf16[64,2,1792]{2,1,0:T(2,128)(2,1)S(1)} async-done(((bf16[64,2,1792]{2,1,0:T(2,128)(2,1)}), bf16[64,2,1792]{2,1,0:T(2,128)(2,1)S(1)}, u32[]{:S(2)}, u32[]{:S(2)}) %all-to-all-start.2) | async-done | bytes 458784 | tf_op jit(solution)/shard_map/all_to_all | solution.py:68
  58.7 5.6 all-to-all-start.6
  65.0 2.7 reduce.2
  68.4 1.2 convolution_convert_fusion.2
  70.6 3.4 reduce.15
  74.9 8.5 %all-to-all-done.6 = bf16[64,2,1792]{2,1,0:T(2,128)(2,1)S(1)} async-done(((bf16[64,2,1792]{2,1,0:T(2,128)(2,1)}), bf16[64,2,1792]{2,1,0:T(2,128)(2,1)S(1)}, u32[]{:S(2)}, u32[]{:S(2)}) %all-to-all-start.6) | async-done | bytes 458784 | tf_op jit(solution)/shard_map/all_to_all | solution.py:69
  83.4 5.7 %all-to-all-start = ((bf16[64,2,1792]{2,1,0:T(2,128)(2,1)}), bf16[64,2,1792]{2,1,0:T(2,128)(2,1)}, u32[]{:S(2)}, u32[]{:S(2)}) async-start(bf16[64,2,1792]{2,1,0:T(2,128)(2,1)} %reshape.150), calls=%async_computation | async-start | bytes 917504 | tf_op jit(solution)/shard_map/all_to_all | solution.py:68
  90.1 2.7 reduce.6
  93.9 1.2 convolution_convert_fusion
  96.1 3.4 reduce.16
  100.4 9.2 %all-to-all-done = bf16[64,2,1792]{2,1,0:T(2,128)(2,1)} async-done(((bf16[64,2,1792]{2,1,0:T(2,128)(2,1)}), bf16[64,2,1792]{2,1,0:T(2,128)(2,1)}, u32[]{:S(2)}, u32[]{:S(2)}) %all-to-all-start) | async-done | bytes 458784 | tf_op jit(solution)/shard_map/all_to_all | solution.py:68
  109.7 5.7 %all-to-all-start.4 = ((bf16[64,2,1792]{2,1,0:T(2,128)(2,1)}), bf16[64,2,1792]{2,1,0:T(2,128)(2,1)}, u32[]{:S(2)}, u32[]{:S(2)}) async-start(bf16[64,2,1792]{2,1,0:T(2,128)(2,1)} %reshape.158), calls=%async_computation.6 | async-start | bytes 917504 | tf_op jit(solution)/shard_map/all_to_all | solution.py:69
  115.6 2.9 reshape.151
  118.5 2.7 reduce
  121.9 1.2 convolution_convert_fusion.3
  123.2 12.7 %all-to-all-done.4 = bf16[64,2,1792]{2,1,0:T(2,128)(2,1)} async-done(((bf16[64,2,1792]{2,1,0:T(2,128)(2,1)}), bf16[64,2,1792]{2,1,0:T(2,128)(2,1)}, u32[]{:S(2)}, u32[]{:S(2)}) %all-to-all-start.4) | async-done | bytes 458784 | tf_op jit(solution)/shard_map/all_to_all | solution.py:69
  135.9 2.9 reshape.159
  138.8 3.5 reduce.4
  142.3 1.6 reshape.127
  144.0 1.2 convolution_convert_fusion.1
  145.3 68.1 %reduce-scatter.11.cloned.1.call-done = bf16[32,512]{1,0:T(8,128)(2,1)} async-done(((bf16[512,512]{1,0:T(8,128)(2,1)}), bf16[32,512]{1,0:T(8,128)(2,1)}) %reduce-scatter.11.cloned.1.call-update) | async-done | bytes 32784 | tf_op jit(solution)/shard_map/reduce_scatter | solution.py:23
  213.4 1.4 fusion.25
  214.8 26.5 %all_gather.15 = bf16[512,512]{1,0:T(8,128)(2,1)S(1)} all-gather(bf16[32,512]{1,0:T(8,128)(2,1)S(1)} %get-tuple-element.6), channel_id=1, replica_groups=mesh['dp'=16,'expert'=64] {'dp'}, dimensions={0}, use_global_device_ids=true | all-gather | bytes 557056 | tf_op jit(solution)/shard_map/all_gather | solution.py:27
  242.4 1.2 copy.44
  243.7 2.0 all_to_all.71
  245.7 4.4 reduce.18
  250.9 32.6 %all-to-all-start.7 = ((bf16[64,2,1792]{2,1,0:T(2,128)(2,1)}), bf16[64,2,1792]{2,1,0:T(2,128)(2,1)}, u32[]{:S(2)}, u32[]{:S(2)}) async-start(bf16[64,2,1792]{2,1,0:T(2,128)(2,1)} %reshape.156), calls=%async_computation.11 | async-start | bytes 917504 | tf_op jit(solution)/shard_map/all_to_all | solution.py:99
  283.6 35.4 %all_gather.13 = bf16[512,512]{1,0:T(8,128)(2,1)S(1)} all-gather(bf16[32,512]{1,0:T(8,128)(2,1)} %get-tuple-element.7), channel_id=1, replica_groups=mesh['dp'=16,'expert'=64] {'dp'}, dimensions={0}, use_global_device_ids=true | all-gather | bytes 557056 | tf_op jit(solution)/shard_map/all_gather | solution.py:27
  319.0 1.2 convolution_convert_fusion.6
  320.2 2.0 copy.36
  322.2 3.6 all_to_all.67
  325.8 5.2 reduce.14
  330.9 1.9 reshape.148
  332.8 37.9 %reduce-scatter.9.cloned.1.call-done = bf16[32,512]{1,0:T(8,128)(2,1)} async-done(((bf16[512,512]{1,0:T(8,128)(2,1)}), bf16[32,512]{1,0:T(8,128)(2,1)}) %reduce-scatter.9.cloned.1.call-update) | async-done | bytes 32784 | tf_op jit(solution)/shard_map/reduce_scatter | solution.py:23
  370.7 1.4 fusion.17
  372.2 24.5 %all-to-all-start.3 = ((bf16[64,2,1792]{2,1,0:T(2,128)(2,1)}), bf16[64,2,1792]{2,1,0:T(2,128)(2,1)}, u32[]{:S(2)}, u32[]{:S(2)}) async-start(bf16[64,2,1792]{2,1,0:T(2,128)(2,1)} %reshape.148), calls=%async_computation.5 | async-start | bytes 917504 | tf_op jit(solution)/shard_map/all_to_all | solution.py:92
  396.6 32.8 %all_gather.14 = bf16[512,512]{1,0:T(8,128)(2,1)S(1)} all-gather(bf16[32,512]{1,0:T(8,128)(2,1)} %get-tuple-element.4), channel_id=1, replica_groups=mesh['dp'=16,'expert'=64] {'dp'}, dimensions={0}, use_global_device_ids=true | all-gather | bytes 557056 | tf_op jit(solution)/shard_map/all_gather | solution.py:27
  430.3 1.2 convolution_convert_fusion.5
  431.5 2.0 copy.40
  433.5 3.6 all_to_all.69
  437.1 5.2 reduce.19
  442.3 1.9 reshape.160
  444.2 29.8 %all_gather.12 = bf16[512,512]{1,0:T(8,128)(2,1)} all-gather(bf16[32,512]{1,0:T(8,128)(2,1)} %get-tuple-element.5), channel_id=1, replica_groups=mesh['dp'=16,'expert'=64] {'dp'}, dimensions={0}, use_global_device_ids=true | all-gather | bytes 557056 | tf_op jit(solution)/shard_map/all_gather | solution.py:27
  474.0 1.4 fusion.48
  475.4 25.8 %all-to-all-start.5 = ((bf16[64,2,1792]{2,1,0:T(2,128)(2,1)}), bf16[64,2,1792]{2,1,0:T(2,128)(2,1)}, u32[]{:S(2)}, u32[]{:S(2)}) async-start(bf16[64,2,1792]{2,1,0:T(2,128)(2,1)} %reshape.160), calls=%async_computation.8 | async-start | bytes 917504 | tf_op jit(solution)/shard_map/all_to_all | solution.py:99
  501.2 1.2 convolution_convert_fusion.7
  502.4 2.0 copy.32
  504.4 2.4 all_to_all.65
  506.8 4.2 reduce.17
  511.0 1.9 reshape.152
  513.0 1.6 fusion.49
  514.6 1.2 fusion
  515.8 1.2 fusion.1
  517.0 2.9 reshape.157
  519.9 13.0 %all-to-all-start.1 = ((bf16[64,2,1792]{2,1,0:T(2,128)(2,1)}), bf16[64,2,1792]{2,1,0:T(2,128)(2,1)S(1)}, u32[]{:S(2)}, u32[]{:S(2)}) async-start(bf16[64,2,1792]{2,1,0:T(2,128)(2,1)} %reshape.152), calls=%async_computation.2 | async-start | bytes 917504 | tf_op jit(solution)/shard_map/all_to_all | solution.py:92
  532.9 2.6 convert_reduce_fusion
  536.4 2.9 reshape.149
  539.3 2.6 convert_reduce_fusion.2
  542.9 3.1 reshape.161
  546.0 2.6 convert_reduce_fusion.1
  550.7 2.6 convert_reduce_fusion.3
  (97 shorter events, 23.4 us)
Async XLA Ops:
  7.2 61.2 %copy-start = (bf16[448,512]{1,0:T(8,128)(2,1)S(1)}, bf16[448,512]{1,0:T(8,128)(2,1)}, u32[]{:S(2)}) copy-start(bf16[448,512]{1,0:T(8,128)(2,1)} %param.10) | copy-start | bytes 1376260
  7.9 1.2 copy-start.8
  8.4 0.7 copy-start.9
  15.0 24.6 %copy-start.10 = (f32[2,64,1]{1,2,0:T(1,128)S(1)}, f32[2,64,1]{1,2,0:T(1,128)}, u32[]{:S(2)}) copy-start(f32[2,64,1]{1,2,0:T(1,128)} %param.9) | copy-start | bytes 1540
  15.0 24.6 %copy-start.11 = (bf16[2,64,448]{2,1,0:T(8,128)(2,1)S(1)}, bf16[2,64,448]{2,1,0:T(8,128)(2,1)}, u32[]{:S(2)}) copy-start(bf16[2,64,448]{2,1,0:T(8,128)(2,1)} %param.7) | copy-start | bytes 344068
  15.0 43.7 %all-to-all-start.2 = ((bf16[64,2,1792]{2,1,0:T(2,128)(2,1)}), bf16[64,2,1792]{2,1,0:T(2,128)(2,1)S(1)}, u32[]{:S(2)}, u32[]{:S(2)}) async-start(bf16[64,2,1792]{2,1,0:T(2,128)(2,1)} %reshape.146), calls=%async_computation.3 | async-start | bytes 917504 | tf_op jit(solution)/shard_map/all_to_all | solution.py:68
  58.7 24.7 %all-to-all-start.6 = ((bf16[64,2,1792]{2,1,0:T(2,128)(2,1)}), bf16[64,2,1792]{2,1,0:T(2,128)(2,1)S(1)}, u32[]{:S(2)}, u32[]{:S(2)}) async-start(bf16[64,2,1792]{2,1,0:T(2,128)(2,1)} %reshape.154), calls=%async_computation.9 | async-start | bytes 917504 | tf_op jit(solution)/shard_map/all_to_all | solution.py:69
  64.3 81.0 %reduce-scatter.7.cloned.1.call-start = ((), (), s32[]{:S(2)}) async-start(), calls=%async_computation.13 | async-start | bytes 557056 | tf_op jit(solution)/shard_map/reduce_scatter | solution.py:23
  83.4 26.2 %all-to-all-start = ((bf16[64,2,1792]{2,1,0:T(2,128)(2,1)}), bf16[64,2,1792]{2,1,0:T(2,128)(2,1)}, u32[]{:S(2)}, u32[]{:S(2)}) async-start(bf16[64,2,1792]{2,1,0:T(2,128)(2,1)} %reshape.150), calls=%async_computation | async-start | bytes 917504 | tf_op jit(solution)/shard_map/all_to_all | solution.py:68
  89.1 124.2 %reduce-scatter.11.cloned.1.call-start = ((), (), s32[]{:S(2)}) async-start(), calls=%async_computation.15 | async-start | bytes 557056 | tf_op jit(solution)/shard_map/reduce_scatter | solution.py:23
  92.8 1.0 copy-start.1
  109.7 26.3 %all-to-all-start.4 = ((bf16[64,2,1792]{2,1,0:T(2,128)(2,1)}), bf16[64,2,1792]{2,1,0:T(2,128)(2,1)}, u32[]{:S(2)}, u32[]{:S(2)}) async-start(bf16[64,2,1792]{2,1,0:T(2,128)(2,1)} %reshape.158), calls=%async_computation.6 | async-start | bytes 917504 | tf_op jit(solution)/shard_map/all_to_all | solution.py:69
  115.4 217.4 %reduce-scatter.5.cloned.1.call-start = ((), (), s32[]{:S(2)}) async-start(), calls=%async_computation.12 | async-start | bytes 557056 | tf_op jit(solution)/shard_map/reduce_scatter | solution.py:23
  123.1 247.6 %reduce-scatter.9.cloned.1.call-start = ((), (), s32[]{:S(2)}) async-start(), calls=%async_computation.14 | async-start | bytes 557056 | tf_op jit(solution)/shard_map/reduce_scatter | solution.py:23
  144.0 1.3 copy-start.2
  250.9 121.3 %all-to-all-start.7 = ((bf16[64,2,1792]{2,1,0:T(2,128)(2,1)}), bf16[64,2,1792]{2,1,0:T(2,128)(2,1)}, u32[]{:S(2)}, u32[]{:S(2)}) async-start(bf16[64,2,1792]{2,1,0:T(2,128)(2,1)} %reshape.156), calls=%async_computation.11 | async-start | bytes 917504 | tf_op jit(solution)/shard_map/all_to_all | solution.py:99
  372.2 103.2 %all-to-all-start.3 = ((bf16[64,2,1792]{2,1,0:T(2,128)(2,1)}), bf16[64,2,1792]{2,1,0:T(2,128)(2,1)}, u32[]{:S(2)}, u32[]{:S(2)}) async-start(bf16[64,2,1792]{2,1,0:T(2,128)(2,1)} %reshape.148), calls=%async_computation.5 | async-start | bytes 917504 | tf_op jit(solution)/shard_map/all_to_all | solution.py:92
  429.5 0.8 copy-start.5
  444.2 29.8 %copy-start.6 = (bf16[512,512]{1,0:T(8,128)(2,1)S(1)}, bf16[512,512]{1,0:T(8,128)(2,1)}, u32[]{:S(2)}) copy-start(bf16[512,512]{1,0:T(8,128)(2,1)} %copy-done.5) | copy-start | bytes 1572868
  475.4 25.8 %copy-start.4 = (bf16[512,512]{1,0:T(8,128)(2,1)S(1)}, bf16[512,512]{1,0:T(8,128)(2,1)}, u32[]{:S(2)}) copy-start(bf16[512,512]{1,0:T(8,128)(2,1)} %all_gather.12) | copy-start | bytes 1572868
  475.4 44.5 %all-to-all-start.5 = ((bf16[64,2,1792]{2,1,0:T(2,128)(2,1)}), bf16[64,2,1792]{2,1,0:T(2,128)(2,1)}, u32[]{:S(2)}, u32[]{:S(2)}) async-start(bf16[64,2,1792]{2,1,0:T(2,128)(2,1)} %reshape.160), calls=%async_computation.8 | async-start | bytes 917504 | tf_op jit(solution)/shard_map/all_to_all | solution.py:99
  511.0 2.0 copy-start.3
  513.0 1.6 copy-start.7
  519.9 30.4 %all-to-all-start.1 = ((bf16[64,2,1792]{2,1,0:T(2,128)(2,1)}), bf16[64,2,1792]{2,1,0:T(2,128)(2,1)S(1)}, u32[]{:S(2)}, u32[]{:S(2)}) async-start(bf16[64,2,1792]{2,1,0:T(2,128)(2,1)} %reshape.152), calls=%async_computation.2 | async-start | bytes 917504 | tf_op jit(solution)/shard_map/all_to_all | solution.py:92
Sparse Core Ops, SparseCore 0:
  69.8 68.3 reduce-scatter.6
  142.0 71.3 reduce-scatter.10
  216.7 76.5 reduce-scatter.4
  296.9 73.7 reduce-scatter.8
where the time goes:
time: 573 us; the launch traced here: 563 us
  waiting for transfers between devices  150 us (26%)
  starting transfers between devices  139 us (24%)
  blocking collectives  125 us (22%)
  other arithmetic  61.6 us (11%)
  local copies, waits for them, and re-layouts  55.7 us (10%)
  matrix products  17.3 us (3%)
  between operations  14.6 us (3%)
    all_gather x4, blocking collectives, reduce_then(): return (lax.all_gather(share_value, 'dp', axis=0, tiled=True), kept_value)  125 us
    reduce_scatter x4, waiting for transfers between devices, reduce_then(): lax.psum_scatter(partial_term.astype(jnp.bfloat16), 'dp', scatter_dimensi...  106 us
    all_to_all x2, starting transfers between devices, on_device(): lax.all_to_all(token_part.reshape(columns, capacity * features), 'expert'...  58.4 us
    all_to_all x2, starting transfers between devices, on_device(): lax.all_to_all(mixed_part.reshape(columns, capacity * features), 'expert'...  37.5 us
    all_to_all x2, starting transfers between devices, on_device(): lax.all_to_all(outgoing_in, 'expert', split_axis=0, concat_axis=0, tiled=...  30.3 us
    unnamed x40, local copies, waits for them, and re-layouts  27.8 us
    all_to_all x2, waiting for transfers between devices, on_device(): lax.all_to_all(outgoing_in, 'expert', split_axis=0, concat_axis=0, tiled=...  23 us
    all_to_all x2, waiting for transfers between devices, on_device(): lax.all_to_all(outgoing_grad, 'expert', split_axis=0, concat_axis=0, tile...  21.2 us
  transfers between devices with their start and end apart: 12, of which 6 were waited for; matrix products, arithmetic and copies ran while one was open for 19% of the time, Pallas kernels for 0%

commit v1 on v0

v1 whole, which is shorter than its diff:
```python
import jax
import jax.numpy as jnp
from jax import lax
from jax.sharding import PartitionSpec as P

FF = 2048
GROUPS = ((0, 1),)


def silu_grad(preact):
    logistic = jax.nn.sigmoid(preact)
    return logistic * (1.0 + preact * (1.0 - logistic))


def on_device(tokens, out_grad, expert_ids, gate_weights, w_up, w_down):
    micro_count, token_count, features = tokens.shape
    hidden_cols = w_up.shape[1]
    columns = lax.axis_size("expert")
    dp = lax.axis_size("dp")
    groups_per = FF // hidden_cols
    chips_per = groups_per // 2
    experts = columns // groups_per
    capacity = 2 * token_count // experts
    slot_count = experts * capacity
    bf16 = jnp.bfloat16
    f32 = jnp.float32
    contract_last = (((1,), (1,)), ((), ()))
    contract_first = (((0,), (0,)), ((), ()))
    pairs = [[2 * i, 2 * i + 1] for i in range(columns // 2)]
    swap = [(i, i ^ 1) for i in range(columns)]
    first_core = lax.rem(lax.axis_index("expert"), 2) == 0

    routing = expert_ids[:, :, 0]
    earlier = jnp.tril(jnp.ones((token_count, token_count), jnp.bool_), -1)
    same = (routing[:, :, None] == routing[:, None, :]) & earlier[None]
    slots = routing * capacity + jnp.sum(same.astype(jnp.int32), axis=2)
    slot_range = jnp.arange(slot_count, dtype=jnp.int32)
    table = (slots[:, None, :] == slot_range[None, :, None]).astype(bf16)
    table_back = (slots[:, :, None] == slot_range[None, None, :]).astype(bf16)
    scaled = (gate_weights * out_grad.astype(f32)).astype(bf16)

    def dispatch(micros):
        count = len(micros)
        both = jnp.stack([tokens[micros[0] : micros[-1] + 1], scaled[micros[0] : micros[-1] + 1]])
        packed = jnp.einsum(
            "mst,amtf->amsf", table[micros[0] : micros[-1] + 1], both, preferred_element_type=f32
        ).astype(bf16)
        packed = packed.reshape(2, count, experts, capacity, features).transpose(2, 0, 1, 3, 4)
        packed = packed.reshape(experts, 1, 2, count * capacity, features)
        packed = jnp.broadcast_to(packed, (experts, chips_per, 2, count * capacity, features))
        packed = packed.reshape(columns, count * capacity, features)
        arrived = lax.all_to_all(packed, "expert", 0, 0, tiled=True)
        arrived = arrived.reshape(2, 1, columns * count * capacity // 2, features)
        halves = [
            lax.all_gather(half, "expert", axis=0, axis_index_groups=pairs, tiled=True)
            for half in (arrived[0], arrived[1])
        ]
        return [half[0] for half in halves], [half[1] for half in halves]

    def reduce_middle(rows_in, rows_grad):
        halves = []
        for one_in, one_grad in zip(rows_in, rows_grad):
            pre = jnp.dot(one_in, w_up, preferred_element_type=f32)
            back = lax.dot_general(one_grad, w_down, contract_last, preferred_element_type=f32)
            halves.append(jnp.concatenate([pre.astype(bf16), back.astype(bf16)], axis=1))
        parts = jnp.concatenate(halves, axis=0).reshape(dp, -1, 2 * hidden_cols)
        got = lax.all_to_all(parts, "dp", 0, 0, tiled=True)
        return jnp.sum(got.astype(f32), axis=0)

    def gather_middle(total):
        pre, back = total[:, :hidden_cols], total[:, hidden_cols:]
        share = jnp.concatenate(
            [jax.nn.silu(pre).astype(bf16), (back * silu_grad(pre)).astype(bf16)], axis=1
        )
        share = jnp.broadcast_to(share[None], (dp,) + share.shape)
        full = lax.all_to_all(share, "dp", 0, 0, tiled=True).reshape(-1, 2 * hidden_cols)
        return full[:, :hidden_cols], full[:, hidden_cols:]

    def combine(micros, hidden, preact_grad):
        count = len(micros)
        mixed_part = jnp.dot(hidden, w_down, preferred_element_type=f32).astype(bf16)
        token_part = lax.dot_general(
            preact_grad, w_up, contract_last, preferred_element_type=f32
        ).astype(bf16)
        keep = jnp.where(first_core, mixed_part, token_part)
        give = jnp.where(first_core, token_part, mixed_part)
        came = lax.ppermute(give, "expert", swap)
        total = (keep.astype(f32) + came.astype(f32)).astype(bf16)
        back = lax.all_to_all(
            total.reshape(columns, count * capacity, features), "expert", 0, 0, tiled=True
        )
        back = back.reshape(experts, chips_per, 2, count, capacity, features)
        back = back.transpose(2, 3, 1, 0, 4, 5).reshape(2, count, chips_per * slot_count, features)
        spread = jnp.concatenate([table_back[micros[0] : micros[-1] + 1]] * chips_per, axis=2)
        return jnp.einsum("mts,amsf->amtf", spread, back, preferred_element_type=f32)

    rows = [dispatch(micros) for micros in GROUPS]
    totals = [reduce_middle(*r) for r in rows]
    middles = [gather_middle(t) for t in totals]
    outs = [combine(micros, *m) for micros, m in zip(GROUPS, middles)]
    grad_in = 0.0
    grad_out = 0.0
    for (rows_in, rows_grad), (hidden, preact_grad) in zip(rows, middles):
        start = 0
        for one_in, one_grad in zip(rows_in, rows_grad):
            stop = start + one_in.shape[0]
            grad_in = grad_in + lax.dot_general(
                one_in, preact_grad[start:stop], contract_first, preferred_element_type=f32
            )
            grad_out = grad_out + lax.dot_general(
                hidden[start:stop], one_grad, contract_first, preferred_element_type=f32
            )
            start = stop
    both = jnp.concatenate(outs, axis=1)
    return (
        (gate_weights * both[0]).astype(bf16),
        both[1].astype(bf16),
        grad_in.astype(bf16),
        grad_out.astype(bf16),
    )


def solution(mesh):
    in_specs = (
        P(None, "expert", "dp"),
        P(None, "expert", "dp"),
        P(None, "expert", None),
        P(None, "expert", None),
        P("dp", "expert"),
        P("expert", "dp"),
    )
    out_specs = (
        P(None, "expert", "dp"),
        P(None, "expert", "dp"),
        P("dp", "expert"),
        P("expert", "dp"),
    )
    return jax.shard_map(
        on_device, mesh=mesh, in_specs=in_specs, out_specs=out_specs, check_vma=False
    )
```

time: 573 us -> 242 us (0.42); the launches traced: 563 us -> 241 us
  starting transfers between devices: 139 us -> 16.1 us
  waiting for transfers between devices: 150 us -> 78.4 us
  other arithmetic: 61.6 us -> 5.82 us
  local copies, waits for them, and re-layouts: 55.7 us -> 9.74 us
  between operations: 14.6 us -> 0.9 us
  blocking collectives: 125 us -> 118 us
    all_to_all x8 -> x2, starting transfers between devices: 137 us -> 10.7 us  [the longest x1 6.23 us: combine(): lax.all_to_all(total.reshape(columns, count * capacity, features), 'exper...]
    all_gather x4 -> x2, blocking collectives: 125 us -> 5.52 us  [dispatch(): lax.all_gather(half, 'expert', axis=0, axis_index_groups=pairs, tiled=True)]
    all_to_all x0 -> x2, blocking collectives: none -> 113 us  [the longest x1 56.5 us: dispatch(): arrived = lax.all_to_all(packed, 'expert', 0, 0, tiled=True)]
    reduce_scatter x4 -> x0, waiting for transfers between devices: 106 us -> none  [reduce_then(): lax.psum_scatter(partial_term.astype(jnp.bfloat16), 'dp', scatter_dimensi...]
    all_to_all x12 -> x0, other arithmetic: 44.4 us -> none  [the longest x4 13.1 us: on_device(): lax.all_to_all(outgoing_grad, 'expert', split_axis=0, concat_axis=0, tile...]
    all_to_all x8 -> x2, waiting for transfers between devices: 44.2 us -> 76.3 us  [the longest x1 47.9 us: gather_middle(): lax.all_to_all(share, 'dp', 0, 0, tiled=True).reshape(-1, 2 * hidden_cols)]
    unnamed x40 -> x16, local copies, waits for them, and re-layouts: 27.8 us -> 0.5 us
    all_to_all x9 -> x0, local copies, waits for them, and re-layouts: 13.2 us -> none  [the longest x2 6 us: on_device(): lax.all_to_all(mixed_part.reshape(columns, capacity * features), 'expert'...]
  transfers between devices with their start and end apart: 12 -> 3, of which waited for: 6 -> 3; matrix products, arithmetic and copies ran while one was open for 19% -> 2% of each run, Pallas kernels for 0% -> 0%
where the time goes in v1:
time: 242 us; the launch traced here: 241 us
  blocking collectives  118 us (49%)
  waiting for transfers between devices  78.4 us (32%)
  starting transfers between devices  16.1 us (7%)
  matrix products  11.7 us (5%)
  local copies, waits for them, and re-layouts  9.74 us (4%)
  other arithmetic  5.82 us (2%)
    all_to_all x1, blocking collectives, dispatch(): arrived = lax.all_to_all(packed, 'expert', 0, 0, tiled=True)  56.5 us
    all_to_all x1, blocking collectives, reduce_middle(): got = lax.all_to_all(parts, 'dp', 0, 0, tiled=True)  56.3 us
    all_to_all x1, waiting for transfers between devices, gather_middle(): lax.all_to_all(share, 'dp', 0, 0, tiled=True).reshape(-1, 2 * hidden_cols)  47.9 us
    all_to_all x1, waiting for transfers between devices, combine(): lax.all_to_all(total.reshape(columns, count * capacity, features), 'exper...  28.4 us
    all_to_all x1, starting transfers between devices, combine(): lax.all_to_all(total.reshape(columns, count * capacity, features), 'exper...  6.23 us
    all_gather x2, blocking collectives, dispatch(): lax.all_gather(half, 'expert', axis=0, axis_index_groups=pairs, tiled=True)  5.52 us
    ppermute x1, starting transfers between devices, combine(): came = lax.ppermute(give, 'expert', swap)  5.4 us
  transfers between devices with their start and end apart: 3, of which 3 were waited for; matrix products, arithmetic and copies ran while one was open for 2% of the time, Pallas kernels for 0%

profile of v1, /device:TPU:1, one launch (start us, length us, event | category | flops | bytes accessed | tf_op | source)
XLA Modules:
  0.0 240.9 jit_solution(5358391650224628085)
XLA Ops:
  0.6 0.0 copy-start
  0.7 0.1 iota_compare_fusion.2
  0.7 0.9 convert_reduce_fusion.1
  1.7 0.7 multiply_add_fusion
  2.4 1.0 fusion.16
  3.4 1.3 fusion.2
  4.6 0.2 copy.40
  4.8 0.1 copy_bitcast_fusion
  4.9 0.1 broadcast_in_dim.9
  5.0 56.5 %all_to_all.20 = bf16[64,16,448]{2,1,0:T(8,128)(2,1)S(1)} all-to-all(bf16[64,16,448]{2,1,0:T(8,128)(2,1)S(1)} %bitcast.80), channel_id=1, replica_groups=mesh['dp'=16,'expert'=64] {'expert'}, dimensions={0} | all-to-all | bytes 1835008 | tf_op jit(solution)/shard_map/all_to_all | solution.py:52
  61.5 0.0 copy-start.7
  61.5 0.1 fusion.27
  61.6 0.2 copy.43
  61.8 2.9 %all_gather.7 = bf16[2,512,448]{1,2,0:T(8,128)(2,1)S(1)} all-gather(bf16[1,512,448]{1,2,0:T(8,128)(2,1)S(1)} %copy.43), channel_id=1, replica_groups={{0,1},{2,3},{4,5},{6,7},{8,9},{10,11},{12,13},{14,15},{16,17},{18,19},{..., dimensions={0}, use_global_device_ids=true | all-gather | bytes 1376256 | tf_op jit(solution)/shard_map/all_gather | solution.py:55
  64.7 0.0 copy-done.7
  64.7 1.3 convolution_convert_fusion.2
  66.0 0.0 copy-done
  66.0 1.3 convolution_convert_fusion.3
  67.3 0.2 copy.42
  67.5 0.0 copy-start.3
  67.5 0.0 copy-start.4
  67.5 2.6 %all_gather.6 = bf16[2,512,448]{1,2,0:T(8,128)(2,1)S(1)} all-gather(bf16[1,512,448]{1,2,0:T(8,128)(2,1)S(1)} %copy.42), channel_id=1, replica_groups={{0,1},{2,3},{4,5},{6,7},{8,9},{10,11},{12,13},{14,15},{16,17},{18,19},{..., dimensions={0}, use_global_device_ids=true | all-gather | bytes 1376256 | tf_op jit(solution)/shard_map/all_gather | solution.py:55
  70.1 0.0 copy-start.1
  70.1 0.5 convolution_convert_fusion.4
  70.6 0.5 copy-done.1
  71.0 0.5 convolution_convert_fusion.5
  71.5 0.0 copy-done.3
  71.5 0.0 copy-done.4
  71.5 0.3 maximum_maximum_fusion
  71.8 2.6 %copy.44 = bf16[1024,1024]{1,0:T(8,128)(2,1)} copy(bf16[1024,1024]{0,1:T(8,128)(2,1)S(1)} %maximum_maximum_fusion) | data formatting | bytes 4194304 | tf_op jit(solution)/shard_map/concatenate | solution.py:66
  74.4 56.3 %all_to_all.21 = bf16[16,64,1024]{2,1,0:T(8,128)(2,1)S(1)} all-to-all(bf16[16,64,1024]{2,1,0:T(8,128)(2,1)} %bitcast.72), channel_id=1, replica_groups=mesh['dp'=16,'expert'=64] {'dp'}, dimensions={0} | all-to-all | bytes 4194304 | tf_op jit(solution)/shard_map/all_to_all | solution.py:67
  130.7 0.4 convert_reduce_fusion
  131.1 0.1 multiply_convert_fusion.1
  131.2 1.6 broadcast_in_dim.10
  132.8 4.4 %all-to-all-start.2 = ((bf16[16,64,1024]{2,1,0:T(8,128)(2,1)}), bf16[16,64,1024]{2,1,0:T(8,128)(2,1)S(1)}, u32[]{:S(2)}, u32[]{:S(2)}) async-start(bf16[16,64,1024]{2,1,0:T(8,128)(2,1)} %broadcast_in_dim.10), calls=%async_computation.2 | async-start | bytes 4194304 | tf_op jit(solution)/shard_map/all_to_all | solution.py:76
  137.2 47.9 %all-to-all-done.2 = bf16[16,64,1024]{2,1,0:T(8,128)(2,1)S(1)} async-done(((bf16[16,64,1024]{2,1,0:T(8,128)(2,1)}), bf16[16,64,1024]{2,1,0:T(8,128)(2,1)S(1)}, u32[]{:S(2)}, u32[]{:S(2)}) %all-to-all-start.2) | async-done | bytes 2097184 | tf_op jit(solution)/shard_map/all_to_all | solution.py:76
  185.2 1.7 convolution_convert_fusion.1
  186.8 0.7 broadcast_select_fusion
  187.5 5.4 %collective-permute-start = (bf16[1024,448]{0,1:T(8,128)(2,1)S(1)}, bf16[1024,448]{0,1:T(8,128)(2,1)S(1)}, u32[]{:S(2)}, u32[]{:S(2)}) collective-permute-start(bf16[1024,448]{0,1:T(8,128)(2,1)S(1)} %get-tuple-element.8), channel_id=1, source_target_pairs={{0,1},{1,0},{2,3},{3,2},{4,5},{5,4},{6,7},{7,6},{8,9},{9,8},{10,11... | collective-permute-start | bytes 2752520 | tf_op jit(solution)/shard_map/ppermute | solution.py:87
  193.0 2.1 collective-permute-done
  195.0 1.5 add_convert_fusion
  196.6 0.0 copy-start.5
  196.6 2.2 copy.45
  198.8 6.2 %all-to-all-start.3 = ((bf16[64,16,448]{2,1,0:T(8,128)(2,1)}), bf16[64,16,448]{2,1,0:T(8,128)(2,1)}, u32[]{:S(2)}, u32[]{:S(2)}) async-start(bf16[64,16,448]{2,1,0:T(8,128)(2,1)} %bitcast.81), calls=%async_computation.3 | async-start | bytes 2097152 | tf_op jit(solution)/shard_map/all_to_all | solution.py:89
  205.0 0.0 copy-start.2
  205.0 0.0 copy-done.5
  205.1 0.1 iota_compare_fusion
  205.2 1.5 fusion.6
  206.6 0.0 copy-done.2
  206.7 0.4 fusion.9
  207.1 1.2 fusion.1
  208.2 1.2 fusion
  209.4 0.0 copy-start.6
  209.4 28.4 %all-to-all-done.3 = bf16[64,16,448]{2,1,0:T(8,128)(2,1)} async-done(((bf16[64,16,448]{2,1,0:T(8,128)(2,1)}), bf16[64,16,448]{2,1,0:T(8,128)(2,1)}, u32[]{:S(2)}, u32[]{:S(2)}) %all-to-all-start.3) | async-done | bytes 917536 | tf_op jit(solution)/shard_map/all_to_all | solution.py:89
  237.8 1.3 copy.46
  239.2 0.3 convolution_bitcast_fusion
  239.5 0.0 copy-done.6
  239.5 0.7 fusion.12
  240.2 0.7 fusion.17
  (3 shorter events, 0.0 us)
Async XLA Ops:
  0.6 65.4 %copy-start = (bf16[448,512]{1,0:T(8,128)(2,1)S(1)}, bf16[448,512]{1,0:T(8,128)(2,1)}, u32[]{:S(2)}) copy-start(bf16[448,512]{1,0:T(8,128)(2,1)} %param.10) | copy-start | bytes 1376260
  61.5 3.2 %copy-start.7 = (bf16[512,448]{0,1:T(8,128)(2,1)S(1)}, bf16[512,448]{0,1:T(8,128)(2,1)}, u32[]{:S(2)}) copy-start(bf16[512,448]{0,1:T(8,128)(2,1)} %param.11) | copy-start | bytes 1376260
  67.5 4.1 %copy-start.3 = (bf16[512,512]{0,1:T(8,128)(2,1)S(1)}, bf16[512,512]{0,1:T(8,128)(2,1)}, u32[]{:S(2)}) copy-start(bf16[512,512]{0,1:T(8,128)(2,1)} %convolution_convert_fusion.2) | copy-start | bytes 1572868
  67.5 4.1 %copy-start.4 = (bf16[512,512]{0,1:T(8,128)(2,1)S(1)}, bf16[512,512]{0,1:T(8,128)(2,1)}, u32[]{:S(2)}) copy-start(bf16[512,512]{0,1:T(8,128)(2,1)} %convolution_convert_fusion.3) | copy-start | bytes 1572868
  70.1 1.0 copy-start.1
  132.8 52.4 %all-to-all-start.2 = ((bf16[16,64,1024]{2,1,0:T(8,128)(2,1)}), bf16[16,64,1024]{2,1,0:T(8,128)(2,1)S(1)}, u32[]{:S(2)}, u32[]{:S(2)}) async-start(bf16[16,64,1024]{2,1,0:T(8,128)(2,1)} %broadcast_in_dim.10), calls=%async_computation.2 | async-start | bytes 4194304 | tf_op jit(solution)/shard_map/all_to_all | solution.py:76
  187.5 7.5 %collective-permute-start = (bf16[1024,448]{0,1:T(8,128)(2,1)S(1)}, bf16[1024,448]{0,1:T(8,128)(2,1)S(1)}, u32[]{:S(2)}, u32[]{:S(2)}) collective-permute-start(bf16[1024,448]{0,1:T(8,128)(2,1)S(1)} %get-tuple-element.8), channel_id=1, source_target_pairs={{0,1},{1,0},{2,3},{3,2},{4,5},{5,4},{6,7},{7,6},{8,9},{9,8},{10,11... | collective-permute-start | bytes 2752520 | tf_op jit(solution)/shard_map/ppermute | solution.py:87
  196.6 8.5 %copy-start.5 = (s32[2,64,1]{1,2,0:T(1,128)S(1)}, s32[2,64,1]{1,2,0:T(1,128)}, u32[]{:S(2)}) copy-start(s32[2,64,1]{1,2,0:T(1,128)} %param.8) | copy-start | bytes 1540
  198.8 39.0 %all-to-all-start.3 = ((bf16[64,16,448]{2,1,0:T(8,128)(2,1)}), bf16[64,16,448]{2,1,0:T(8,128)(2,1)}, u32[]{:S(2)}, u32[]{:S(2)}) async-start(bf16[64,16,448]{2,1,0:T(8,128)(2,1)} %bitcast.81), calls=%async_computation.3 | async-start | bytes 2097152 | tf_op jit(solution)/shard_map/all_to_all | solution.py:89
  205.0 1.6 copy-start.2
  209.4 30.0 %copy-start.6 = (f32[2,64,1]{1,2,0:T(1,128)S(1)}, f32[2,64,1]{1,2,0:T(1,128)}, u32[]{:S(2)}) copy-start(f32[2,64,1]{1,2,0:T(1,128)} %param.9) | copy-start | bytes 1540

commit v2 on v1

v2 whole, which is shorter than its diff:
```python
import jax
import jax.numpy as jnp
from jax import lax
from jax.sharding import PartitionSpec as P

FF = 2048


def silu_grad(preact):
    logistic = jax.nn.sigmoid(preact)
    return logistic * (1.0 + preact * (1.0 - logistic))


def on_device(tokens, out_grad, expert_ids, gate_weights, w_up, w_down):
    micro_count, token_count, features = tokens.shape
    hidden_cols = w_up.shape[1]
    columns = lax.axis_size("expert")
    dp = lax.axis_size("dp")
    lines = dp // 2
    groups_per = FF // hidden_cols
    chips_per = groups_per // 2
    experts = columns // groups_per
    capacity = 2 * token_count // experts
    slot_count = experts * capacity
    wide = 2 * features
    bf16 = jnp.bfloat16
    f32 = jnp.float32
    contract_last = (((1,), (1,)), ((), ()))
    contract_first = (((0,), (0,)), ((), ()))
    cores = [[2 * i, 2 * i + 1] for i in range(columns // 2)]
    swap_core = [(i, i ^ 1) for i in range(columns)]
    swap_side = [(i, i ^ 1) for i in range(dp)]
    along_x = [[2 * i + side for i in range(lines)] for side in range(2)]
    first_core = lax.rem(lax.axis_index("expert"), 2) == 0
    mine = lax.rem(lax.axis_index("dp"), 2)

    def pick(array, index):
        return lax.dynamic_index_in_dim(array, index, 0, keepdims=False)

    both = jnp.stack(
        [tokens, (gate_weights * out_grad.astype(f32)).astype(bf16)], axis=1
    )
    came_rows = lax.ppermute(pick(both, 1 - mine), "dp", swap_side)
    came_up = lax.ppermute(w_up, "dp", swap_side)
    came_down = lax.ppermute(w_down.T, "dp", swap_side)
    up = jnp.concatenate([w_up, came_up], axis=0)
    down_t = jnp.concatenate([w_down.T, came_down], axis=0)

    routing = pick(expert_ids, mine)[:, 0]
    gate = pick(gate_weights, mine)
    earlier = jnp.tril(jnp.ones((token_count, token_count), jnp.bool_), -1)
    same = (routing[:, None] == routing[None, :]) & earlier
    slots = routing * capacity + jnp.sum(same.astype(jnp.int32), axis=1)
    slot_range = jnp.arange(slot_count, dtype=jnp.int32)
    table = (slots[None, :] == slot_range[:, None]).astype(bf16)
    table_back = (slots[:, None] == slot_range[None, :]).astype(bf16)

    sent = jnp.concatenate([pick(both, mine), came_rows], axis=2)
    packed = jnp.einsum("st,atf->asf", table, sent, preferred_element_type=f32).astype(bf16)
    packed = packed.reshape(2, experts, capacity, wide).transpose(1, 0, 2, 3)
    packed = jnp.broadcast_to(packed[:, None], (experts, chips_per, 2, capacity, wide))
    packed = packed.reshape(columns, capacity, wide)
    arrived = lax.all_to_all(packed, "expert", 0, 0, tiled=True)
    arrived = arrived.reshape(2, 1, columns * capacity // 2, wide)
    halves = [
        lax.all_gather(half, "expert", axis=0, axis_index_groups=cores, tiled=True)
        for half in (arrived[0], arrived[1])
    ]

    parts = []
    for half in halves:
        pre = jnp.dot(half[0], up, preferred_element_type=f32)
        back = jnp.dot(half[1], down_t, preferred_element_type=f32)
        parts.append(jnp.concatenate([pre.astype(bf16), back.astype(bf16)], axis=1))
    parts = jnp.concatenate(parts, axis=0).reshape(lines, -1, 2 * hidden_cols)
    got = lax.all_to_all(parts, "dp", 0, 0, axis_index_groups=along_x, tiled=True)
    total = jnp.sum(got.astype(f32), axis=0)
    pre, back = total[:, :hidden_cols], total[:, hidden_cols:]
    share = jnp.concatenate(
        [jax.nn.silu(pre).astype(bf16), (back * silu_grad(pre)).astype(bf16)], axis=1
    )
    share = jnp.broadcast_to(share[None], (lines,) + share.shape)
    full = lax.all_to_all(share, "dp", 0, 0, axis_index_groups=along_x, tiled=True)
    full = full.reshape(-1, 2 * hidden_cols)
    hidden, preact_grad = full[:, :hidden_cols], full[:, hidden_cols:]

    mixed_part = lax.dot_general(
        hidden, down_t, contract_last, preferred_element_type=f32
    ).astype(bf16)
    token_part = lax.dot_general(
        preact_grad, up, contract_last, preferred_element_type=f32
    ).astype(bf16)
    keep = jnp.where(first_core, mixed_part, token_part)
    give = jnp.where(first_core, token_part, mixed_part)
    came = lax.ppermute(give, "expert", swap_core)
    chip_sum = (keep.astype(f32) + came.astype(f32)).astype(bf16)
    home = lax.all_to_all(
        chip_sum.reshape(columns, capacity, wide), "expert", 0, 0, tiled=True
    )
    home = home.reshape(experts, chips_per, 2, capacity, wide).transpose(2, 1, 0, 3, 4)
    home = home.reshape(2, chips_per * slot_count, wide)
    spread = jnp.concatenate([table_back] * chips_per, axis=1)
    summed = jnp.einsum("ts,asf->atf", spread, home, preferred_element_type=f32)
    done = jnp.stack([gate * summed[0], summed[1]]).astype(bf16)
    came_done = lax.ppermute(done[:, :, features:], "dp", swap_side)
    own_done = done[:, :, :features]
    first = jnp.where(mine == 0, own_done, came_done)
    second = jnp.where(mine == 0, came_done, own_done)

    grad_up = 0.0
    grad_down_t = 0.0
    rows = columns * capacity // 2
    for number, half in enumerate(halves):
        at = slice(number * rows, (number + 1) * rows)
        grad_up = grad_up + lax.dot_general(
            half[0], preact_grad[at], contract_first, preferred_element_type=f32
        )
        grad_down_t = grad_down_t + lax.dot_general(
            half[1], hidden[at], contract_first, preferred_element_type=f32
        )
    came_grad_up = lax.ppermute(grad_up[features:].astype(bf16), "dp", swap_side)
    came_grad_down = lax.ppermute(grad_down_t[features:].astype(bf16), "dp", swap_side)
    grad_up = grad_up[:features] + came_grad_up.astype(f32)
    grad_down_t = grad_down_t[:features] + came_grad_down.astype(f32)
    return (
        jnp.stack([first[0], second[0]]),
        jnp.stack([first[1], second[1]]),
        grad_up.astype(bf16),
        grad_down_t.astype(bf16).T,
    )


def solution(mesh):
    in_specs = (
        P(None, "expert", "dp"),
        P(None, "expert", "dp"),
        P(None, "expert", None),
        P(None, "expert", None),
        P("dp", "expert"),
        P("expert", "dp"),
    )
    out_specs = (
        P(None, "expert", "dp"),
        P(None, "expert", "dp"),
        P("dp", "expert"),
        P("expert", "dp"),
    )
    return jax.shard_map(
        on_device, mesh=mesh, in_specs=in_specs, out_specs=out_specs, check_vma=False
    )
```

time: 242 us -> 217 us (0.90)
  blocking collectives: 118 us -> 39.1 us
  starting transfers between devices: 16.1 us -> 63.7 us
  waiting for transfers between devices: 78.4 us -> 88.1 us
  local copies, waits for them, and re-layouts: 9.74 us -> 4.4 us
  other arithmetic: 5.82 us -> 9.32 us
    all_to_all x2 -> x1, blocking collectives: 113 us -> 33.3 us  [on_device(): lax.all_to_all(parts, 'dp', 0, 0, axis_index_groups=along_x, tiled=True)]
    ppermute x1 -> x7, waiting for transfers between devices: 2.08 us -> 61 us  [the longest x1 25.3 us: on_device(): came_up = lax.ppermute(w_up, 'dp', swap_side)]
    all_to_all x2 -> x3, waiting for transfers between devices: 76.3 us -> 27.2 us  [the longest x1 27.2 us: on_device(): lax.all_to_all(share, 'dp', 0, 0, axis_index_groups=along_x, tiled=True)]
    all_to_all x2 -> x3, starting transfers between devices: 10.7 us -> 41.6 us  [the longest x1 25.1 us: on_device(): arrived = lax.all_to_all(packed, 'expert', 0, 0, tiled=True)]
    ppermute x1 -> x7, starting transfers between devices: 5.4 us -> 22.1 us  [the longest x1 4.33 us: on_device(): came = lax.ppermute(give, 'expert', swap_core)]
    convert_element_type x3 -> x0, local copies, waits for them, and re-layouts: 3.12 us -> none  [the longest x1 2.24 us: combine(): total = (keep.astype(f32) + came.astype(f32)).astype(bf16)]
    reshape x0 -> x1, other arithmetic: none -> 2.73 us  [on_device(): chip_sum.reshape(columns, capacity, wide)]
    concatenate x1, local copies, waits for them, and re-layouts: 2.57 us -> 0.03 us  [on_device(): up = jnp.concatenate([w_up, came_up], axis=0)]
  transfers between devices with their start and end apart: 3 -> 10, of which waited for: 3 -> 8; matrix products, arithmetic and copies ran while one was open for 2% -> 4% of each run, Pallas kernels for 0% -> 0%
where the time goes in v2:
time: 217 us; the launch traced here: 216 us
  waiting for transfers between devices  88.1 us (41%)
  starting transfers between devices  63.7 us (29%)
  blocking collectives  39.1 us (18%)
  matrix products  9.98 us (5%)
  other arithmetic  9.32 us (4%)
  local copies, waits for them, and re-layouts  4.4 us (2%)
    all_to_all x1, blocking collectives, on_device(): lax.all_to_all(parts, 'dp', 0, 0, axis_index_groups=along_x, tiled=True)  33.3 us
    all_to_all x1, waiting for transfers between devices, on_device(): lax.all_to_all(share, 'dp', 0, 0, axis_index_groups=along_x, tiled=True)  27.2 us
    ppermute x1, waiting for transfers between devices, on_device(): came_up = lax.ppermute(w_up, 'dp', swap_side)  25.3 us
    all_to_all x1, starting transfers between devices, on_device(): arrived = lax.all_to_all(packed, 'expert', 0, 0, tiled=True)  25.1 us
    ppermute x1, waiting for transfers between devices, on_device(): lax.ppermute(grad_up[features:].astype(bf16), 'dp', swap_side)  23.2 us
    all_to_all x1, starting transfers between devices, on_device(): lax.all_to_all(chip_sum.reshape(columns, capacity, wide), 'expert', 0, 0,...  13 us
    all_gather x2, blocking collectives, on_device(): lax.all_gather(half, 'expert', axis=0, axis_index_groups=cores, tiled=True)  5.82 us
  transfers between devices with their start and end apart: 10, of which 8 were waited for; matrix products, arithmetic and copies ran while one was open for 4% of the time, Pallas kernels for 0%

profile of v2, /device:TPU:1, one launch (start us, length us, event | category | flops | bytes accessed | tf_op | source)
XLA Modules:
  0.0 215.7 jit_solution(9823301739780075668)
XLA Ops:
  0.6 1.0 fusion.18
  1.6 0.9 fusion.22
  2.6 4.1 %collective-permute-start = (bf16[2,64,448]{2,1,0:T(8,128)(2,1)S(1)}, bf16[2,64,448]{2,1,0:T(8,128)(2,1)S(1)}, u32[]{:S(2)}, u32[]{:S(2)}) collective-permute-start(bf16[2,64,448]{2,1,0:T(8,128)(2,1)S(1)} %get-tuple-element.11), channel_id=1, source_target_pairs={{0,64},{64,0},{128,192},{192,128},{256,320},{320,256},{384,448},{4... | collective-permute-start | bytes 344072 | tf_op jit(solution)/shard_map/ppermute | solution.py:43
  6.7 0.7 fusion.31
  7.4 0.2 convert_reduce_fusion.1
  7.6 0.7 multiply_add_fusion
  8.2 0.8 collective-permute-done
  9.1 0.4 fusion
  9.5 0.0 copy-start.5
  9.5 0.0 copy-start.7
  9.5 1.0 broadcast_in_dim.6
  10.5 25.1 %all-to-all-start = ((bf16[64,8,896]{2,1,0:T(8,128)(2,1)}), bf16[64,8,896]{2,1,0:T(8,128)(2,1)S(1)}, u32[]{:S(2)}, u32[]{:S(2)}) async-start(bf16[64,8,896]{2,1,0:T(8,128)(2,1)} %bitcast.11), calls=%async_computation | async-start | bytes 1835008 | tf_op jit(solution)/shard_map/all_to_all | solution.py:63
  35.6 0.0 copy-done.5
  35.6 2.4 %collective-permute-start.1 = (bf16[448,512]{1,0:T(8,128)(2,1)S(1)}, bf16[448,512]{1,0:T(8,128)(2,1)S(1)}, u32[]{:S(2)}, u32[]{:S(2)}) collective-permute-start(bf16[448,512]{1,0:T(8,128)(2,1)S(1)} %copy-done.5), channel_id=1, source_target_pairs={{0,64},{64,0},{128,192},{192,128},{256,320},{320,256},{384,448},{4... | collective-permute-start | bytes 1376264 | tf_op jit(solution)/shard_map/ppermute | solution.py:44
  38.1 0.0 copy-done.7
  38.1 2.9 %collective-permute-start.2 = (bf16[448,512]{1,0:T(8,128)(2,1)S(1)}, bf16[448,512]{1,0:T(8,128)(2,1)}, u32[]{:S(2)}, u32[]{:S(2)}) collective-permute-start(bf16[448,512]{1,0:T(8,128)(2,1)S(1)} %bitcast.74), channel_id=1, source_target_pairs={{0,64},{64,0},{128,192},{192,128},{256,320},{320,256},{384,448},{4... | collective-permute-start | bytes 1376264 | tf_op jit(solution)/shard_map/ppermute | solution.py:45
  41.0 25.3 %collective-permute-done.1 = bf16[448,512]{1,0:T(8,128)(2,1)S(1)} collective-permute-done((bf16[448,512]{1,0:T(8,128)(2,1)S(1)}, bf16[448,512]{1,0:T(8,128)(2,1)S(1)}, u32[]{:S(2)}, u32[]{:S(2)}) %collective-permute-start.1) | collective-permute-done | bytes 458784 | tf_op jit(solution)/shard_map/ppermute | solution.py:44
  66.4 0.0 copy-start.3
  66.4 0.0 all-to-all-done
  66.4 0.1 slice_bitcast_fusion.5
  66.5 3.4 %all_gather.7 = bf16[2,256,896]{2,1,0:T(8,128)(2,1)S(1)} all-gather(bf16[1,256,896]{2,1,0:T(8,128)(2,1)S(1)} %get-tuple-element.5), channel_id=1, replica_groups={{0,1},{2,3},{4,5},{6,7},{8,9},{10,11},{12,13},{14,15},{16,17},{18,19},{..., dimensions={0}, use_global_device_ids=true | all-gather | bytes 1376256 | tf_op jit(solution)/shard_map/all_gather | solution.py:66
  69.8 0.4 convolution_convert_fusion.4
  70.3 2.5 %all_gather.6 = bf16[2,256,896]{2,1,0:T(8,128)(2,1)S(1)} all-gather(bf16[1,256,896]{2,1,0:T(8,128)(2,1)S(1)} %get-tuple-element.4), channel_id=1, replica_groups={{0,1},{2,3},{4,5},{6,7},{8,9},{10,11},{12,13},{14,15},{16,17},{18,19},{..., dimensions={0}, use_global_device_ids=true | all-gather | bytes 1376256 | tf_op jit(solution)/shard_map/all_gather | solution.py:66
  72.7 0.4 convolution_convert_fusion.6
  73.2 3.1 %collective-permute-done.2 = bf16[448,512]{1,0:T(8,128)(2,1)} collective-permute-done((bf16[448,512]{1,0:T(8,128)(2,1)S(1)}, bf16[448,512]{1,0:T(8,128)(2,1)}, u32[]{:S(2)}, u32[]{:S(2)}) %collective-permute-start.2) | collective-permute-done | bytes 458784 | tf_op jit(solution)/shard_map/ppermute | solution.py:45
  76.3 1.5 convolution_convert_fusion.3
  77.7 1.5 convolution_convert_fusion.5
  79.2 0.1 maximum_maximum_fusion
  79.3 33.3 %all_to_all.20 = bf16[8,64,1024]{2,1,0:T(8,128)(2,1)S(1)} all-to-all(bf16[8,64,1024]{2,1,0:T(8,128)(2,1)S(1)} %bitcast.70), channel_id=1, replica_groups={{0,128,256,384,512,640,768,896},{64,192,320,448,576,704,832,960},{1,129..., dimensions={0} | all-to-all | bytes 2097152 | tf_op jit(solution)/shard_map/all_to_all | solution.py:76
  112.6 0.2 convert_reduce_fusion
  112.8 0.1 multiply_convert_fusion.1
  112.9 1.1 broadcast_in_dim.7
  114.0 3.6 %all-to-all-start.2 = ((bf16[8,64,1024]{2,1,0:T(8,128)(2,1)}), bf16[8,64,1024]{2,1,0:T(8,128)(2,1)S(1)}, u32[]{:S(2)}, u32[]{:S(2)}) async-start(bf16[8,64,1024]{2,1,0:T(8,128)(2,1)} %broadcast_in_dim.7), calls=%async_computation.2 | async-start | bytes 2097152 | tf_op jit(solution)/shard_map/all_to_all | solution.py:83
  117.6 27.2 %all-to-all-done.2 = bf16[8,64,1024]{2,1,0:T(8,128)(2,1)S(1)} async-done(((bf16[8,64,1024]{2,1,0:T(8,128)(2,1)}), bf16[8,64,1024]{2,1,0:T(8,128)(2,1)S(1)}, u32[]{:S(2)}, u32[]{:S(2)}) %all-to-all-start.2) | async-done | bytes 1048608 | tf_op jit(solution)/shard_map/all_to_all | solution.py:83
  144.7 1.8 convolution_convert_fusion.1
  146.6 2.0 broadcast_select_fusion
  148.6 0.0 copy-done.2
  148.6 4.3 %collective-permute-start.3 = (bf16[512,896]{1,0:T(8,128)(2,1)}, bf16[512,896]{1,0:T(8,128)(2,1)}, u32[]{:S(2)}, u32[]{:S(2)}) collective-permute-start(bf16[512,896]{1,0:T(8,128)(2,1)} %get-tuple-element.16), channel_id=1, source_target_pairs={{0,1},{1,0},{2,3},{3,2},{4,5},{5,4},{6,7},{7,6},{8,9},{9,8},{10,11... | collective-permute-start | bytes 2752520 | tf_op jit(solution)/shard_map/ppermute | solution.py:95
  152.9 2.4 %collective-permute-done.3 = bf16[512,896]{1,0:T(8,128)(2,1)} collective-permute-done((bf16[512,896]{1,0:T(8,128)(2,1)}, bf16[512,896]{1,0:T(8,128)(2,1)}, u32[]{:S(2)}, u32[]{:S(2)}) %collective-permute-start.3) | collective-permute-done | bytes 917536 | tf_op jit(solution)/shard_map/ppermute | solution.py:95
  155.4 2.7 %fusion.1 = bf16[64,8,896]{2,1,0:T(8,128)(2,1)} fusion(bf16[512,896]{1,0:T(8,128)(2,1)} %collective-permute-done.3, bf16[512,896]{1,0:T(8,128)(2,1)} %copy-done.2, bf16[512,896]{1,0:T(8,128)(2,1)} %get-tuple-element.17, pred[]{:T(512)S(6)} %eq.23), kind=kLoop, calls=%fused_computation.14 | loop fusion | flops 2293760 | bytes 3670017 | tf_op jit(solution)/shard_map/reshape | solution.py:98
  158.1 13.0 %all-to-all-start.3 = ((bf16[64,8,896]{2,1,0:T(8,128)(2,1)}), bf16[64,8,896]{2,1,0:T(8,128)(2,1)}, u32[]{:S(2)}, u32[]{:S(2)}) async-start(bf16[64,8,896]{2,1,0:T(8,128)(2,1)} %fusion.1), calls=%async_computation.3 | async-start | bytes 1835008 | tf_op jit(solution)/shard_map/all_to_all | solution.py:97
  171.1 0.1 iota_compare_fusion
  171.2 0.4 fusion.7
  171.6 0.0 copy-done
  171.6 0.4 convolution_add_fusion.1
  172.1 0.1 slice.203
  172.1 2.6 %collective-permute-start.5 = (bf16[448,512]{1,0:T(8,128)(2,1)S(1)}, bf16[448,512]{1,0:T(8,128)(2,1)S(1)}, u32[]{:S(2)}, u32[]{:S(2)}) collective-permute-start(bf16[448,512]{1,0:T(8,128)(2,1)S(1)} %slice.203), channel_id=1, source_target_pairs={{0,64},{64,0},{128,192},{192,128},{256,320},{320,256},{384,448},{4... | collective-permute-start | bytes 1376264 | tf_op jit(solution)/shard_map/ppermute | solution.py:121
  174.7 0.4 fusion.8
  175.2 0.4 convolution_add_fusion
  175.6 0.1 slice.202
  175.7 2.8 %collective-permute-start.6 = (bf16[448,512]{1,0:T(8,128)(2,1)S(1)}, bf16[448,512]{1,0:T(8,128)(2,1)S(1)}, u32[]{:S(2)}, u32[]{:S(2)}) collective-permute-start(bf16[448,512]{1,0:T(8,128)(2,1)S(1)} %slice.202), channel_id=1, source_target_pairs={{0,64},{64,0},{128,192},{192,128},{256,320},{320,256},{384,448},{4... | collective-permute-start | bytes 1376264 | tf_op jit(solution)/shard_map/ppermute | solution.py:122
  178.5 23.2 %collective-permute-done.5 = bf16[448,512]{1,0:T(8,128)(2,1)S(1)} collective-permute-done((bf16[448,512]{1,0:T(8,128)(2,1)S(1)}, bf16[448,512]{1,0:T(8,128)(2,1)S(1)}, u32[]{:S(2)}, u32[]{:S(2)}) %collective-permute-start.5) | collective-permute-done | bytes 458784 | tf_op jit(solution)/shard_map/ppermute | solution.py:121
  201.7 0.9 fusion.3
  202.6 0.0 all-to-all-done.3
  202.6 1.3 copy.15
  203.8 0.3 convolution_bitcast_fusion
  204.1 0.1 fusion.13
  204.2 0.1 pad_maximum_fusion.4
  204.3 2.9 %collective-permute-start.4 = (bf16[2,64,448]{2,1,0:T(8,128)(2,1)S(1)}, bf16[2,64,448]{2,1,0:T(8,128)(2,1)S(1)}, u32[]{:S(2)}, u32[]{:S(2)}) collective-permute-start(bf16[2,64,448]{2,1,0:T(8,128)(2,1)S(1)} %pad_maximum_fusion.4), channel_id=1, source_target_pairs={{0,64},{64,0},{128,192},{192,128},{256,320},{320,256},{384,448},{4... | collective-permute-start | bytes 344072 | tf_op jit(solution)/shard_map/ppermute | solution.py:105
  207.2 4.3 %collective-permute-done.6 = bf16[448,512]{1,0:T(8,128)(2,1)S(1)} collective-permute-done((bf16[448,512]{1,0:T(8,128)(2,1)S(1)}, bf16[448,512]{1,0:T(8,128)(2,1)S(1)}, u32[]{:S(2)}, u32[]{:S(2)}) %collective-permute-start.6) | collective-permute-done | bytes 458784 | tf_op jit(solution)/shard_map/ppermute | solution.py:122
  211.5 0.9 fusion.6
  212.4 1.9 collective-permute-done.4
  214.4 0.7 pad_maximum_fusion.6
  215.0 0.7 pad_maximum_fusion.7
  (18 shorter events, 0.2 us)
Async XLA Ops:
  2.6 6.5 %collective-permute-start = (bf16[2,64,448]{2,1,0:T(8,128)(2,1)S(1)}, bf16[2,64,448]{2,1,0:T(8,128)(2,1)S(1)}, u32[]{:S(2)}, u32[]{:S(2)}) collective-permute-start(bf16[2,64,448]{2,1,0:T(8,128)(2,1)S(1)} %get-tuple-element.11), channel_id=1, source_target_pairs={{0,64},{64,0},{128,192},{192,128},{256,320},{320,256},{384,448},{4... | collective-permute-start | bytes 344072 | tf_op jit(solution)/shard_map/ppermute | solution.py:43
  9.5 26.1 %copy-start.5 = (bf16[448,512]{1,0:T(8,128)(2,1)S(1)}, bf16[448,512]{1,0:T(8,128)(2,1)}, u32[]{:S(2)}) copy-start(bf16[448,512]{1,0:T(8,128)(2,1)} %param.10) | copy-start | bytes 1376260
  9.5 28.5 %copy-start.7 = (bf16[512,448]{0,1:T(8,128)(2,1)S(1)}, bf16[512,448]{0,1:T(8,128)(2,1)}, u32[]{:S(2)}) copy-start(bf16[512,448]{0,1:T(8,128)(2,1)} %param.11) | copy-start | bytes 1376260
  10.5 55.8 %all-to-all-start = ((bf16[64,8,896]{2,1,0:T(8,128)(2,1)}), bf16[64,8,896]{2,1,0:T(8,128)(2,1)S(1)}, u32[]{:S(2)}, u32[]{:S(2)}) async-start(bf16[64,8,896]{2,1,0:T(8,128)(2,1)} %bitcast.11), calls=%async_computation | async-start | bytes 1835008 | tf_op jit(solution)/shard_map/all_to_all | solution.py:63
  35.6 30.7 %collective-permute-start.1 = (bf16[448,512]{1,0:T(8,128)(2,1)S(1)}, bf16[448,512]{1,0:T(8,128)(2,1)S(1)}, u32[]{:S(2)}, u32[]{:S(2)}) collective-permute-start(bf16[448,512]{1,0:T(8,128)(2,1)S(1)} %copy-done.5), channel_id=1, source_target_pairs={{0,64},{64,0},{128,192},{192,128},{256,320},{320,256},{384,448},{4... | collective-permute-start | bytes 1376264 | tf_op jit(solution)/shard_map/ppermute | solution.py:44
  38.1 38.2 %collective-permute-start.2 = (bf16[448,512]{1,0:T(8,128)(2,1)S(1)}, bf16[448,512]{1,0:T(8,128)(2,1)}, u32[]{:S(2)}, u32[]{:S(2)}) collective-permute-start(bf16[448,512]{1,0:T(8,128)(2,1)S(1)} %bitcast.74), channel_id=1, source_target_pairs={{0,64},{64,0},{128,192},{192,128},{256,320},{320,256},{384,448},{4... | collective-permute-start | bytes 1376264 | tf_op jit(solution)/shard_map/ppermute | solution.py:45
  66.4 6.4 %copy-start.3 = (bf16[896,512]{1,0:T(8,128)(2,1)}, bf16[896,512]{1,0:T(8,128)(2,1)S(1)}, u32[]{:S(2)}) copy-start(bf16[896,512]{1,0:T(8,128)(2,1)S(1)} %constant_dynamic-update-slice_fusion) | copy-start | bytes 2752516
  69.8 101.8 %copy-start = (bf16[2,256,896]{2,1,0:T(8,128)(2,1)}, bf16[2,256,896]{2,1,0:T(8,128)(2,1)S(1)}, u32[]{:S(2)}) copy-start(bf16[2,256,896]{2,1,0:T(8,128)(2,1)S(1)} %all_gather.7) | copy-start | bytes 2752516
  114.0 30.7 %all-to-all-start.2 = ((bf16[8,64,1024]{2,1,0:T(8,128)(2,1)}), bf16[8,64,1024]{2,1,0:T(8,128)(2,1)S(1)}, u32[]{:S(2)}, u32[]{:S(2)}) async-start(bf16[8,64,1024]{2,1,0:T(8,128)(2,1)} %broadcast_in_dim.7), calls=%async_computation.2 | async-start | bytes 2097152 | tf_op jit(solution)/shard_map/all_to_all | solution.py:83
  144.7 1.9 copy-start.4
  146.6 2.0 copy-start.2
  148.6 6.8 %collective-permute-start.3 = (bf16[512,896]{1,0:T(8,128)(2,1)}, bf16[512,896]{1,0:T(8,128)(2,1)}, u32[]{:S(2)}, u32[]{:S(2)}) collective-permute-start(bf16[512,896]{1,0:T(8,128)(2,1)} %get-tuple-element.16), channel_id=1, source_target_pairs={{0,1},{1,0},{2,3},{3,2},{4,5},{5,4},{6,7},{7,6},{8,9},{9,8},{10,11... | collective-permute-start | bytes 2752520 | tf_op jit(solution)/shard_map/ppermute | solution.py:95
  158.1 13.0 %copy-start.6 = (f32[2,64,1]{1,2,0:T(1,128)S(1)}, f32[2,64,1]{1,2,0:T(1,128)}, u32[]{:S(2)}) copy-start(f32[2,64,1]{1,2,0:T(1,128)} %param.9) | copy-start | bytes 1540
  158.1 44.5 %all-to-all-start.3 = ((bf16[64,8,896]{2,1,0:T(8,128)(2,1)}), bf16[64,8,896]{2,1,0:T(8,128)(2,1)}, u32[]{:S(2)}, u32[]{:S(2)}) async-start(bf16[64,8,896]{2,1,0:T(8,128)(2,1)} %fusion.1), calls=%async_computation.3 | async-start | bytes 1835008 | tf_op jit(solution)/shard_map/all_to_all | solution.py:97
  172.1 3.1 %copy-start.1 = (bf16[2,256,896]{2,1,0:T(8,128)(2,1)S(1)}, bf16[2,256,896]{2,1,0:T(8,128)(2,1)}, u32[]{:S(2)}) copy-start(bf16[2,256,896]{2,1,0:T(8,128)(2,1)} %copy-done) | copy-start | bytes 2752516
  172.1 29.5 %collective-permute-start.5 = (bf16[448,512]{1,0:T(8,128)(2,1)S(1)}, bf16[448,512]{1,0:T(8,128)(2,1)S(1)}, u32[]{:S(2)}, u32[]{:S(2)}) collective-permute-start(bf16[448,512]{1,0:T(8,128)(2,1)S(1)} %slice.203), channel_id=1, source_target_pairs={{0,64},{64,0},{128,192},{192,128},{256,320},{320,256},{384,448},{4... | collective-permute-start | bytes 1376264 | tf_op jit(solution)/shard_map/ppermute | solution.py:121
  175.7 35.8 %collective-permute-start.6 = (bf16[448,512]{1,0:T(8,128)(2,1)S(1)}, bf16[448,512]{1,0:T(8,128)(2,1)S(1)}, u32[]{:S(2)}, u32[]{:S(2)}) collective-permute-start(bf16[448,512]{1,0:T(8,128)(2,1)S(1)} %slice.202), channel_id=1, source_target_pairs={{0,64},{64,0},{128,192},{192,128},{256,320},{320,256},{384,448},{4... | collective-permute-start | bytes 1376264 | tf_op jit(solution)/shard_map/ppermute | solution.py:122
  204.3 10.0 %collective-permute-start.4 = (bf16[2,64,448]{2,1,0:T(8,128)(2,1)S(1)}, bf16[2,64,448]{2,1,0:T(8,128)(2,1)S(1)}, u32[]{:S(2)}, u32[]{:S(2)}) collective-permute-start(bf16[2,64,448]{2,1,0:T(8,128)(2,1)S(1)} %pad_maximum_fusion.4), channel_id=1, source_target_pairs={{0,64},{64,0},{128,192},{192,128},{256,320},{320,256},{384,448},{4... | collective-permute-start | bytes 344072 | tf_op jit(solution)/shard_map/ppermute | solution.py:105

commit v3 on v2

--- a/solution.py
+++ b/solution.py
@@ -29,10 +29,10 @@
     contract_first = (((0,), (0,)), ((), ()))
     cores = [[2 * i, 2 * i + 1] for i in range(columns // 2)]
     swap_core = [(i, i ^ 1) for i in range(columns)]
-    swap_side = [(i, i ^ 1) for i in range(dp)]
-    along_x = [[2 * i + side for i in range(lines)] for side in range(2)]
+    swap_side = [(i, i ^ 2) for i in range(dp)]
+    peers = [[i for i in range(dp) if i // 2 % 2 == side] for side in range(2)]
     first_core = lax.rem(lax.axis_index("expert"), 2) == 0
-    mine = lax.rem(lax.axis_index("dp"), 2)
+    mine = lax.rem(lax.axis_index("dp") // 2, 2)
 
     def pick(array, index):
         return lax.dynamic_index_in_dim(array, index, 0, keepdims=False)
@@ -73,14 +73,14 @@
         back = jnp.dot(half[1], down_t, preferred_element_type=f32)
         parts.append(jnp.concatenate([pre.astype(bf16), back.astype(bf16)], axis=1))
     parts = jnp.concatenate(parts, axis=0).reshape(lines, -1, 2 * hidden_cols)
-    got = lax.all_to_all(parts, "dp", 0, 0, axis_index_groups=along_x, tiled=True)
+    got = lax.all_to_all(parts, "dp", 0, 0, axis_index_groups=peers, tiled=True)
     total = jnp.sum(got.astype(f32), axis=0)
     pre, back = total[:, :hidden_cols], total[:, hidden_cols:]
     share = jnp.concatenate(
         [jax.nn.silu(pre).astype(bf16), (back * silu_grad(pre)).astype(bf16)], axis=1
     )
     share = jnp.broadcast_to(share[None], (lines,) + share.shape)
-    full = lax.all_to_all(share, "dp", 0, 0, axis_index_groups=along_x, tiled=True)
+    full = lax.all_to_all(share, "dp", 0, 0, axis_index_groups=peers, tiled=True)
     full = full.reshape(-1, 2 * hidden_cols)
     hidden, preact_grad = full[:, :hidden_cols], full[:, hidden_cols:]
 

time: 217 us -> 197 us (0.908)
  waiting for transfers between devices: 88.1 us -> 74.3 us
  starting transfers between devices: 63.7 us -> 58.6 us
    ppermute x1, waiting for transfers between devices: 25.3 us -> 8.18 us  [on_device(): came_up = lax.ppermute(w_up, 'dp', swap_side)]
    ppermute x1, waiting for transfers between devices: 23.2 us -> 7.33 us  [on_device(): lax.ppermute(grad_up[features:].astype(bf16), 'dp', swap_side)]
    all_to_all x1, waiting for transfers between devices: 0.01 us -> 15.3 us  [on_device(): arrived = lax.all_to_all(packed, 'expert', 0, 0, tiled=True)]
    all_to_all x1, waiting for transfers between devices: 0.01 us -> 14.3 us  [on_device(): lax.all_to_all(chip_sum.reshape(columns, capacity, wide), 'expert', 0, 0,...]
    all_to_all x1, starting transfers between devices: 13 us -> 7.75 us  [on_device(): lax.all_to_all(chip_sum.reshape(columns, capacity, wide), 'expert', 0, 0,...]
    all_to_all x1, waiting for transfers between devices: 27.2 us -> 22.3 us  [on_device(): lax.all_to_all(share, 'dp', 0, 0, axis_index_groups=peers, tiled=True)]
    ppermute x1, waiting for transfers between devices: 4.25 us -> 0.01 us  [on_device(): lax.ppermute(grad_down_t[features:].astype(bf16), 'dp', swap_side)]
    ppermute x1, waiting for transfers between devices: 3.1 us -> 0.01 us  [on_device(): came_down = lax.ppermute(w_down.T, 'dp', swap_side)]
where the time goes in v3:
time: 197 us
  waiting for transfers between devices  74.3 us (38%)
  starting transfers between devices  58.6 us (30%)
  blocking collectives  38.9 us (20%)
  matrix products  9.98 us (5%)
  other arithmetic  9.32 us (5%)
  local copies, waits for them, and re-layouts  4.4 us (2%)
    all_to_all x1, blocking collectives, on_device(): got = lax.all_to_all(parts, 'dp', 0, 0, axis_index_groups=peers, tiled=True)  33.4 us
    all_to_all x1, starting transfers between devices, on_device(): arrived = lax.all_to_all(packed, 'expert', 0, 0, tiled=True)  25.3 us
    all_to_all x1, waiting for transfers between devices, on_device(): lax.all_to_all(share, 'dp', 0, 0, axis_index_groups=peers, tiled=True)  22.3 us
    all_to_all x1, waiting for transfers between devices, on_device(): arrived = lax.all_to_all(packed, 'expert', 0, 0, tiled=True)  15.3 us
    all_to_all x1, waiting for transfers between devices, on_device(): lax.all_to_all(chip_sum.reshape(columns, capacity, wide), 'expert', 0, 0,...  14.3 us
    ppermute x1, waiting for transfers between devices, on_device(): came_up = lax.ppermute(w_up, 'dp', swap_side)  8.18 us
    all_to_all x1, starting transfers between devices, on_device(): lax.all_to_all(chip_sum.reshape(columns, capacity, wide), 'expert', 0, 0,...  7.75 us
    ppermute x1, waiting for transfers between devices, on_device(): lax.ppermute(grad_up[features:].astype(bf16), 'dp', swap_side)  7.33 us
  transfers between devices with their start and end apart: 10, of which 8 were waited for; matrix products, arithmetic and copies ran while one was open for 4% of the time, Pallas kernels for 0%

profile of v3, /device:TPU:1, one launch (start us, length us, event | category | flops | bytes accessed | tf_op | source)
XLA Modules:
  0.0 196.6 jit_solution(3148328011948992851)
XLA Ops:
  0.7 1.0 fusion.18
  1.7 0.9 fusion.22
  2.6 3.9 %collective-permute-start = (bf16[2,64,448]{2,1,0:T(8,128)(2,1)S(1)}, bf16[2,64,448]{2,1,0:T(8,128)(2,1)S(1)}, u32[]{:S(2)}, u32[]{:S(2)}) collective-permute-start(bf16[2,64,448]{2,1,0:T(8,128)(2,1)S(1)} %get-tuple-element.11), channel_id=1, source_target_pairs={{0,128},{64,192},{128,0},{192,64},{256,384},{320,448},{384,256},{4... | collective-permute-start | bytes 344072 | tf_op jit(solution)/shard_map/ppermute | solution.py:43
  6.5 0.7 fusion.31
  7.2 0.2 convert_reduce_fusion.1
  7.4 0.7 multiply_add_fusion
  8.0 0.8 collective-permute-done
  8.9 0.4 fusion
  9.3 0.0 copy-start.5
  9.3 0.0 copy-start.7
  9.3 1.0 broadcast_in_dim.6
  10.3 25.3 %all-to-all-start = ((bf16[64,8,896]{2,1,0:T(8,128)(2,1)}), bf16[64,8,896]{2,1,0:T(8,128)(2,1)S(1)}, u32[]{:S(2)}, u32[]{:S(2)}) async-start(bf16[64,8,896]{2,1,0:T(8,128)(2,1)} %bitcast.11), calls=%async_computation | async-start | bytes 1835008 | tf_op jit(solution)/shard_map/all_to_all | solution.py:63
  35.6 0.0 copy-done.5
  35.6 3.1 %collective-permute-start.1 = (bf16[448,512]{1,0:T(8,128)(2,1)S(1)}, bf16[448,512]{1,0:T(8,128)(2,1)S(1)}, u32[]{:S(2)}, u32[]{:S(2)}) collective-permute-start(bf16[448,512]{1,0:T(8,128)(2,1)S(1)} %copy-done.5), channel_id=1, source_target_pairs={{0,128},{64,192},{128,0},{192,64},{256,384},{320,448},{384,256},{4... | collective-permute-start | bytes 1376264 | tf_op jit(solution)/shard_map/ppermute | solution.py:44
  38.8 0.0 copy-done.7
  38.8 2.2 %collective-permute-start.2 = (bf16[448,512]{1,0:T(8,128)(2,1)S(1)}, bf16[448,512]{1,0:T(8,128)(2,1)}, u32[]{:S(2)}, u32[]{:S(2)}) collective-permute-start(bf16[448,512]{1,0:T(8,128)(2,1)S(1)} %bitcast.74), channel_id=1, source_target_pairs={{0,128},{64,192},{128,0},{192,64},{256,384},{320,448},{384,256},{4... | collective-permute-start | bytes 1376264 | tf_op jit(solution)/shard_map/ppermute | solution.py:45
  41.0 8.2 %collective-permute-done.1 = bf16[448,512]{1,0:T(8,128)(2,1)S(1)} collective-permute-done((bf16[448,512]{1,0:T(8,128)(2,1)S(1)}, bf16[448,512]{1,0:T(8,128)(2,1)S(1)}, u32[]{:S(2)}, u32[]{:S(2)}) %collective-permute-start.1) | collective-permute-done | bytes 458784 | tf_op jit(solution)/shard_map/ppermute | solution.py:44
  49.2 0.0 copy-start.3
  49.2 15.3 %all-to-all-done = bf16[64,8,896]{2,1,0:T(8,128)(2,1)S(1)} async-done(((bf16[64,8,896]{2,1,0:T(8,128)(2,1)}), bf16[64,8,896]{2,1,0:T(8,128)(2,1)S(1)}, u32[]{:S(2)}, u32[]{:S(2)}) %all-to-all-start) | async-done | bytes 917536 | tf_op jit(solution)/shard_map/all_to_all | solution.py:63
  64.5 0.1 slice_bitcast_fusion.5
  64.6 3.1 %all_gather.7 = bf16[2,256,896]{2,1,0:T(8,128)(2,1)S(1)} all-gather(bf16[1,256,896]{2,1,0:T(8,128)(2,1)S(1)} %get-tuple-element.5), channel_id=1, replica_groups={{0,1},{2,3},{4,5},{6,7},{8,9},{10,11},{12,13},{14,15},{16,17},{18,19},{..., dimensions={0}, use_global_device_ids=true | all-gather | bytes 1376256 | tf_op jit(solution)/shard_map/all_gather | solution.py:66
  67.7 0.4 convolution_convert_fusion.4
  68.1 2.5 %all_gather.6 = bf16[2,256,896]{2,1,0:T(8,128)(2,1)S(1)} all-gather(bf16[1,256,896]{2,1,0:T(8,128)(2,1)S(1)} %get-tuple-element.4), channel_id=1, replica_groups={{0,1},{2,3},{4,5},{6,7},{8,9},{10,11},{12,13},{14,15},{16,17},{18,19},{..., dimensions={0}, use_global_device_ids=true | all-gather | bytes 1376256 | tf_op jit(solution)/shard_map/all_gather | solution.py:66
  70.6 0.0 copy-done.3
  70.6 0.4 convolution_convert_fusion.6
  71.0 0.0 collective-permute-done.2
  71.0 1.5 convolution_convert_fusion.3
  72.5 1.5 convolution_convert_fusion.5
  73.9 0.1 maximum_maximum_fusion
  74.1 33.4 %all_to_all.20 = bf16[8,64,1024]{2,1,0:T(8,128)(2,1)S(1)} all-to-all(bf16[8,64,1024]{2,1,0:T(8,128)(2,1)S(1)} %bitcast.70), channel_id=1, replica_groups={{0,64,256,320,512,576,768,832},{128,192,384,448,640,704,896,960},{1,65,..., dimensions={0} | all-to-all | bytes 2097152 | tf_op jit(solution)/shard_map/all_to_all | solution.py:76
  107.4 0.2 convert_reduce_fusion
  107.6 0.1 multiply_convert_fusion.1
  107.7 1.1 broadcast_in_dim.7
  108.8 4.5 %all-to-all-start.2 = ((bf16[8,64,1024]{2,1,0:T(8,128)(2,1)}), bf16[8,64,1024]{2,1,0:T(8,128)(2,1)S(1)}, u32[]{:S(2)}, u32[]{:S(2)}) async-start(bf16[8,64,1024]{2,1,0:T(8,128)(2,1)} %broadcast_in_dim.7), calls=%async_computation.2 | async-start | bytes 2097152 | tf_op jit(solution)/shard_map/all_to_all | solution.py:83
  113.4 22.3 %all-to-all-done.2 = bf16[8,64,1024]{2,1,0:T(8,128)(2,1)S(1)} async-done(((bf16[8,64,1024]{2,1,0:T(8,128)(2,1)}), bf16[8,64,1024]{2,1,0:T(8,128)(2,1)S(1)}, u32[]{:S(2)}, u32[]{:S(2)}) %all-to-all-start.2) | async-done | bytes 1048608 | tf_op jit(solution)/shard_map/all_to_all | solution.py:83
  135.7 1.8 convolution_convert_fusion.1
  137.6 2.0 %broadcast_select_fusion = (bf16[512,896]{1,0:T(8,128)(2,1)}, bf16[512,896]{1,0:T(8,128)(2,1)}) fusion(bf16[512,896]{1,0:T(8,128)(2,1)S(1)} %convolution_convert_fusion.1, pred[]{:T(512)S(6)} %eq.23, bf16[896,512]{1,0:T(8,128)(2,1)S(1)} %copy-done.4, bf16[512,1024]{1,0:T(8,128)(2,1)S(1)} %bitcast.65), kind=kOutput, calls=%fused_computation.22 | convolution fusion | flops 470679552 | bytes 4194305 | tf_op jit(solution)/shard_map/dot_general | solution.py:90
  139.6 4.5 %collective-permute-start.3 = (bf16[512,896]{1,0:T(8,128)(2,1)}, bf16[512,896]{1,0:T(8,128)(2,1)}, u32[]{:S(2)}, u32[]{:S(2)}) collective-permute-start(bf16[512,896]{1,0:T(8,128)(2,1)} %get-tuple-element.16), channel_id=1, source_target_pairs={{0,1},{1,0},{2,3},{3,2},{4,5},{5,4},{6,7},{7,6},{8,9},{9,8},{10,11... | collective-permute-start | bytes 2752520 | tf_op jit(solution)/shard_map/ppermute | solution.py:95
  144.1 2.4 %collective-permute-done.3 = bf16[512,896]{1,0:T(8,128)(2,1)} collective-permute-done((bf16[512,896]{1,0:T(8,128)(2,1)}, bf16[512,896]{1,0:T(8,128)(2,1)}, u32[]{:S(2)}, u32[]{:S(2)}) %collective-permute-start.3) | collective-permute-done | bytes 917536 | tf_op jit(solution)/shard_map/ppermute | solution.py:95
  146.5 2.7 %fusion.1 = bf16[64,8,896]{2,1,0:T(8,128)(2,1)} fusion(bf16[512,896]{1,0:T(8,128)(2,1)} %collective-permute-done.3, bf16[512,896]{1,0:T(8,128)(2,1)} %copy-done.2, bf16[512,896]{1,0:T(8,128)(2,1)} %get-tuple-element.17, pred[]{:T(512)S(6)} %eq.23), kind=kLoop, calls=%fused_computation.14 | loop fusion | flops 2293760 | bytes 3670017 | tf_op jit(solution)/shard_map/reshape | solution.py:98
  149.2 7.7 %all-to-all-start.3 = ((bf16[64,8,896]{2,1,0:T(8,128)(2,1)}), bf16[64,8,896]{2,1,0:T(8,128)(2,1)}, u32[]{:S(2)}, u32[]{:S(2)}) async-start(bf16[64,8,896]{2,1,0:T(8,128)(2,1)} %fusion.1), calls=%async_computation.3 | async-start | bytes 1835008 | tf_op jit(solution)/shard_map/all_to_all | solution.py:97
  157.0 0.0 copy-done.6
  157.0 0.1 iota_compare_fusion
  157.1 0.4 fusion.7
  157.5 0.4 convolution_add_fusion.1
  158.0 0.1 slice.203
  158.0 2.1 %collective-permute-start.5 = (bf16[448,512]{1,0:T(8,128)(2,1)S(1)}, bf16[448,512]{1,0:T(8,128)(2,1)S(1)}, u32[]{:S(2)}, u32[]{:S(2)}) collective-permute-start(bf16[448,512]{1,0:T(8,128)(2,1)S(1)} %slice.203), channel_id=1, source_target_pairs={{0,128},{64,192},{128,0},{192,64},{256,384},{320,448},{384,256},{4... | collective-permute-start | bytes 1376264 | tf_op jit(solution)/shard_map/ppermute | solution.py:121
  160.1 0.4 fusion.8
  160.5 0.4 convolution_add_fusion
  161.0 0.1 slice.202
  161.0 3.4 %collective-permute-start.6 = (bf16[448,512]{1,0:T(8,128)(2,1)S(1)}, bf16[448,512]{1,0:T(8,128)(2,1)S(1)}, u32[]{:S(2)}, u32[]{:S(2)}) collective-permute-start(bf16[448,512]{1,0:T(8,128)(2,1)S(1)} %slice.202), channel_id=1, source_target_pairs={{0,128},{64,192},{128,0},{192,64},{256,384},{320,448},{384,256},{4... | collective-permute-start | bytes 1376264 | tf_op jit(solution)/shard_map/ppermute | solution.py:122
  164.4 7.3 %collective-permute-done.5 = bf16[448,512]{1,0:T(8,128)(2,1)S(1)} collective-permute-done((bf16[448,512]{1,0:T(8,128)(2,1)S(1)}, bf16[448,512]{1,0:T(8,128)(2,1)S(1)}, u32[]{:S(2)}, u32[]{:S(2)}) %collective-permute-start.5) | collective-permute-done | bytes 458784 | tf_op jit(solution)/shard_map/ppermute | solution.py:121
  171.7 0.9 fusion.3
  172.7 14.3 %all-to-all-done.3 = bf16[64,8,896]{2,1,0:T(8,128)(2,1)} async-done(((bf16[64,8,896]{2,1,0:T(8,128)(2,1)}), bf16[64,8,896]{2,1,0:T(8,128)(2,1)}, u32[]{:S(2)}, u32[]{:S(2)}) %all-to-all-start.3) | async-done | bytes 917536 | tf_op jit(solution)/shard_map/all_to_all | solution.py:97
  186.9 1.3 copy.15
  188.2 0.3 convolution_bitcast_fusion
  188.5 0.1 fusion.13
  188.6 0.1 pad_maximum_fusion.4
  188.7 1.9 collective-permute-start.4
  190.6 0.0 collective-permute-done.6
  190.6 0.9 fusion.6
  191.5 3.7 %collective-permute-done.4 = bf16[2,64,448]{2,1,0:T(8,128)(2,1)S(1)} collective-permute-done((bf16[2,64,448]{2,1,0:T(8,128)(2,1)S(1)}, bf16[2,64,448]{2,1,0:T(8,128)(2,1)S(1)}, u32[]{:S(2)}, u32[]{:S(2)}) %collective-permute-start.4) | collective-permute-done | bytes 114720 | tf_op jit(solution)/shard_map/ppermute | solution.py:105
  195.3 0.7 pad_maximum_fusion.6
  195.9 0.7 pad_maximum_fusion.7
  (18 shorter events, 0.2 us)
Async XLA Ops:
  2.6 6.3 %collective-permute-start = (bf16[2,64,448]{2,1,0:T(8,128)(2,1)S(1)}, bf16[2,64,448]{2,1,0:T(8,128)(2,1)S(1)}, u32[]{:S(2)}, u32[]{:S(2)}) collective-permute-start(bf16[2,64,448]{2,1,0:T(8,128)(2,1)S(1)} %get-tuple-element.11), channel_id=1, source_target_pairs={{0,128},{64,192},{128,0},{192,64},{256,384},{320,448},{384,256},{4... | collective-permute-start | bytes 344072 | tf_op jit(solution)/shard_map/ppermute | solution.py:43
  9.3 26.3 %copy-start.5 = (bf16[448,512]{1,0:T(8,128)(2,1)S(1)}, bf16[448,512]{1,0:T(8,128)(2,1)}, u32[]{:S(2)}) copy-start(bf16[448,512]{1,0:T(8,128)(2,1)} %param.10) | copy-start | bytes 1376260
  9.3 29.4 %copy-start.7 = (bf16[512,448]{0,1:T(8,128)(2,1)S(1)}, bf16[512,448]{0,1:T(8,128)(2,1)}, u32[]{:S(2)}) copy-start(bf16[512,448]{0,1:T(8,128)(2,1)} %param.11) | copy-start | bytes 1376260
  10.3 54.2 %all-to-all-start = ((bf16[64,8,896]{2,1,0:T(8,128)(2,1)}), bf16[64,8,896]{2,1,0:T(8,128)(2,1)S(1)}, u32[]{:S(2)}, u32[]{:S(2)}) async-start(bf16[64,8,896]{2,1,0:T(8,128)(2,1)} %bitcast.11), calls=%async_computation | async-start | bytes 1835008 | tf_op jit(solution)/shard_map/all_to_all | solution.py:63
  35.6 13.5 %collective-permute-start.1 = (bf16[448,512]{1,0:T(8,128)(2,1)S(1)}, bf16[448,512]{1,0:T(8,128)(2,1)S(1)}, u32[]{:S(2)}, u32[]{:S(2)}) collective-permute-start(bf16[448,512]{1,0:T(8,128)(2,1)S(1)} %copy-done.5), channel_id=1, source_target_pairs={{0,128},{64,192},{128,0},{192,64},{256,384},{320,448},{384,256},{4... | collective-permute-start | bytes 1376264 | tf_op jit(solution)/shard_map/ppermute | solution.py:44
  38.8 32.2 %collective-permute-start.2 = (bf16[448,512]{1,0:T(8,128)(2,1)S(1)}, bf16[448,512]{1,0:T(8,128)(2,1)}, u32[]{:S(2)}, u32[]{:S(2)}) collective-permute-start(bf16[448,512]{1,0:T(8,128)(2,1)S(1)} %bitcast.74), channel_id=1, source_target_pairs={{0,128},{64,192},{128,0},{192,64},{256,384},{320,448},{384,256},{4... | collective-permute-start | bytes 1376264 | tf_op jit(solution)/shard_map/ppermute | solution.py:45
  49.2 21.4 %copy-start.3 = (bf16[896,512]{1,0:T(8,128)(2,1)}, bf16[896,512]{1,0:T(8,128)(2,1)S(1)}, u32[]{:S(2)}) copy-start(bf16[896,512]{1,0:T(8,128)(2,1)S(1)} %constant_dynamic-update-slice_fusion) | copy-start | bytes 2752516
  67.7 89.9 %copy-start = (bf16[2,256,896]{2,1,0:T(8,128)(2,1)}, bf16[2,256,896]{2,1,0:T(8,128)(2,1)S(1)}, u32[]{:S(2)}) copy-start(bf16[2,256,896]{2,1,0:T(8,128)(2,1)S(1)} %all_gather.7) | copy-start | bytes 2752516
  108.8 26.9 %all-to-all-start.2 = ((bf16[8,64,1024]{2,1,0:T(8,128)(2,1)}), bf16[8,64,1024]{2,1,0:T(8,128)(2,1)S(1)}, u32[]{:S(2)}, u32[]{:S(2)}) async-start(bf16[8,64,1024]{2,1,0:T(8,128)(2,1)} %broadcast_in_dim.7), calls=%async_computation.2 | async-start | bytes 2097152 | tf_op jit(solution)/shard_map/all_to_all | solution.py:83
  135.7 1.9 copy-start.4
  137.6 2.0 %copy-start.2 = (bf16[512,896]{1,0:T(8,128)(2,1)}, bf16[512,896]{1,0:T(8,128)(2,1)S(1)}, u32[]{:S(2)}) copy-start(bf16[512,896]{1,0:T(8,128)(2,1)S(1)} %convolution_convert_fusion.1) | copy-start | bytes 2752516
  139.6 6.9 %collective-permute-start.3 = (bf16[512,896]{1,0:T(8,128)(2,1)}, bf16[512,896]{1,0:T(8,128)(2,1)}, u32[]{:S(2)}, u32[]{:S(2)}) collective-permute-start(bf16[512,896]{1,0:T(8,128)(2,1)} %get-tuple-element.16), channel_id=1, source_target_pairs={{0,1},{1,0},{2,3},{3,2},{4,5},{5,4},{6,7},{7,6},{8,9},{9,8},{10,11... | collective-permute-start | bytes 2752520 | tf_op jit(solution)/shard_map/ppermute | solution.py:95
  149.2 7.8 %copy-start.6 = (f32[2,64,1]{1,2,0:T(1,128)S(1)}, f32[2,64,1]{1,2,0:T(1,128)}, u32[]{:S(2)}) copy-start(f32[2,64,1]{1,2,0:T(1,128)} %param.9) | copy-start | bytes 1540
  149.2 37.7 %all-to-all-start.3 = ((bf16[64,8,896]{2,1,0:T(8,128)(2,1)}), bf16[64,8,896]{2,1,0:T(8,128)(2,1)}, u32[]{:S(2)}, u32[]{:S(2)}) async-start(bf16[64,8,896]{2,1,0:T(8,128)(2,1)} %fusion.1), calls=%async_computation.3 | async-start | bytes 1835008 | tf_op jit(solution)/shard_map/all_to_all | solution.py:97
  158.0 2.6 %copy-start.1 = (bf16[2,256,896]{2,1,0:T(8,128)(2,1)S(1)}, bf16[2,256,896]{2,1,0:T(8,128)(2,1)}, u32[]{:S(2)}) copy-start(bf16[2,256,896]{2,1,0:T(8,128)(2,1)} %copy-done) | copy-start | bytes 2752516
  158.0 13.7 %collective-permute-start.5 = (bf16[448,512]{1,0:T(8,128)(2,1)S(1)}, bf16[448,512]{1,0:T(8,128)(2,1)S(1)}, u32[]{:S(2)}, u32[]{:S(2)}) collective-permute-start(bf16[448,512]{1,0:T(8,128)(2,1)S(1)} %slice.203), channel_id=1, source_target_pairs={{0,128},{64,192},{128,0},{192,64},{256,384},{320,448},{384,256},{4... | collective-permute-start | bytes 1376264 | tf_op jit(solution)/shard_map/ppermute | solution.py:121
  161.0 29.6 %collective-permute-start.6 = (bf16[448,512]{1,0:T(8,128)(2,1)S(1)}, bf16[448,512]{1,0:T(8,128)(2,1)S(1)}, u32[]{:S(2)}, u32[]{:S(2)}) collective-permute-start(bf16[448,512]{1,0:T(8,128)(2,1)S(1)} %slice.202), channel_id=1, source_target_pairs={{0,128},{64,192},{128,0},{192,64},{256,384},{320,448},{384,256},{4... | collective-permute-start | bytes 1376264 | tf_op jit(solution)/shard_map/ppermute | solution.py:122
  188.7 6.5 %collective-permute-start.4 = (bf16[2,64,448]{2,1,0:T(8,128)(2,1)S(1)}, bf16[2,64,448]{2,1,0:T(8,128)(2,1)S(1)}, u32[]{:S(2)}, u32[]{:S(2)}) collective-permute-start(bf16[2,64,448]{2,1,0:T(8,128)(2,1)S(1)} %pad_maximum_fusion.4), channel_id=1, source_target_pairs={{0,128},{64,192},{128,0},{192,64},{256,384},{320,448},{384,256},{4... | collective-permute-start | bytes 344072 | tf_op jit(solution)/shard_map/ppermute | solution.py:105

commit v4 on v3

v4 whole, which is shorter than its diff:
```python
import jax
import jax.numpy as jnp
from jax import lax
from jax.sharding import PartitionSpec as P

FF = 2048


def silu_grad(preact):
    logistic = jax.nn.sigmoid(preact)
    return logistic * (1.0 + preact * (1.0 - logistic))


def on_device(tokens, out_grad, expert_ids, gate_weights, w_up, w_down):
    micro_count, token_count, features = tokens.shape
    hidden_cols = w_up.shape[1]
    columns = lax.axis_size("expert")
    dp = lax.axis_size("dp")
    lines = dp // 2
    groups_per = FF // hidden_cols
    chips_per = groups_per // 2
    experts = columns // groups_per
    capacity = 2 * token_count // experts
    wide = 2 * features
    bf16 = jnp.bfloat16
    f32 = jnp.float32
    contract_last = (((1,), (1,)), ((), ()))
    contract_first = (((0,), (0,)), ((), ()))
    swap_core = [(i, i ^ 1) for i in range(columns)]
    swap_side = [(i, i ^ 2) for i in range(dp)]
    peers = [[i for i in range(dp) if i // 2 % 2 == side] for side in range(2)]
    first_core = (lax.axis_index("expert") & 1) == 0
    on_second = (lax.axis_index("dp") & 2) == 2

    def pick(array):
        return jnp.where(on_second, array[1], array[0])

    given = jnp.stack(
        [jnp.where(on_second, array[0], array[1]) for array in (tokens, out_grad)]
    )
    came_rows = lax.ppermute(given, "dp", swap_side)

    w_down_t = w_down.T
    in_own = jnp.where(first_core, w_up, w_down_t)
    out_own = jnp.where(first_core, w_down_t, w_up)
    in_own = jnp.concatenate([in_own, lax.ppermute(in_own, "dp", swap_side)], axis=0)
    out_own = jnp.concatenate([out_own, lax.ppermute(out_own, "dp", swap_side)], axis=0)
    in_other = lax.ppermute(out_own, "expert", swap_core)
    out_other = lax.ppermute(in_own, "expert", swap_core)
    in_both = lax.optimization_barrier(jnp.concatenate([in_own, in_other], axis=1))
    out_both = lax.optimization_barrier(jnp.concatenate([out_own, out_other], axis=1))

    routing = pick(expert_ids)[:, 0]
    gate = pick(gate_weights)
    ones = jnp.ones_like(gate)
    earlier = jnp.tril(jnp.ones((token_count, token_count), jnp.bool_), -1)
    same = (routing[:, None] == routing[None, :]) & earlier
    slots = routing * capacity + jnp.sum(same.astype(jnp.int32), axis=1)
    row = jnp.arange(columns * capacity, dtype=jnp.int32)
    device, place = row // capacity, row % capacity
    row_key = (device // groups_per * capacity + place) * 2 + device % 2
    column_key = jnp.concatenate([2 * slots, 2 * slots + 1])
    table = (row_key[:, None] == column_key[None, :]).astype(bf16)

    held = jnp.stack([pick(tokens), pick(out_grad)])
    sent = jnp.concatenate([held, came_rows], axis=2).astype(f32)
    sent = (jnp.stack([ones, gate]) * sent).astype(bf16).reshape(2 * token_count, wide)
    packed = jnp.dot(table, sent, preferred_element_type=f32).astype(bf16)
    packed = packed.reshape(columns, capacity, wide)
    rows = lax.all_to_all(packed, "expert", 0, 0, tiled=True)
    rows = rows.reshape(columns * capacity, wide)
    other_rows = lax.ppermute(rows, "expert", swap_core)

    parts = jnp.dot(rows, in_both, preferred_element_type=f32).astype(bf16)
    parts = parts.reshape(lines, -1, 2 * hidden_cols)
    got = lax.all_to_all(parts, "dp", 0, 0, axis_index_groups=peers, tiled=True)
    total = jnp.sum(got.astype(f32), axis=0)
    pre = lax.ppermute(total, "expert", swap_core)
    pre = jnp.concatenate([pre[:, hidden_cols:], pre[:, :hidden_cols]], axis=1)
    share = jnp.where(first_core, jax.nn.silu(total), total * silu_grad(pre)).astype(bf16)
    share = jnp.broadcast_to(share[None], (lines,) + share.shape)
    full = lax.all_to_all(share, "dp", 0, 0, axis_index_groups=peers, tiled=True)
    full = full.reshape(-1, 2 * hidden_cols)
    chip_sum = lax.dot_general(
        full, out_both, contract_last, preferred_element_type=f32
    ).astype(bf16)

    home = lax.all_to_all(
        chip_sum.reshape(columns, capacity, wide), "expert", 0, 0, tiled=True
    )
    summed = lax.dot_general(
        table, home.reshape(-1, wide), contract_first, preferred_element_type=f32
    )
    done = (jnp.stack([gate, ones]) * summed.reshape(2, token_count, wide)).astype(bf16)
    came_done = lax.ppermute(done[:, :, features:], "dp", swap_side)
    own_done = done[:, :, :features]
    is_mine = (jnp.arange(micro_count) == 1)[:, None, None] == on_second

    def grad_of(columns_of):
        whole = lax.dot_general(
            other_rows, columns_of, contract_first, preferred_element_type=f32
        )
        came = lax.ppermute(whole[features:].astype(bf16), "dp", swap_side)
        return (whole[:features] + came.astype(f32)).astype(bf16)

    grad_given = grad_of(full[:, hidden_cols:])
    grad_came = lax.ppermute(grad_given, "expert", swap_core)
    grad_own = grad_of(full[:, :hidden_cols])
    return (
        jnp.where(is_mine, own_done[0][None], came_done[0][None]),
        jnp.where(is_mine, own_done[1][None], came_done[1][None]),
        jnp.where(first_core, grad_came, grad_own),
        jnp.where(first_core, grad_own, grad_came).T,
    )


def solution(mesh):
    in_specs = (
        P(None, "expert", "dp"),
        P(None, "expert", "dp"),
        P(None, "expert", None),
        P(None, "expert", None),
        P("dp", "expert"),
        P("expert", "dp"),
    )
    out_specs = (
        P(None, "expert", "dp"),
        P(None, "expert", "dp"),
        P("dp", "expert"),
        P("expert", "dp"),
    )
    return jax.shard_map(
        on_device, mesh=mesh, in_specs=in_specs, out_specs=out_specs, check_vma=False
    )
```

time: 197 us -> 197 us (level)
  starting transfers between devices: 58.6 us -> 76 us
  waiting for transfers between devices: 74.3 us -> 65 us
  blocking collectives: 38.9 us -> 33.6 us
  local copies, waits for them, and re-layouts: 4.4 us -> 1.5 us
    ppermute x6 -> x10, waiting for transfers between devices: 18.8 us -> 35.6 us  [the longest x2 13 us: grad_of(): came = lax.ppermute(whole[features:].astype(bf16), 'dp', swap_side)]
    all_to_all x1, waiting for transfers between devices: 15.3 us -> 0.01 us  [on_device(): rows = lax.all_to_all(packed, 'expert', 0, 0, tiled=True)]
    ppermute x6 -> x10, starting transfers between devices: 19.1 us -> 30.5 us  [the longest x2 5.29 us: grad_of(): came = lax.ppermute(whole[features:].astype(bf16), 'dp', swap_side)]
    all_to_all x1, waiting for transfers between devices: 14.3 us -> 4.82 us  [on_device(): lax.all_to_all(chip_sum.reshape(columns, capacity, wide), 'expert', 0, 0,...]
    all_to_all x1, starting transfers between devices: 7.75 us -> 14.4 us  [on_device(): lax.all_to_all(chip_sum.reshape(columns, capacity, wide), 'expert', 0, 0,...]
    all_gather x2 -> x0, blocking collectives: 5.52 us -> none  [on_device(): lax.all_gather(half, 'expert', axis=0, axis_index_groups=cores, tiled=True)]
    select_n x1 -> x5, other arithmetic: 0.02 us -> 3.17 us  [the longest x3 2.31 us: pick(): return jnp.where(on_second, array[1], array[0])]
    concatenate x2 -> x6, other arithmetic: 0.15 us -> 3.24 us  [the longest x1 1.52 us: on_device(): jnp.concatenate([in_own, in_other], axis=1)]
  transfers between devices with their start and end apart: 10 -> 14, of which waited for: 8 -> 9; matrix products, arithmetic and copies ran while one was open for 4% -> 6% of each run, Pallas kernels for 0% -> 0%
where the time goes in v4:
time: 197 us; the launch traced here: 196 us
  starting transfers between devices  76 us (39%)
  waiting for transfers between devices  65 us (33%)
  blocking collectives  33.6 us (17%)
  matrix products  9.86 us (5%)
  other arithmetic  8.98 us (5%)
    all_to_all x1, blocking collectives, on_device(): got = lax.all_to_all(parts, 'dp', 0, 0, axis_index_groups=peers, tiled=True)  33.6 us
    all_to_all x1, starting transfers between devices, on_device(): rows = lax.all_to_all(packed, 'expert', 0, 0, tiled=True)  25.3 us
    all_to_all x1, waiting for transfers between devices, on_device(): lax.all_to_all(share, 'dp', 0, 0, axis_index_groups=peers, tiled=True)  20.1 us
    all_to_all x1, starting transfers between devices, on_device(): lax.all_to_all(chip_sum.reshape(columns, capacity, wide), 'expert', 0, 0,...  14.4 us
    ppermute x2, waiting for transfers between devices, grad_of(): came = lax.ppermute(whole[features:].astype(bf16), 'dp', swap_side)  13 us
    ppermute x1, waiting for transfers between devices, on_device(): lax.ppermute(in_own, 'dp', swap_side)  10.9 us
    ppermute x1, waiting for transfers between devices, on_device(): lax.ppermute(out_own, 'dp', swap_side)  10.4 us
    ppermute x2, starting transfers between devices, grad_of(): came = lax.ppermute(whole[features:].astype(bf16), 'dp', swap_side)  5.29 us
  transfers between devices with their start and end apart: 14, of which 9 were waited for; matrix products, arithmetic and copies ran while one was open for 6% of the time, Pallas kernels for 0%

profile of v4, /device:TPU:1, one launch (start us, length us, event | category | flops | bytes accessed | tf_op | source)
XLA Modules:
  0.0 195.9 jit_solution(8471181116500124556)
XLA Ops:
  0.6 1.0 broadcast_select_fusion.5
  1.6 0.0 copy-start
  1.6 0.0 copy-start.1
  1.7 4.1 %collective-permute-start = (bf16[2,64,448]{2,1,0:T(8,128)(2,1)S(1)}, bf16[2,64,448]{2,1,0:T(8,128)(2,1)S(1)}, u32[]{:S(2)}, u32[]{:S(2)}) collective-permute-start(bf16[2,64,448]{2,1,0:T(8,128)(2,1)S(1)} %pad_maximum_fusion.6), channel_id=1, source_target_pairs={{0,128},{64,192},{128,0},{192,64},{256,384},{320,448},{384,256},{4... | collective-permute-start | bytes 344072 | tf_op jit(solution)/shard_map/ppermute | solution.py:41
  5.8 0.7 broadcast_select_fusion.8
  6.5 0.1 mul.100
  6.6 0.7 fusion.49
  7.2 0.2 convert_reduce_fusion.1
  7.4 0.7 broadcast_add_fusion
  8.1 0.1 pad_add_fusion.1
  8.2 0.0 collective-permute-done
  8.2 1.4 fusion
  9.6 25.3 %all-to-all-start = ((bf16[64,8,896]{2,1,0:T(8,128)(2,1)}), bf16[64,8,896]{2,1,0:T(8,128)(2,1)}, u32[]{:S(2)}, u32[]{:S(2)}) async-start(bf16[64,8,896]{2,1,0:T(8,128)(2,1)} %fusion), calls=%async_computation | async-start | bytes 1835008 | tf_op jit(solution)/shard_map/all_to_all | solution.py:70
  35.0 0.0 copy-done
  35.0 0.0 copy-done.1
  35.0 0.1 bitcast_select_fusion.1
  35.0 3.1 %collective-permute-start.2 = (bf16[448,512]{1,0:T(8,128)(2,1)S(1)}, bf16[448,512]{1,0:T(8,128)(2,1)S(1)}, u32[]{:S(2)}, u32[]{:S(2)}) collective-permute-start(bf16[448,512]{1,0:T(8,128)(2,1)S(1)} %get-tuple-element.11), channel_id=1, source_target_pairs={{0,128},{64,192},{128,0},{192,64},{256,384},{320,448},{384,256},{4... | collective-permute-start | bytes 1376264 | tf_op jit(solution)/shard_map/ppermute | solution.py:47
  38.2 10.4 %collective-permute-done.2 = bf16[448,512]{1,0:T(8,128)(2,1)S(1)} collective-permute-done((bf16[448,512]{1,0:T(8,128)(2,1)S(1)}, bf16[448,512]{1,0:T(8,128)(2,1)S(1)}, u32[]{:S(2)}, u32[]{:S(2)}) %collective-permute-start.2) | collective-permute-done | bytes 458784 | tf_op jit(solution)/shard_map/ppermute | solution.py:47
  48.6 0.1 pad_maximum_fusion.3
  48.7 3.2 %collective-permute-start.3 = (bf16[896,512]{1,0:T(8,128)(2,1)S(1)}, bf16[896,512]{1,0:T(8,128)(2,1)S(1)}, u32[]{:S(2)}, u32[]{:S(2)}) collective-permute-start(bf16[896,512]{1,0:T(8,128)(2,1)S(1)} %pad_maximum_fusion.3), channel_id=1, source_target_pairs={{0,1},{1,0},{2,3},{3,2},{4,5},{5,4},{6,7},{7,6},{8,9},{9,8},{10,11... | collective-permute-start | bytes 2752520 | tf_op jit(solution)/shard_map/ppermute | solution.py:48
  51.9 3.1 %collective-permute-start.1 = (bf16[448,512]{1,0:T(8,128)(2,1)S(1)}, bf16[448,512]{1,0:T(8,128)(2,1)S(1)}, u32[]{:S(2)}, u32[]{:S(2)}) collective-permute-start(bf16[448,512]{1,0:T(8,128)(2,1)S(1)} %get-tuple-element.10), channel_id=1, source_target_pairs={{0,128},{64,192},{128,0},{192,64},{256,384},{320,448},{384,256},{4... | collective-permute-start | bytes 1376264 | tf_op jit(solution)/shard_map/ppermute | solution.py:46
  55.0 10.9 %collective-permute-done.1 = bf16[448,512]{1,0:T(8,128)(2,1)S(1)} collective-permute-done((bf16[448,512]{1,0:T(8,128)(2,1)S(1)}, bf16[448,512]{1,0:T(8,128)(2,1)S(1)}, u32[]{:S(2)}, u32[]{:S(2)}) %collective-permute-start.1) | collective-permute-done | bytes 458784 | tf_op jit(solution)/shard_map/ppermute | solution.py:46
  65.9 0.0 collective-permute-done.3
  65.9 1.5 pad_maximum_fusion
  67.4 0.0 all-to-all-done
  67.4 3.0 %convolution_convert_fusion = bf16[512,1024]{1,0:T(8,128)(2,1)S(1)} fusion(bf16[896,1024]{1,0:T(8,128)(2,1)} %pad_maximum_fusion, bf16[64,8,896]{2,1,0:T(8,128)(2,1)} %all-to-all-done), kind=kOutput, calls=%fused_computation.3 | convolution fusion | flops 940048384 | bytes 3801088 | tf_op jit(solution)/shard_map/dot_general | solution.py:74
  70.5 33.6 %all_to_all.20 = bf16[8,64,1024]{2,1,0:T(8,128)(2,1)S(1)} all-to-all(bf16[8,64,1024]{2,1,0:T(8,128)(2,1)S(1)} %bitcast.48), channel_id=1, replica_groups={{0,64,256,320,512,576,768,832},{128,192,384,448,640,704,896,960},{1,65,..., dimensions={0} | all-to-all | bytes 2097152 | tf_op jit(solution)/shard_map/all_to_all | solution.py:76
  104.0 0.2 convert_reduce_fusion
  104.2 3.1 %collective-permute-start.4 = (f32[64,1024]{1,0:T(8,128)S(1)}, f32[64,1024]{1,0:T(8,128)S(1)}, u32[]{:S(2)}, u32[]{:S(2)}) collective-permute-start(f32[64,1024]{1,0:T(8,128)S(1)} %convert_reduce_fusion), channel_id=1, source_target_pairs={{0,1},{1,0},{2,3},{3,2},{4,5},{5,4},{6,7},{7,6},{8,9},{9,8},{10,11... | collective-permute-start | bytes 786440 | tf_op jit(solution)/shard_map/ppermute | solution.py:78
  107.3 1.1 collective-permute-done.4
  108.5 0.2 select_convert_fusion
  108.7 1.1 broadcast_in_dim.58
  109.8 3.9 %all-to-all-start.2 = ((bf16[8,64,1024]{2,1,0:T(8,128)(2,1)}), bf16[8,64,1024]{2,1,0:T(8,128)(2,1)S(1)}, u32[]{:S(2)}, u32[]{:S(2)}) async-start(bf16[8,64,1024]{2,1,0:T(8,128)(2,1)} %broadcast_in_dim.58), calls=%async_computation.2 | async-start | bytes 2097152 | tf_op jit(solution)/shard_map/all_to_all | solution.py:82
  113.7 0.1 pad_maximum_fusion.2
  113.7 2.6 %collective-permute-start.5 = (bf16[896,512]{1,0:T(8,128)(2,1)S(1)}, bf16[896,512]{1,0:T(8,128)(2,1)S(1)}, u32[]{:S(2)}, u32[]{:S(2)}) collective-permute-start(bf16[896,512]{1,0:T(8,128)(2,1)S(1)} %pad_maximum_fusion.2), channel_id=1, source_target_pairs={{0,1},{1,0},{2,3},{3,2},{4,5},{5,4},{6,7},{7,6},{8,9},{9,8},{10,11... | collective-permute-start | bytes 2752520 | tf_op jit(solution)/shard_map/ppermute | solution.py:49
  116.3 1.9 collective-permute-start.7
  118.2 0.1 collective-permute-done.5
  118.4 1.5 pad_maximum_fusion.1
  119.9 20.1 %all-to-all-done.2 = bf16[8,64,1024]{2,1,0:T(8,128)(2,1)S(1)} async-done(((bf16[8,64,1024]{2,1,0:T(8,128)(2,1)}), bf16[8,64,1024]{2,1,0:T(8,128)(2,1)S(1)}, u32[]{:S(2)}, u32[]{:S(2)}) %all-to-all-start.2) | async-done | bytes 1048608 | tf_op jit(solution)/shard_map/all_to_all | solution.py:82
  139.9 3.7 %fusion.1 = bf16[64,8,896]{2,1,0:T(8,128)(2,1)} fusion(bf16[512,1024]{1,0:T(8,128)(2,1)S(1)} %bitcast.45, bf16[896,1024]{1,0:T(8,128)(2,1)} %pad_maximum_fusion.1), kind=kOutput, calls=%fused_computation.7 | convolution fusion | flops 939982848 | bytes 3801088 | tf_op jit(solution)/shard_map/dot_general | solution.py:84
  143.7 14.4 %all-to-all-start.3 = ((bf16[64,8,896]{2,1,0:T(8,128)(2,1)}), bf16[64,8,896]{2,1,0:T(8,128)(2,1)S(1)}, u32[]{:S(2)}, u32[]{:S(2)}) async-start(bf16[64,8,896]{2,1,0:T(8,128)(2,1)} %fusion.1), calls=%async_computation.3 | async-start | bytes 1835008 | tf_op jit(solution)/shard_map/all_to_all | solution.py:88
  158.1 0.0 collective-permute-done.7
  158.1 0.7 fusion.8
  158.8 0.1 slice.139
  158.9 1.9 collective-permute-start.8
  160.8 0.7 fusion.6
  161.5 0.0 copy-start.2
  161.5 0.1 slice.138
  161.5 3.4 %collective-permute-start.10 = (bf16[448,512]{1,0:T(8,128)(2,1)S(1)}, bf16[448,512]{1,0:T(8,128)(2,1)S(1)}, u32[]{:S(2)}, u32[]{:S(2)}) collective-permute-start(bf16[448,512]{1,0:T(8,128)(2,1)S(1)} %slice.138), channel_id=1, source_target_pairs={{0,128},{64,192},{128,0},{192,64},{256,384},{320,448},{384,256},{4... | collective-permute-start | bytes 1376264 | tf_op jit(solution)/shard_map/ppermute | solution.py:103
  164.9 7.5 %collective-permute-done.8 = bf16[448,512]{1,0:T(8,128)(2,1)S(1)} collective-permute-done((bf16[448,512]{1,0:T(8,128)(2,1)S(1)}, bf16[448,512]{1,0:T(8,128)(2,1)S(1)}, u32[]{:S(2)}, u32[]{:S(2)}) %collective-permute-start.8) | collective-permute-done | bytes 458784 | tf_op jit(solution)/shard_map/ppermute | solution.py:103
  172.4 0.1 fusion.4
  172.5 4.1 %collective-permute-start.9 = (bf16[448,512]{1,0:T(8,128)(2,1)S(1)}, bf16[448,512]{1,0:T(8,128)(2,1)S(1)}, u32[]{:S(2)}, u32[]{:S(2)}) collective-permute-start(bf16[448,512]{1,0:T(8,128)(2,1)S(1)} %fusion.4), channel_id=1, source_target_pairs={{0,1},{1,0},{2,3},{3,2},{4,5},{5,4},{6,7},{7,6},{8,9},{9,8},{10,11... | collective-permute-start | bytes 1376264 | tf_op jit(solution)/shard_map/ppermute | solution.py:107
  176.7 0.0 copy-done.2
  176.7 5.5 %collective-permute-done.10 = bf16[448,512]{1,0:T(8,128)(2,1)S(1)} collective-permute-done((bf16[448,512]{1,0:T(8,128)(2,1)S(1)}, bf16[448,512]{1,0:T(8,128)(2,1)S(1)}, u32[]{:S(2)}, u32[]{:S(2)}) %collective-permute-start.10) | collective-permute-done | bytes 458784 | tf_op jit(solution)/shard_map/ppermute | solution.py:103
  182.2 0.0 collective-permute-done.9
  182.2 1.2 select_bitcast_fusion
  183.4 4.8 %all-to-all-done.3 = bf16[64,8,896]{2,1,0:T(8,128)(2,1)S(1)} async-done(((bf16[64,8,896]{2,1,0:T(8,128)(2,1)}), bf16[64,8,896]{2,1,0:T(8,128)(2,1)S(1)}, u32[]{:S(2)}, u32[]{:S(2)}) %all-to-all-start.3) | async-done | bytes 917536 | tf_op jit(solution)/shard_map/all_to_all | solution.py:88
  188.2 0.4 fusion.2
  188.6 0.1 slice.96
  188.7 1.9 collective-permute-start.6
  190.6 4.5 %collective-permute-done.6 = bf16[2,64,448]{2,1,0:T(8,128)(2,1)S(1)} collective-permute-done((bf16[2,64,448]{2,1,0:T(8,128)(2,1)S(1)}, bf16[2,64,448]{2,1,0:T(8,128)(2,1)S(1)}, u32[]{:S(2)}, u32[]{:S(2)}) %collective-permute-start.6) | collective-permute-done | bytes 114720 | tf_op jit(solution)/shard_map/ppermute | solution.py:95
  195.1 0.8 broadcast_select_fusion.1
  (11 shorter events, 0.1 us)
Async XLA Ops:
  1.6 33.4 %copy-start = (bf16[448,512]{1,0:T(8,128)(2,1)S(1)}, bf16[448,512]{1,0:T(8,128)(2,1)}, u32[]{:S(2)}) copy-start(bf16[448,512]{1,0:T(8,128)(2,1)} %param.10) | copy-start | bytes 1376260
  1.6 33.4 %copy-start.1 = (bf16[512,448]{0,1:T(8,128)(2,1)S(1)}, bf16[512,448]{0,1:T(8,128)(2,1)}, u32[]{:S(2)}) copy-start(bf16[512,448]{0,1:T(8,128)(2,1)} %param.11) | copy-start | bytes 1376260
  1.7 6.5 %collective-permute-start = (bf16[2,64,448]{2,1,0:T(8,128)(2,1)S(1)}, bf16[2,64,448]{2,1,0:T(8,128)(2,1)S(1)}, u32[]{:S(2)}, u32[]{:S(2)}) collective-permute-start(bf16[2,64,448]{2,1,0:T(8,128)(2,1)S(1)} %pad_maximum_fusion.6), channel_id=1, source_target_pairs={{0,128},{64,192},{128,0},{192,64},{256,384},{320,448},{384,256},{4... | collective-permute-start | bytes 344072 | tf_op jit(solution)/shard_map/ppermute | solution.py:41
  9.6 57.8 %all-to-all-start = ((bf16[64,8,896]{2,1,0:T(8,128)(2,1)}), bf16[64,8,896]{2,1,0:T(8,128)(2,1)}, u32[]{:S(2)}, u32[]{:S(2)}) async-start(bf16[64,8,896]{2,1,0:T(8,128)(2,1)} %fusion), calls=%async_computation | async-start | bytes 1835008 | tf_op jit(solution)/shard_map/all_to_all | solution.py:70
  35.0 13.6 %collective-permute-start.2 = (bf16[448,512]{1,0:T(8,128)(2,1)S(1)}, bf16[448,512]{1,0:T(8,128)(2,1)S(1)}, u32[]{:S(2)}, u32[]{:S(2)}) collective-permute-start(bf16[448,512]{1,0:T(8,128)(2,1)S(1)} %get-tuple-element.11), channel_id=1, source_target_pairs={{0,128},{64,192},{128,0},{192,64},{256,384},{320,448},{384,256},{4... | collective-permute-start | bytes 1376264 | tf_op jit(solution)/shard_map/ppermute | solution.py:47
  48.7 17.2 %collective-permute-start.3 = (bf16[896,512]{1,0:T(8,128)(2,1)S(1)}, bf16[896,512]{1,0:T(8,128)(2,1)S(1)}, u32[]{:S(2)}, u32[]{:S(2)}) collective-permute-start(bf16[896,512]{1,0:T(8,128)(2,1)S(1)} %pad_maximum_fusion.3), channel_id=1, source_target_pairs={{0,1},{1,0},{2,3},{3,2},{4,5},{5,4},{6,7},{7,6},{8,9},{9,8},{10,11... | collective-permute-start | bytes 2752520 | tf_op jit(solution)/shard_map/ppermute | solution.py:48
  51.9 14.0 %collective-permute-start.1 = (bf16[448,512]{1,0:T(8,128)(2,1)S(1)}, bf16[448,512]{1,0:T(8,128)(2,1)S(1)}, u32[]{:S(2)}, u32[]{:S(2)}) collective-permute-start(bf16[448,512]{1,0:T(8,128)(2,1)S(1)} %get-tuple-element.10), channel_id=1, source_target_pairs={{0,128},{64,192},{128,0},{192,64},{256,384},{320,448},{384,256},{4... | collective-permute-start | bytes 1376264 | tf_op jit(solution)/shard_map/ppermute | solution.py:46
  104.2 4.3 %collective-permute-start.4 = (f32[64,1024]{1,0:T(8,128)S(1)}, f32[64,1024]{1,0:T(8,128)S(1)}, u32[]{:S(2)}, u32[]{:S(2)}) collective-permute-start(f32[64,1024]{1,0:T(8,128)S(1)} %convert_reduce_fusion), channel_id=1, source_target_pairs={{0,1},{1,0},{2,3},{3,2},{4,5},{5,4},{6,7},{7,6},{8,9},{9,8},{10,11... | collective-permute-start | bytes 786440 | tf_op jit(solution)/shard_map/ppermute | solution.py:78
  109.8 30.2 %all-to-all-start.2 = ((bf16[8,64,1024]{2,1,0:T(8,128)(2,1)}), bf16[8,64,1024]{2,1,0:T(8,128)(2,1)S(1)}, u32[]{:S(2)}, u32[]{:S(2)}) async-start(bf16[8,64,1024]{2,1,0:T(8,128)(2,1)} %broadcast_in_dim.58), calls=%async_computation.2 | async-start | bytes 2097152 | tf_op jit(solution)/shard_map/all_to_all | solution.py:82
  113.7 4.6 %collective-permute-start.5 = (bf16[896,512]{1,0:T(8,128)(2,1)S(1)}, bf16[896,512]{1,0:T(8,128)(2,1)S(1)}, u32[]{:S(2)}, u32[]{:S(2)}) collective-permute-start(bf16[896,512]{1,0:T(8,128)(2,1)S(1)} %pad_maximum_fusion.2), channel_id=1, source_target_pairs={{0,1},{1,0},{2,3},{3,2},{4,5},{5,4},{6,7},{7,6},{8,9},{9,8},{10,11... | collective-permute-start | bytes 2752520 | tf_op jit(solution)/shard_map/ppermute | solution.py:49
  116.3 41.8 %collective-permute-start.7 = (bf16[512,896]{1,0:T(8,128)(2,1)}, bf16[512,896]{1,0:T(8,128)(2,1)S(1)}, u32[]{:S(2)}, u32[]{:S(2)}) collective-permute-start(bf16[512,896]{1,0:T(8,128)(2,1)} %bitcast.7), channel_id=1, source_target_pairs={{0,1},{1,0},{2,3},{3,2},{4,5},{5,4},{6,7},{7,6},{8,9},{9,8},{10,11... | collective-permute-start | bytes 2752520 | tf_op jit(solution)/shard_map/ppermute | solution.py:72
  143.7 44.5 %all-to-all-start.3 = ((bf16[64,8,896]{2,1,0:T(8,128)(2,1)}), bf16[64,8,896]{2,1,0:T(8,128)(2,1)S(1)}, u32[]{:S(2)}, u32[]{:S(2)}) async-start(bf16[64,8,896]{2,1,0:T(8,128)(2,1)} %fusion.1), calls=%async_computation.3 | async-start | bytes 1835008 | tf_op jit(solution)/shard_map/all_to_all | solution.py:88
  158.9 13.5 %collective-permute-start.8 = (bf16[448,512]{1,0:T(8,128)(2,1)S(1)}, bf16[448,512]{1,0:T(8,128)(2,1)S(1)}, u32[]{:S(2)}, u32[]{:S(2)}) collective-permute-start(bf16[448,512]{1,0:T(8,128)(2,1)S(1)} %slice.139), channel_id=1, source_target_pairs={{0,128},{64,192},{128,0},{192,64},{256,384},{320,448},{384,256},{4... | collective-permute-start | bytes 1376264 | tf_op jit(solution)/shard_map/ppermute | solution.py:103
  161.5 15.2 %copy-start.2 = (s32[2,64,1]{1,2,0:T(1,128)S(1)}, s32[2,64,1]{1,2,0:T(1,128)}, u32[]{:S(2)}) copy-start(s32[2,64,1]{1,2,0:T(1,128)} %param.8) | copy-start | bytes 1540
  161.5 20.7 %collective-permute-start.10 = (bf16[448,512]{1,0:T(8,128)(2,1)S(1)}, bf16[448,512]{1,0:T(8,128)(2,1)S(1)}, u32[]{:S(2)}, u32[]{:S(2)}) collective-permute-start(bf16[448,512]{1,0:T(8,128)(2,1)S(1)} %slice.138), channel_id=1, source_target_pairs={{0,128},{64,192},{128,0},{192,64},{256,384},{320,448},{384,256},{4... | collective-permute-start | bytes 1376264 | tf_op jit(solution)/shard_map/ppermute | solution.py:103
  172.5 9.7 %collective-permute-start.9 = (bf16[448,512]{1,0:T(8,128)(2,1)S(1)}, bf16[448,512]{1,0:T(8,128)(2,1)S(1)}, u32[]{:S(2)}, u32[]{:S(2)}) collective-permute-start(bf16[448,512]{1,0:T(8,128)(2,1)S(1)} %fusion.4), channel_id=1, source_target_pairs={{0,1},{1,0},{2,3},{3,2},{4,5},{5,4},{6,7},{7,6},{8,9},{9,8},{10,11... | collective-permute-start | bytes 1376264 | tf_op jit(solution)/shard_map/ppermute | solution.py:107
  188.7 6.4 %collective-permute-start.6 = (bf16[2,64,448]{2,1,0:T(8,128)(2,1)S(1)}, bf16[2,64,448]{2,1,0:T(8,128)(2,1)S(1)}, u32[]{:S(2)}, u32[]{:S(2)}) collective-permute-start(bf16[2,64,448]{2,1,0:T(8,128)(2,1)S(1)} %slice.96), channel_id=1, source_target_pairs={{0,128},{64,192},{128,0},{192,64},{256,384},{320,448},{384,256},{4... | collective-permute-start | bytes 344072 | tf_op jit(solution)/shard_map/ppermute | solution.py:95

commit v5 on v4

--- a/solution.py
+++ b/solution.py
@@ -41,14 +41,12 @@
     came_rows = lax.ppermute(given, "dp", swap_side)
 
     w_down_t = w_down.T
-    in_own = jnp.where(first_core, w_up, w_down_t)
-    out_own = jnp.where(first_core, w_down_t, w_up)
-    in_own = jnp.concatenate([in_own, lax.ppermute(in_own, "dp", swap_side)], axis=0)
-    out_own = jnp.concatenate([out_own, lax.ppermute(out_own, "dp", swap_side)], axis=0)
-    in_other = lax.ppermute(out_own, "expert", swap_core)
-    out_other = lax.ppermute(in_own, "expert", swap_core)
-    in_both = lax.optimization_barrier(jnp.concatenate([in_own, in_other], axis=1))
-    out_both = lax.optimization_barrier(jnp.concatenate([out_own, out_other], axis=1))
+    weights = jnp.concatenate(
+        [jnp.where(first_core, w_up, w_down_t), jnp.where(first_core, w_down_t, w_up)], axis=1
+    )
+    weights = jnp.concatenate([weights, lax.ppermute(weights, "dp", swap_side)], axis=0)
+    weights = lax.optimization_barrier(weights)
+    first, second = weights[:, :hidden_cols], weights[:, hidden_cols:]
 
     routing = pick(expert_ids)[:, 0]
     gate = pick(gate_weights)
@@ -71,20 +69,38 @@
     rows = rows.reshape(columns * capacity, wide)
     other_rows = lax.ppermute(rows, "expert", swap_core)
 
-    parts = jnp.dot(rows, in_both, preferred_element_type=f32).astype(bf16)
-    parts = parts.reshape(lines, -1, 2 * hidden_cols)
+    parts = jnp.concatenate(
+        [
+            jnp.dot(one, weight, preferred_element_type=f32)
+            .astype(bf16)
+            .reshape(lines, -1, hidden_cols)
+            for one, weight in ((rows, first), (other_rows, second))
+        ],
+        axis=1,
+    )
     got = lax.all_to_all(parts, "dp", 0, 0, axis_index_groups=peers, tiled=True)
     total = jnp.sum(got.astype(f32), axis=0)
-    pre = lax.ppermute(total, "expert", swap_core)
-    pre = jnp.concatenate([pre[:, hidden_cols:], pre[:, :hidden_cols]], axis=1)
-    share = jnp.where(first_core, jax.nn.silu(total), total * silu_grad(pre)).astype(bf16)
+    left, right = total[: total.shape[0] // 2], total[total.shape[0] // 2 :]
+    on_first = (lax.axis_index("expert") & 1) < 1
+    pre, back = jnp.where(on_first, left, right), jnp.where(on_first, right, left)
+    hidden, preact_grad = jax.nn.silu(pre), back * silu_grad(pre)
+    share = jnp.concatenate(
+        [
+            jnp.where(on_first, hidden, preact_grad).astype(bf16),
+            jnp.where(on_first, preact_grad, hidden).astype(bf16),
+        ],
+        axis=1,
+    )
     share = jnp.broadcast_to(share[None], (lines,) + share.shape)
     full = lax.all_to_all(share, "dp", 0, 0, axis_index_groups=peers, tiled=True)
     full = full.reshape(-1, 2 * hidden_cols)
-    chip_sum = lax.dot_general(
-        full, out_both, contract_last, preferred_element_type=f32
-    ).astype(bf16)
+    kept, given = full[:, :hidden_cols], full[:, hidden_cols:]
 
+    first, second = lax.optimization_barrier((first, second))
+    part = lax.dot_general(given, first, contract_last, preferred_element_type=f32)
+    came_part = lax.ppermute(part.astype(bf16), "expert", swap_core)
+    part = lax.dot_general(kept, second, contract_last, preferred_element_type=f32)
+    chip_sum = (part + came_part.astype(f32)).astype(bf16)
     home = lax.all_to_all(
         chip_sum.reshape(columns, capacity, wide), "expert", 0, 0, tiled=True
     )
@@ -96,21 +112,20 @@
     own_done = done[:, :, :features]
     is_mine = (jnp.arange(micro_count) == 1)[:, None, None] == on_second
 
-    def grad_of(columns_of):
+    def grad_of(rows_of, columns_of):
         whole = lax.dot_general(
-            other_rows, columns_of, contract_first, preferred_element_type=f32
+            rows_of, columns_of, contract_first, preferred_element_type=f32
         )
         came = lax.ppermute(whole[features:].astype(bf16), "dp", swap_side)
         return (whole[:features] + came.astype(f32)).astype(bf16)
 
-    grad_given = grad_of(full[:, hidden_cols:])
-    grad_came = lax.ppermute(grad_given, "expert", swap_core)
-    grad_own = grad_of(full[:, :hidden_cols])
+    grad_first = grad_of(rows, given)
+    grad_second = grad_of(other_rows, kept)
     return (
         jnp.where(is_mine, own_done[0][None], came_done[0][None]),
         jnp.where(is_mine, own_done[1][None], came_done[1][None]),
-        jnp.where(first_core, grad_came, grad_own),
-        jnp.where(first_core, grad_own, grad_came).T,
+        jnp.where(first_core, grad_first, grad_second),
+        jnp.where(first_core, grad_second, grad_first).T,
     )
 
 

time: 197 us -> 192 us (0.975)
  waiting for transfers between devices: 65 us -> 100 us
  blocking collectives: 33.6 us -> 0 us
  starting transfers between devices: 76 us -> 67.5 us
  local copies, waits for them, and re-layouts: 1.5 us -> 3.83 us
    all_to_all x1 -> x0, blocking collectives: 33.6 us -> none  [on_device(): got = lax.all_to_all(parts, 'dp', 0, 0, axis_index_groups=peers, tiled=True)]
    all_to_all x0 -> x1, waiting for transfers between devices: none -> 27.1 us  [on_device(): got = lax.all_to_all(parts, 'dp', 0, 0, axis_index_groups=peers, tiled=True)]
    all_to_all x1, waiting for transfers between devices: 0.01 us -> 25.5 us  [on_device(): rows = lax.all_to_all(packed, 'expert', 0, 0, tiled=True)]
    ppermute x6 -> x2, waiting for transfers between devices: 22.6 us -> 2.08 us  [the longest x1 2.08 us: on_device(): came_part = lax.ppermute(part.astype(bf16), 'expert', swap_core)]
    ppermute x6 -> x2, starting transfers between devices: 19.2 us -> 6.99 us  [the longest x1 3.87 us: on_device(): came_part = lax.ppermute(part.astype(bf16), 'expert', swap_core)]
    all_to_all x1, starting transfers between devices: 14.4 us -> 6 us  [on_device(): lax.all_to_all(chip_sum.reshape(columns, capacity, wide), 'expert', 0, 0,...]
    all_to_all x0 -> x1, starting transfers between devices: none -> 6.46 us  [on_device(): got = lax.all_to_all(parts, 'dp', 0, 0, axis_index_groups=peers, tiled=True)]
    all_to_all x1, waiting for transfers between devices: 20.1 us -> 25 us  [on_device(): lax.all_to_all(share, 'dp', 0, 0, axis_index_groups=peers, tiled=True)]
  transfers between devices with their start and end apart: 14 -> 11, of which waited for: 9 -> 7; matrix products, arithmetic and copies ran while one was open for 6% -> 6% of each run, Pallas kernels for 0% -> 0%
where the time goes in v5:
time: 192 us; the launch traced here: 191 us
  waiting for transfers between devices  100 us (52%)
  starting transfers between devices  67.5 us (35%)
  matrix products  10.6 us (6%)
  other arithmetic  8.2 us (4%)
  local copies, waits for them, and re-layouts  3.83 us (2%)
    all_to_all x1, waiting for transfers between devices, on_device(): got = lax.all_to_all(parts, 'dp', 0, 0, axis_index_groups=peers, tiled=True)  27.1 us
    all_to_all x1, waiting for transfers between devices, on_device(): rows = lax.all_to_all(packed, 'expert', 0, 0, tiled=True)  25.5 us
    all_to_all x1, starting transfers between devices, on_device(): rows = lax.all_to_all(packed, 'expert', 0, 0, tiled=True)  25.3 us
    all_to_all x1, waiting for transfers between devices, on_device(): lax.all_to_all(share, 'dp', 0, 0, axis_index_groups=peers, tiled=True)  25 us
    ppermute x2, waiting for transfers between devices, grad_of(): came = lax.ppermute(whole[features:].astype(bf16), 'dp', swap_side)  17.3 us
    all_to_all x1, starting transfers between devices, on_device(): got = lax.all_to_all(parts, 'dp', 0, 0, axis_index_groups=peers, tiled=True)  6.46 us
    all_to_all x1, starting transfers between devices, on_device(): lax.all_to_all(chip_sum.reshape(columns, capacity, wide), 'expert', 0, 0,...  6 us
    ppermute x1, starting transfers between devices, on_device(): came_done = lax.ppermute(done[:, :, features:], 'dp', swap_side)  5.97 us
  transfers between devices with their start and end apart: 11, of which 7 were waited for; matrix products, arithmetic and copies ran while one was open for 6% of the time, Pallas kernels for 0%

profile of v5, /device:TPU:1, one launch (start us, length us, event | category | flops | bytes accessed | tf_op | source)
XLA Modules:
  0.0 191.4 jit_solution(8015060018680560088)
XLA Ops:
  0.6 1.0 broadcast_select_fusion.5
  1.6 0.0 copy-start.3
  1.6 0.0 copy-start.4
  1.7 4.1 %collective-permute-start = (bf16[2,64,448]{2,1,0:T(8,128)(2,1)S(1)}, bf16[2,64,448]{2,1,0:T(8,128)(2,1)S(1)}, u32[]{:S(2)}, u32[]{:S(2)}) collective-permute-start(bf16[2,64,448]{2,1,0:T(8,128)(2,1)S(1)} %pad_maximum_fusion.4), channel_id=1, source_target_pairs={{0,128},{64,192},{128,0},{192,64},{256,384},{320,448},{384,256},{4... | collective-permute-start | bytes 344072 | tf_op jit(solution)/shard_map/ppermute | solution.py:41
  5.8 0.7 broadcast_select_fusion.8
  6.5 0.1 mul.84
  6.6 0.7 fusion.57
  7.2 0.2 convert_reduce_fusion.1
  7.4 0.7 broadcast_add_fusion
  8.1 0.1 pad_add_fusion.1
  8.2 0.0 collective-permute-done
  8.2 1.4 fusion
  9.6 25.3 %all-to-all-start = ((bf16[64,8,896]{2,1,0:T(8,128)(2,1)}), bf16[64,8,896]{2,1,0:T(8,128)(2,1)}, u32[]{:S(2)}, u32[]{:S(2)}) async-start(bf16[64,8,896]{2,1,0:T(8,128)(2,1)} %fusion), calls=%async_computation | async-start | bytes 1835008 | tf_op jit(solution)/shard_map/all_to_all | solution.py:68
  35.0 0.0 copy-done.3
  35.0 0.0 copy-done.4
  35.0 0.1 bitcast_select_fusion.1
  35.1 0.1 pad_maximum_fusion.2
  35.2 3.1 %collective-permute-start.1 = (bf16[448,1024]{1,0:T(8,128)(2,1)S(1)}, bf16[448,1024]{1,0:T(8,128)(2,1)}, u32[]{:S(2)}, u32[]{:S(2)}) collective-permute-start(bf16[448,1024]{1,0:T(8,128)(2,1)S(1)} %pad_maximum_fusion.2), channel_id=1, source_target_pairs={{0,128},{64,192},{128,0},{192,64},{256,384},{320,448},{384,256},{4... | collective-permute-start | bytes 2752520 | tf_op jit(solution)/shard_map/ppermute | solution.py:47
  38.3 25.5 %all-to-all-done = bf16[64,8,896]{2,1,0:T(8,128)(2,1)} async-done(((bf16[64,8,896]{2,1,0:T(8,128)(2,1)}), bf16[64,8,896]{2,1,0:T(8,128)(2,1)}, u32[]{:S(2)}, u32[]{:S(2)}) %all-to-all-start) | async-done | bytes 917536 | tf_op jit(solution)/shard_map/all_to_all | solution.py:68
  63.8 2.9 %collective-permute-start.2 = (bf16[512,896]{1,0:T(8,128)(2,1)}, bf16[512,896]{1,0:T(8,128)(2,1)S(1)}, u32[]{:S(2)}, u32[]{:S(2)}) collective-permute-start(bf16[512,896]{1,0:T(8,128)(2,1)} %bitcast.7), channel_id=1, source_target_pairs={{0,1},{1,0},{2,3},{3,2},{4,5},{5,4},{6,7},{7,6},{8,9},{9,8},{10,11... | collective-permute-start | bytes 2752520 | tf_op jit(solution)/shard_map/ppermute | solution.py:70
  66.7 0.0 collective-permute-done.1
  66.7 1.3 pad_maximum_fusion
  68.0 1.9 convolution_convert_fusion.3
  69.9 0.0 collective-permute-done.2
  69.9 0.0 copy-start.1
  69.9 0.9 copy-done.1
  70.9 0.7 convolution_convert_fusion.2
  71.6 1.1 pad_maximum_fusion.1
  72.7 6.5 %all-to-all-start.1 = ((bf16[8,128,512]{2,1,0:T(8,128)(2,1)}), bf16[8,128,512]{2,1,0:T(8,128)(2,1)S(1)}, u32[]{:S(2)}, u32[]{:S(2)}) async-start(bf16[8,128,512]{2,1,0:T(8,128)(2,1)} %pad_maximum_fusion.1), calls=%async_computation.1 | async-start | bytes 2097152 | tf_op jit(solution)/shard_map/all_to_all | solution.py:81
  79.1 27.1 %all-to-all-done.1 = bf16[8,128,512]{2,1,0:T(8,128)(2,1)S(1)} async-done(((bf16[8,128,512]{2,1,0:T(8,128)(2,1)}), bf16[8,128,512]{2,1,0:T(8,128)(2,1)S(1)}, u32[]{:S(2)}, u32[]{:S(2)}) %all-to-all-start.1) | async-done | bytes 1048608 | tf_op jit(solution)/shard_map/all_to_all | solution.py:81
  106.3 0.1 convert_reduce_fusion
  106.4 0.1 select_convert_fusion.1
  106.5 1.1 broadcast_in_dim.58
  107.7 4.5 %all-to-all-start.2 = ((bf16[8,64,1024]{2,1,0:T(8,128)(2,1)}), bf16[8,64,1024]{2,1,0:T(8,128)(2,1)S(1)}, u32[]{:S(2)}, u32[]{:S(2)}) async-start(bf16[8,64,1024]{2,1,0:T(8,128)(2,1)} %broadcast_in_dim.58), calls=%async_computation.2 | async-start | bytes 2097152 | tf_op jit(solution)/shard_map/all_to_all | solution.py:95
  112.1 1.4 fusion.51
  113.5 0.0 copy-start
  113.5 25.0 %all-to-all-done.2 = bf16[8,64,1024]{2,1,0:T(8,128)(2,1)S(1)} async-done(((bf16[8,64,1024]{2,1,0:T(8,128)(2,1)}), bf16[8,64,1024]{2,1,0:T(8,128)(2,1)S(1)}, u32[]{:S(2)}, u32[]{:S(2)}) %all-to-all-start.2) | async-done | bytes 1048608 | tf_op jit(solution)/shard_map/all_to_all | solution.py:95
  138.6 1.9 %convolution_convert_fusion.1 = bf16[512,896]{1,0:T(8,128)(2,1)S(1)} fusion(bf16[896,512]{1,0:T(8,128)(2,1)} %get-tuple-element.7, bf16[512,1024]{1,0:T(8,128)(2,1)S(1)} %bitcast.47), kind=kOutput, calls=%fused_computation.4 | convolution fusion | flops 470220800 | bytes 2359296 | tf_op jit(solution)/shard_map/dot_general | solution.py:100
  140.5 3.9 %collective-permute-start.3 = (bf16[512,896]{1,0:T(8,128)(2,1)S(1)}, bf16[512,896]{1,0:T(8,128)(2,1)S(1)}, u32[]{:S(2)}, u32[]{:S(2)}) collective-permute-start(bf16[512,896]{1,0:T(8,128)(2,1)S(1)} %convolution_convert_fusion.1), channel_id=1, source_target_pairs={{0,1},{1,0},{2,3},{3,2},{4,5},{5,4},{6,7},{7,6},{8,9},{9,8},{10,11... | collective-permute-start | bytes 2752520 | tf_op jit(solution)/shard_map/ppermute | solution.py:101
  144.4 2.1 %collective-permute-done.3 = bf16[512,896]{1,0:T(8,128)(2,1)S(1)} collective-permute-done((bf16[512,896]{1,0:T(8,128)(2,1)S(1)}, bf16[512,896]{1,0:T(8,128)(2,1)S(1)}, u32[]{:S(2)}, u32[]{:S(2)}) %collective-permute-start.3) | collective-permute-done | bytes 917536 | tf_op jit(solution)/shard_map/ppermute | solution.py:101
  146.5 0.0 copy-done
  146.5 1.7 fusion.2
  148.2 6.0 %all-to-all-start.3 = ((bf16[64,8,896]{2,1,0:T(8,128)(2,1)}), bf16[64,8,896]{2,1,0:T(8,128)(2,1)S(1)}, u32[]{:S(2)}, u32[]{:S(2)}) async-start(bf16[64,8,896]{2,1,0:T(8,128)(2,1)} %fusion.2), calls=%async_computation.3 | async-start | bytes 1835008 | tf_op jit(solution)/shard_map/all_to_all | solution.py:104
  154.2 0.0 copy-start.2
  154.2 1.9 %fusion.6 = f32[896,512]{1,0:T(8,128)S(1)} fusion(bf16[512,1024]{1,0:T(8,128)(2,1)S(1)} %bitcast.49, bf16[64,8,896]{2,1,0:T(8,128)(2,1)} %all-to-all-done), kind=kOutput, calls=%fused_computation.20 | convolution fusion | flops 469762048 | bytes 3276800 | tf_op jit(solution)/shard_map/dot_general | solution.py:116
  156.1 0.1 slice.183
  156.2 0.0 copy-start.5
  156.2 2.0 %collective-permute-start.5 = (bf16[448,512]{1,0:T(8,128)(2,1)S(1)}, bf16[448,512]{1,0:T(8,128)(2,1)S(1)}, u32[]{:S(2)}, u32[]{:S(2)}) collective-permute-start(bf16[448,512]{1,0:T(8,128)(2,1)S(1)} %slice.183), channel_id=1, source_target_pairs={{0,128},{64,192},{128,0},{192,64},{256,384},{320,448},{384,256},{4... | collective-permute-start | bytes 1376264 | tf_op jit(solution)/shard_map/ppermute | solution.py:119
  158.2 0.0 copy-done.2
  158.2 0.7 fusion.9
  158.9 0.1 slice.182
  159.0 3.2 %collective-permute-start.6 = (bf16[448,512]{1,0:T(8,128)(2,1)S(1)}, bf16[448,512]{1,0:T(8,128)(2,1)S(1)}, u32[]{:S(2)}, u32[]{:S(2)}) collective-permute-start(bf16[448,512]{1,0:T(8,128)(2,1)S(1)} %slice.182), channel_id=1, source_target_pairs={{0,128},{64,192},{128,0},{192,64},{256,384},{320,448},{384,256},{4... | collective-permute-start | bytes 1376264 | tf_op jit(solution)/shard_map/ppermute | solution.py:119
  162.2 0.0 copy-done.5
  162.3 7.4 %collective-permute-done.5 = bf16[448,512]{1,0:T(8,128)(2,1)S(1)} collective-permute-done((bf16[448,512]{1,0:T(8,128)(2,1)S(1)}, bf16[448,512]{1,0:T(8,128)(2,1)S(1)}, u32[]{:S(2)}, u32[]{:S(2)}) %collective-permute-start.5) | collective-permute-done | bytes 458784 | tf_op jit(solution)/shard_map/ppermute | solution.py:119
  169.7 9.8 %collective-permute-done.6 = bf16[448,512]{1,0:T(8,128)(2,1)S(1)} collective-permute-done((bf16[448,512]{1,0:T(8,128)(2,1)S(1)}, bf16[448,512]{1,0:T(8,128)(2,1)S(1)}, u32[]{:S(2)}, u32[]{:S(2)}) %collective-permute-start.6) | collective-permute-done | bytes 458784 | tf_op jit(solution)/shard_map/ppermute | solution.py:119
  179.5 1.2 select_bitcast_fusion
  180.8 0.0 all-to-all-done.3
  180.8 0.4 fusion.1
  181.1 0.1 slice.108
  181.3 6.0 %collective-permute-start.4 = (bf16[2,64,448]{2,1,0:T(8,128)(2,1)S(1)}, bf16[2,64,448]{2,1,0:T(8,128)(2,1)S(1)}, u32[]{:S(2)}, u32[]{:S(2)}) collective-permute-start(bf16[2,64,448]{2,1,0:T(8,128)(2,1)S(1)} %slice.108), channel_id=1, source_target_pairs={{0,128},{64,192},{128,0},{192,64},{256,384},{320,448},{384,256},{4... | collective-permute-start | bytes 344072 | tf_op jit(solution)/shard_map/ppermute | solution.py:111
  187.2 3.4 %collective-permute-done.4 = bf16[2,64,448]{2,1,0:T(8,128)(2,1)S(1)} collective-permute-done((bf16[2,64,448]{2,1,0:T(8,128)(2,1)S(1)}, bf16[2,64,448]{2,1,0:T(8,128)(2,1)S(1)}, u32[]{:S(2)}, u32[]{:S(2)}) %collective-permute-start.4) | collective-permute-done | bytes 114720 | tf_op jit(solution)/shard_map/ppermute | solution.py:111
  190.7 0.8 broadcast_select_fusion.1
  (11 shorter events, 0.1 us)
Async XLA Ops:
  1.6 33.4 %copy-start.3 = (bf16[448,512]{1,0:T(8,128)(2,1)S(1)}, bf16[448,512]{1,0:T(8,128)(2,1)}, u32[]{:S(2)}) copy-start(bf16[448,512]{1,0:T(8,128)(2,1)} %param.10) | copy-start | bytes 1376260
  1.6 33.4 %copy-start.4 = (bf16[512,448]{0,1:T(8,128)(2,1)S(1)}, bf16[512,448]{0,1:T(8,128)(2,1)}, u32[]{:S(2)}) copy-start(bf16[512,448]{0,1:T(8,128)(2,1)} %param.11) | copy-start | bytes 1376260
  1.7 6.5 %collective-permute-start = (bf16[2,64,448]{2,1,0:T(8,128)(2,1)S(1)}, bf16[2,64,448]{2,1,0:T(8,128)(2,1)S(1)}, u32[]{:S(2)}, u32[]{:S(2)}) collective-permute-start(bf16[2,64,448]{2,1,0:T(8,128)(2,1)S(1)} %pad_maximum_fusion.4), channel_id=1, source_target_pairs={{0,128},{64,192},{128,0},{192,64},{256,384},{320,448},{384,256},{4... | collective-permute-start | bytes 344072 | tf_op jit(solution)/shard_map/ppermute | solution.py:41
  9.6 54.2 %all-to-all-start = ((bf16[64,8,896]{2,1,0:T(8,128)(2,1)}), bf16[64,8,896]{2,1,0:T(8,128)(2,1)}, u32[]{:S(2)}, u32[]{:S(2)}) async-start(bf16[64,8,896]{2,1,0:T(8,128)(2,1)} %fusion), calls=%async_computation | async-start | bytes 1835008 | tf_op jit(solution)/shard_map/all_to_all | solution.py:68
  35.2 31.5 %collective-permute-start.1 = (bf16[448,1024]{1,0:T(8,128)(2,1)S(1)}, bf16[448,1024]{1,0:T(8,128)(2,1)}, u32[]{:S(2)}, u32[]{:S(2)}) collective-permute-start(bf16[448,1024]{1,0:T(8,128)(2,1)S(1)} %pad_maximum_fusion.2), channel_id=1, source_target_pairs={{0,128},{64,192},{128,0},{192,64},{256,384},{320,448},{384,256},{4... | collective-permute-start | bytes 2752520 | tf_op jit(solution)/shard_map/ppermute | solution.py:47
  63.8 6.1 %collective-permute-start.2 = (bf16[512,896]{1,0:T(8,128)(2,1)}, bf16[512,896]{1,0:T(8,128)(2,1)S(1)}, u32[]{:S(2)}, u32[]{:S(2)}) collective-permute-start(bf16[512,896]{1,0:T(8,128)(2,1)} %bitcast.7), channel_id=1, source_target_pairs={{0,1},{1,0},{2,3},{3,2},{4,5},{5,4},{6,7},{7,6},{8,9},{9,8},{10,11... | collective-permute-start | bytes 2752520 | tf_op jit(solution)/shard_map/ppermute | solution.py:70
  69.9 0.9 copy-start.1
  72.7 33.6 %all-to-all-start.1 = ((bf16[8,128,512]{2,1,0:T(8,128)(2,1)}), bf16[8,128,512]{2,1,0:T(8,128)(2,1)S(1)}, u32[]{:S(2)}, u32[]{:S(2)}) async-start(bf16[8,128,512]{2,1,0:T(8,128)(2,1)} %pad_maximum_fusion.1), calls=%async_computation.1 | async-start | bytes 2097152 | tf_op jit(solution)/shard_map/all_to_all | solution.py:81
  107.7 30.9 %all-to-all-start.2 = ((bf16[8,64,1024]{2,1,0:T(8,128)(2,1)}), bf16[8,64,1024]{2,1,0:T(8,128)(2,1)S(1)}, u32[]{:S(2)}, u32[]{:S(2)}) async-start(bf16[8,64,1024]{2,1,0:T(8,128)(2,1)} %broadcast_in_dim.58), calls=%async_computation.2 | async-start | bytes 2097152 | tf_op jit(solution)/shard_map/all_to_all | solution.py:95
  113.5 32.9 %copy-start = (bf16[896,512]{1,0:T(8,128)(2,1)S(1)}, bf16[896,512]{1,0:T(8,128)(2,1)}, u32[]{:S(2)}) copy-start(bf16[896,512]{1,0:T(8,128)(2,1)} %get-tuple-element.6) | copy-start | bytes 2752516
  140.5 6.0 %collective-permute-start.3 = (bf16[512,896]{1,0:T(8,128)(2,1)S(1)}, bf16[512,896]{1,0:T(8,128)(2,1)S(1)}, u32[]{:S(2)}, u32[]{:S(2)}) collective-permute-start(bf16[512,896]{1,0:T(8,128)(2,1)S(1)} %convolution_convert_fusion.1), channel_id=1, source_target_pairs={{0,1},{1,0},{2,3},{3,2},{4,5},{5,4},{6,7},{7,6},{8,9},{9,8},{10,11... | collective-permute-start | bytes 2752520 | tf_op jit(solution)/shard_map/ppermute | solution.py:101
  148.2 32.6 %all-to-all-start.3 = ((bf16[64,8,896]{2,1,0:T(8,128)(2,1)}), bf16[64,8,896]{2,1,0:T(8,128)(2,1)S(1)}, u32[]{:S(2)}, u32[]{:S(2)}) async-start(bf16[64,8,896]{2,1,0:T(8,128)(2,1)} %fusion.2), calls=%async_computation.3 | async-start | bytes 1835008 | tf_op jit(solution)/shard_map/all_to_all | solution.py:104
  154.2 4.1 %copy-start.2 = (bf16[512,896]{1,0:T(8,128)(2,1)S(1)}, bf16[512,896]{1,0:T(8,128)(2,1)}, u32[]{:S(2)}) copy-start(bf16[512,896]{1,0:T(8,128)(2,1)} %copy-done.1) | copy-start | bytes 2752516
  156.2 6.1 %copy-start.5 = (s32[2,64,1]{1,2,0:T(1,128)S(1)}, s32[2,64,1]{1,2,0:T(1,128)}, u32[]{:S(2)}) copy-start(s32[2,64,1]{1,2,0:T(1,128)} %param.8) | copy-start | bytes 1540
  156.2 13.5 %collective-permute-start.5 = (bf16[448,512]{1,0:T(8,128)(2,1)S(1)}, bf16[448,512]{1,0:T(8,128)(2,1)S(1)}, u32[]{:S(2)}, u32[]{:S(2)}) collective-permute-start(bf16[448,512]{1,0:T(8,128)(2,1)S(1)} %slice.183), channel_id=1, source_target_pairs={{0,128},{64,192},{128,0},{192,64},{256,384},{320,448},{384,256},{4... | collective-permute-start | bytes 1376264 | tf_op jit(solution)/shard_map/ppermute | solution.py:119
  159.0 20.5 %collective-permute-start.6 = (bf16[448,512]{1,0:T(8,128)(2,1)S(1)}, bf16[448,512]{1,0:T(8,128)(2,1)S(1)}, u32[]{:S(2)}, u32[]{:S(2)}) collective-permute-start(bf16[448,512]{1,0:T(8,128)(2,1)S(1)} %slice.182), channel_id=1, source_target_pairs={{0,128},{64,192},{128,0},{192,64},{256,384},{320,448},{384,256},{4... | collective-permute-start | bytes 1376264 | tf_op jit(solution)/shard_map/ppermute | solution.py:119
  181.3 9.4 %collective-permute-start.4 = (bf16[2,64,448]{2,1,0:T(8,128)(2,1)S(1)}, bf16[2,64,448]{2,1,0:T(8,128)(2,1)S(1)}, u32[]{:S(2)}, u32[]{:S(2)}) collective-permute-start(bf16[2,64,448]{2,1,0:T(8,128)(2,1)S(1)} %slice.108), channel_id=1, source_target_pairs={{0,128},{64,192},{128,0},{192,64},{256,384},{320,448},{384,256},{4... | collective-permute-start | bytes 344072 | tf_op jit(solution)/shard_map/ppermute | solution.py:111

commit v6 on v5

--- a/solution.py
+++ b/solution.py
@@ -45,8 +45,6 @@
         [jnp.where(first_core, w_up, w_down_t), jnp.where(first_core, w_down_t, w_up)], axis=1
     )
     weights = jnp.concatenate([weights, lax.ppermute(weights, "dp", swap_side)], axis=0)
-    weights = lax.optimization_barrier(weights)
-    first, second = weights[:, :hidden_cols], weights[:, hidden_cols:]
 
     routing = pick(expert_ids)[:, 0]
     gate = pick(gate_weights)
@@ -67,6 +65,8 @@
     packed = packed.reshape(columns, capacity, wide)
     rows = lax.all_to_all(packed, "expert", 0, 0, tiled=True)
     rows = rows.reshape(columns * capacity, wide)
+    rows, weights = lax.optimization_barrier((rows, weights))
+    first, second = weights[:, :hidden_cols], weights[:, hidden_cols:]
     other_rows = lax.ppermute(rows, "expert", swap_core)
 
     parts = jnp.concatenate(
@@ -108,19 +108,22 @@
         table, home.reshape(-1, wide), contract_first, preferred_element_type=f32
     )
     done = (jnp.stack([gate, ones]) * summed.reshape(2, token_count, wide)).astype(bf16)
+
+    wholes = [
+        lax.dot_general(rows_of, columns_of, contract_first, preferred_element_type=f32)
+        for rows_of, columns_of in ((rows, given), (other_rows, kept))
+    ]
+    came = [
+        lax.ppermute(whole[features:].astype(bf16), "dp", swap_side) for whole in wholes
+    ]
     came_done = lax.ppermute(done[:, :, features:], "dp", swap_side)
+    came_done, came = lax.optimization_barrier((came_done, came))
     own_done = done[:, :, :features]
     is_mine = (jnp.arange(micro_count) == 1)[:, None, None] == on_second
-
-    def grad_of(rows_of, columns_of):
-        whole = lax.dot_general(
-            rows_of, columns_of, contract_first, preferred_element_type=f32
-        )
-        came = lax.ppermute(whole[features:].astype(bf16), "dp", swap_side)
-        return (whole[:features] + came.astype(f32)).astype(bf16)
-
-    grad_first = grad_of(rows, given)
-    grad_second = grad_of(other_rows, kept)
+    grad_first, grad_second = [
+        (whole[:features] + part.astype(f32)).astype(bf16)
+        for whole, part in zip(wholes, came)
+    ]
     return (
         jnp.where(is_mine, own_done[0][None], came_done[0][None]),
         jnp.where(is_mine, own_done[1][None], came_done[1][None]),

time: 192 us -> 195 us (1.016); the launches traced: 191 us -> 192 us
    all_to_all x1, waiting for transfers between devices: 25.5 us -> 5.13 us  [on_device(): rows = lax.all_to_all(packed, 'expert', 0, 0, tiled=True)]
    ppermute x1, waiting for transfers between devices: 0.01 us -> 20.2 us  [on_device(): lax.ppermute(weights, 'dp', swap_side)]
    ppermute x2, waiting for transfers between devices: 17.3 us -> 0.01 us  [on_device(): lax.ppermute(whole[features:].astype(bf16), 'dp', swap_side)]
    all_to_all x1, waiting for transfers between devices: 0.01 us -> 15.7 us  [on_device(): lax.all_to_all(chip_sum.reshape(columns, capacity, wide), 'expert', 0, 0,...]
    all_to_all x1, starting transfers between devices: 6 us -> 8.27 us  [on_device(): lax.all_to_all(chip_sum.reshape(columns, capacity, wide), 'expert', 0, 0,...]
  transfers between devices with their start and end apart: 11 -> 11, of which waited for: 7 -> 8; matrix products, arithmetic and copies ran while one was open for 6% -> 5% of each run, Pallas kernels for 0% -> 0%
where the time goes in v6:
time: 195 us; the launch traced here: 192 us
  waiting for transfers between devices  99.1 us (51%)
  starting transfers between devices  69.1 us (35%)
  matrix products  10.7 us (5%)
  other arithmetic  8.07 us (4%)
  local copies, waits for them, and re-layouts  4.41 us (2%)
    all_to_all x1, waiting for transfers between devices, on_device(): got = lax.all_to_all(parts, 'dp', 0, 0, axis_index_groups=peers, tiled=True)  27.1 us
    all_to_all x1, starting transfers between devices, on_device(): rows = lax.all_to_all(packed, 'expert', 0, 0, tiled=True)  25.2 us
    all_to_all x1, waiting for transfers between devices, on_device(): lax.all_to_all(share, 'dp', 0, 0, axis_index_groups=peers, tiled=True)  23.6 us
    ppermute x1, waiting for transfers between devices, on_device(): lax.ppermute(weights, 'dp', swap_side)  20.2 us
    all_to_all x1, waiting for transfers between devices, on_device(): lax.all_to_all(chip_sum.reshape(columns, capacity, wide), 'expert', 0, 0,...  15.7 us
    all_to_all x1, starting transfers between devices, on_device(): lax.all_to_all(chip_sum.reshape(columns, capacity, wide), 'expert', 0, 0,...  8.27 us
    all_to_all x1, starting transfers between devices, on_device(): got = lax.all_to_all(parts, 'dp', 0, 0, axis_index_groups=peers, tiled=True)  6.48 us
    ppermute x1, starting transfers between devices, on_device(): came_done = lax.ppermute(done[:, :, features:], 'dp', swap_side)  6.22 us
  transfers between devices with their start and end apart: 11, of which 8 were waited for; matrix products, arithmetic and copies ran while one was open for 5% of the time, Pallas kernels for 0%

profile of v6, /device:TPU:1, one launch (start us, length us, event | category | flops | bytes accessed | tf_op | source)
XLA Modules:
  0.0 192.4 jit_solution(11332099831848809008)
XLA Ops:
  0.6 1.0 broadcast_select_fusion.5
  1.6 0.0 copy-start.6
  1.6 0.0 copy-start.7
  1.7 4.1 %collective-permute-start = (bf16[2,64,448]{2,1,0:T(8,128)(2,1)S(1)}, bf16[2,64,448]{2,1,0:T(8,128)(2,1)S(1)}, u32[]{:S(2)}, u32[]{:S(2)}) collective-permute-start(bf16[2,64,448]{2,1,0:T(8,128)(2,1)S(1)} %pad_maximum_fusion.4), channel_id=1, source_target_pairs={{0,128},{64,192},{128,0},{192,64},{256,384},{320,448},{384,256},{4... | collective-permute-start | bytes 344072 | tf_op jit(solution)/shard_map/ppermute | solution.py:41
  5.8 0.7 broadcast_select_fusion.8
  6.5 0.1 mul.84
  6.6 0.7 fusion.57
  7.2 0.2 convert_reduce_fusion.1
  7.4 0.7 broadcast_add_fusion
  8.1 0.1 pad_add_fusion.1
  8.2 0.0 collective-permute-done
  8.2 1.4 fusion
  9.6 25.2 %all-to-all-start = ((bf16[64,8,896]{2,1,0:T(8,128)(2,1)}), bf16[64,8,896]{2,1,0:T(8,128)(2,1)S(1)}, u32[]{:S(2)}, u32[]{:S(2)}) async-start(bf16[64,8,896]{2,1,0:T(8,128)(2,1)} %fusion), calls=%async_computation | async-start | bytes 1835008 | tf_op jit(solution)/shard_map/all_to_all | solution.py:66
  34.8 0.0 copy-done.6
  34.8 0.0 copy-done.7
  34.8 0.1 bitcast_select_fusion.1
  34.9 0.1 pad_maximum_fusion.2
  35.0 3.1 %collective-permute-start.1 = (bf16[448,1024]{1,0:T(8,128)(2,1)S(1)}, bf16[448,1024]{1,0:T(8,128)(2,1)S(1)}, u32[]{:S(2)}, u32[]{:S(2)}) collective-permute-start(bf16[448,1024]{1,0:T(8,128)(2,1)S(1)} %pad_maximum_fusion.2), channel_id=1, source_target_pairs={{0,128},{64,192},{128,0},{192,64},{256,384},{320,448},{384,256},{4... | collective-permute-start | bytes 2752520 | tf_op jit(solution)/shard_map/ppermute | solution.py:47
  38.1 20.2 %collective-permute-done.1 = bf16[448,1024]{1,0:T(8,128)(2,1)S(1)} collective-permute-done((bf16[448,1024]{1,0:T(8,128)(2,1)S(1)}, bf16[448,1024]{1,0:T(8,128)(2,1)S(1)}, u32[]{:S(2)}, u32[]{:S(2)}) %collective-permute-start.1) | collective-permute-done | bytes 917536 | tf_op jit(solution)/shard_map/ppermute | solution.py:47
  58.4 0.2 pad_maximum_fusion
  58.5 5.1 %all-to-all-done = bf16[64,8,896]{2,1,0:T(8,128)(2,1)S(1)} async-done(((bf16[64,8,896]{2,1,0:T(8,128)(2,1)}), bf16[64,8,896]{2,1,0:T(8,128)(2,1)S(1)}, u32[]{:S(2)}, u32[]{:S(2)}) %all-to-all-start) | async-done | bytes 917536 | tf_op jit(solution)/shard_map/all_to_all | solution.py:66
  63.7 2.9 %collective-permute-start.2 = (bf16[512,896]{1,0:T(8,128)(2,1)S(1)}, bf16[512,896]{1,0:T(8,128)(2,1)S(1)}, u32[]{:S(2)}, u32[]{:S(2)}) collective-permute-start(bf16[512,896]{1,0:T(8,128)(2,1)S(1)} %bitcast.49), channel_id=1, source_target_pairs={{0,1},{1,0},{2,3},{3,2},{4,5},{5,4},{6,7},{7,6},{8,9},{9,8},{10,11... | collective-permute-start | bytes 2752520 | tf_op jit(solution)/shard_map/ppermute | solution.py:70
  66.6 0.7 convolution_convert_fusion.3
  67.3 1.4 collective-permute-done.2
  68.6 0.7 convolution_convert_fusion.2
  69.3 0.0 copy-done.2
  69.4 0.2 copy-done.4
  69.6 1.1 pad_maximum_fusion.1
  70.6 6.5 %all-to-all-start.1 = ((bf16[8,128,512]{2,1,0:T(8,128)(2,1)}), bf16[8,128,512]{2,1,0:T(8,128)(2,1)S(1)}, u32[]{:S(2)}, u32[]{:S(2)}) async-start(bf16[8,128,512]{2,1,0:T(8,128)(2,1)} %pad_maximum_fusion.1), calls=%async_computation.1 | async-start | bytes 2097152 | tf_op jit(solution)/shard_map/all_to_all | solution.py:81
  77.1 27.1 %all-to-all-done.1 = bf16[8,128,512]{2,1,0:T(8,128)(2,1)S(1)} async-done(((bf16[8,128,512]{2,1,0:T(8,128)(2,1)}), bf16[8,128,512]{2,1,0:T(8,128)(2,1)S(1)}, u32[]{:S(2)}, u32[]{:S(2)}) %all-to-all-start.1) | async-done | bytes 1048608 | tf_op jit(solution)/shard_map/all_to_all | solution.py:81
  104.3 0.1 convert_reduce_fusion
  104.4 0.1 select_convert_fusion.1
  104.5 1.1 broadcast_in_dim.58
  105.7 4.5 %all-to-all-start.2 = ((bf16[8,64,1024]{2,1,0:T(8,128)(2,1)}), bf16[8,64,1024]{2,1,0:T(8,128)(2,1)S(1)}, u32[]{:S(2)}, u32[]{:S(2)}) async-start(bf16[8,64,1024]{2,1,0:T(8,128)(2,1)} %broadcast_in_dim.58), calls=%async_computation.2 | async-start | bytes 2097152 | tf_op jit(solution)/shard_map/all_to_all | solution.py:95
  110.2 1.4 fusion.49
  111.6 23.6 %all-to-all-done.2 = bf16[8,64,1024]{2,1,0:T(8,128)(2,1)S(1)} async-done(((bf16[8,64,1024]{2,1,0:T(8,128)(2,1)}), bf16[8,64,1024]{2,1,0:T(8,128)(2,1)S(1)}, u32[]{:S(2)}, u32[]{:S(2)}) %all-to-all-start.2) | async-done | bytes 1048608 | tf_op jit(solution)/shard_map/all_to_all | solution.py:95
  135.2 1.9 convolution_convert_fusion.1
  137.2 0.0 copy-start.8
  137.2 3.1 %collective-permute-start.3 = (bf16[512,896]{1,0:T(8,128)(2,1)S(1)}, bf16[512,896]{1,0:T(8,128)(2,1)S(1)}, u32[]{:S(2)}, u32[]{:S(2)}) collective-permute-start(bf16[512,896]{1,0:T(8,128)(2,1)S(1)} %convolution_convert_fusion.1), channel_id=1, source_target_pairs={{0,1},{1,0},{2,3},{3,2},{4,5},{5,4},{6,7},{7,6},{8,9},{9,8},{10,11... | collective-permute-start | bytes 2752520 | tf_op jit(solution)/shard_map/ppermute | solution.py:101
  140.3 2.1 %collective-permute-done.3 = bf16[512,896]{1,0:T(8,128)(2,1)S(1)} collective-permute-done((bf16[512,896]{1,0:T(8,128)(2,1)S(1)}, bf16[512,896]{1,0:T(8,128)(2,1)S(1)}, u32[]{:S(2)}, u32[]{:S(2)}) %collective-permute-start.3) | collective-permute-done | bytes 917536 | tf_op jit(solution)/shard_map/ppermute | solution.py:101
  142.4 0.0 copy-done.3
  142.4 1.7 fusion.2
  144.0 8.3 %all-to-all-start.3 = ((bf16[64,8,896]{2,1,0:T(8,128)(2,1)}), bf16[64,8,896]{2,1,0:T(8,128)(2,1)}, u32[]{:S(2)}, u32[]{:S(2)}) async-start(bf16[64,8,896]{2,1,0:T(8,128)(2,1)} %fusion.2), calls=%async_computation.3 | async-start | bytes 1835008 | tf_op jit(solution)/shard_map/all_to_all | solution.py:104
  152.3 0.0 copy-done.8
  152.4 0.0 copy-start.5
  152.4 1.9 %fusion.6 = f32[896,512]{1,0:T(8,128)S(1)} fusion(bf16[512,896]{1,0:T(8,128)(2,1)} %bitcast.51, bf16[512,1024]{1,0:T(8,128)(2,1)S(1)} %bitcast.47), kind=kOutput, calls=%fused_computation.20 | convolution fusion | flops 469762048 | bytes 3276800 | tf_op jit(solution)/shard_map/dot_general | solution.py:113
  154.3 0.1 slice.179
  154.4 2.0 %collective-permute-start.5 = (bf16[448,512]{1,0:T(8,128)(2,1)S(1)}, bf16[448,512]{1,0:T(8,128)(2,1)}, u32[]{:S(2)}, u32[]{:S(2)}) collective-permute-start(bf16[448,512]{1,0:T(8,128)(2,1)S(1)} %slice.179), channel_id=1, source_target_pairs={{0,128},{64,192},{128,0},{192,64},{256,384},{320,448},{384,256},{4... | collective-permute-start | bytes 1376264 | tf_op jit(solution)/shard_map/ppermute | solution.py:117
  156.4 0.0 copy-done.5
  156.4 0.7 fusion.9
  157.1 0.0 copy-start
  157.1 1.3 copy-done
  158.3 0.1 slice.178
  158.4 3.3 %collective-permute-start.6 = (bf16[448,512]{1,0:T(8,128)(2,1)S(1)}, bf16[448,512]{1,0:T(8,128)(2,1)S(1)}, u32[]{:S(2)}, u32[]{:S(2)}) collective-permute-start(bf16[448,512]{1,0:T(8,128)(2,1)S(1)} %slice.178), channel_id=1, source_target_pairs={{0,128},{64,192},{128,0},{192,64},{256,384},{320,448},{384,256},{4... | collective-permute-start | bytes 1376264 | tf_op jit(solution)/shard_map/ppermute | solution.py:117
  161.7 15.7 %all-to-all-done.3 = bf16[64,8,896]{2,1,0:T(8,128)(2,1)} async-done(((bf16[64,8,896]{2,1,0:T(8,128)(2,1)}), bf16[64,8,896]{2,1,0:T(8,128)(2,1)}, u32[]{:S(2)}, u32[]{:S(2)}) %all-to-all-start.3) | async-done | bytes 917536 | tf_op jit(solution)/shard_map/all_to_all | solution.py:104
  177.4 1.7 fusion.1
  179.1 0.1 slice.106
  179.2 6.2 %collective-permute-start.4 = (bf16[2,64,448]{2,1,0:T(8,128)(2,1)S(1)}, bf16[2,64,448]{2,1,0:T(8,128)(2,1)S(1)}, u32[]{:S(2)}, u32[]{:S(2)}) collective-permute-start(bf16[2,64,448]{2,1,0:T(8,128)(2,1)S(1)} %slice.106), channel_id=1, source_target_pairs={{0,128},{64,192},{128,0},{192,64},{256,384},{320,448},{384,256},{4... | collective-permute-start | bytes 344072 | tf_op jit(solution)/shard_map/ppermute | solution.py:119
  185.4 0.0 collective-permute-done.5
  185.4 0.0 collective-permute-done.6
  185.4 3.8 %collective-permute-done.4 = bf16[2,64,448]{2,1,0:T(8,128)(2,1)S(1)} collective-permute-done((bf16[2,64,448]{2,1,0:T(8,128)(2,1)S(1)}, bf16[2,64,448]{2,1,0:T(8,128)(2,1)S(1)}, u32[]{:S(2)}, u32[]{:S(2)}) %collective-permute-start.4) | collective-permute-done | bytes 114720 | tf_op jit(solution)/shard_map/ppermute | solution.py:119
  189.3 0.0 copy-done.1
  189.3 2.3 %select_bitcast_fusion = (bf16[512,448]{0,1:T(8,128)(2,1)}, bf16[448,512]{1,0:T(8,128)(2,1)}) fusion(pred[]{:T(512)S(6)} %eq.78, bf16[448,512]{1,0:T(8,128)(2,1)} %collective-permute-done.5, f32[896,512]{1,0:T(8,128)S(1)} %fusion.6, bf16[448,512]{1,0:T(8,128)(2,1)S(1)} %collective-permute-done.6, f32[896,512]{1,0:T(8,128)S(1)} %copy-done.1), kind=kLoop, calls=%fused_computation.29 | loop fusion | flops 1835008 | bytes 3670017 | tf_op jit(solution)/shard_map/transpose | solution.py:131
  191.6 0.8 broadcast_select_fusion.1
  (15 shorter events, 0.1 us)
Async XLA Ops:
  1.6 33.2 %copy-start.6 = (bf16[448,512]{1,0:T(8,128)(2,1)S(1)}, bf16[448,512]{1,0:T(8,128)(2,1)}, u32[]{:S(2)}) copy-start(bf16[448,512]{1,0:T(8,128)(2,1)} %param.10) | copy-start | bytes 1376260
  1.6 33.2 %copy-start.7 = (bf16[512,448]{0,1:T(8,128)(2,1)S(1)}, bf16[512,448]{0,1:T(8,128)(2,1)}, u32[]{:S(2)}) copy-start(bf16[512,448]{0,1:T(8,128)(2,1)} %param.11) | copy-start | bytes 1376260
  1.7 6.5 %collective-permute-start = (bf16[2,64,448]{2,1,0:T(8,128)(2,1)S(1)}, bf16[2,64,448]{2,1,0:T(8,128)(2,1)S(1)}, u32[]{:S(2)}, u32[]{:S(2)}) collective-permute-start(bf16[2,64,448]{2,1,0:T(8,128)(2,1)S(1)} %pad_maximum_fusion.4), channel_id=1, source_target_pairs={{0,128},{64,192},{128,0},{192,64},{256,384},{320,448},{384,256},{4... | collective-permute-start | bytes 344072 | tf_op jit(solution)/shard_map/ppermute | solution.py:41
  9.6 54.1 %all-to-all-start = ((bf16[64,8,896]{2,1,0:T(8,128)(2,1)}), bf16[64,8,896]{2,1,0:T(8,128)(2,1)S(1)}, u32[]{:S(2)}, u32[]{:S(2)}) async-start(bf16[64,8,896]{2,1,0:T(8,128)(2,1)} %fusion), calls=%async_computation | async-start | bytes 1835008 | tf_op jit(solution)/shard_map/all_to_all | solution.py:66
  35.0 23.4 %collective-permute-start.1 = (bf16[448,1024]{1,0:T(8,128)(2,1)S(1)}, bf16[448,1024]{1,0:T(8,128)(2,1)S(1)}, u32[]{:S(2)}, u32[]{:S(2)}) collective-permute-start(bf16[448,1024]{1,0:T(8,128)(2,1)S(1)} %pad_maximum_fusion.2), channel_id=1, source_target_pairs={{0,128},{64,192},{128,0},{192,64},{256,384},{320,448},{384,256},{4... | collective-permute-start | bytes 2752520 | tf_op jit(solution)/shard_map/ppermute | solution.py:47
  63.7 5.7 %copy-start.2 = (bf16[64,8,896]{2,1,0:T(8,128)(2,1)}, bf16[64,8,896]{2,1,0:T(8,128)(2,1)S(1)}, u32[]{:S(2)}) copy-start(bf16[64,8,896]{2,1,0:T(8,128)(2,1)S(1)} %all-to-all-done) | copy-start | bytes 2752516
  63.7 4.9 %collective-permute-start.2 = (bf16[512,896]{1,0:T(8,128)(2,1)S(1)}, bf16[512,896]{1,0:T(8,128)(2,1)S(1)}, u32[]{:S(2)}, u32[]{:S(2)}) collective-permute-start(bf16[512,896]{1,0:T(8,128)(2,1)S(1)} %bitcast.49), channel_id=1, source_target_pairs={{0,1},{1,0},{2,3},{3,2},{4,5},{5,4},{6,7},{7,6},{8,9},{9,8},{10,11... | collective-permute-start | bytes 2752520 | tf_op jit(solution)/shard_map/ppermute | solution.py:70
  68.6 0.9 copy-start.4
  70.6 33.6 %all-to-all-start.1 = ((bf16[8,128,512]{2,1,0:T(8,128)(2,1)}), bf16[8,128,512]{2,1,0:T(8,128)(2,1)S(1)}, u32[]{:S(2)}, u32[]{:S(2)}) async-start(bf16[8,128,512]{2,1,0:T(8,128)(2,1)} %pad_maximum_fusion.1), calls=%async_computation.1 | async-start | bytes 2097152 | tf_op jit(solution)/shard_map/all_to_all | solution.py:81
  105.7 29.6 %all-to-all-start.2 = ((bf16[8,64,1024]{2,1,0:T(8,128)(2,1)}), bf16[8,64,1024]{2,1,0:T(8,128)(2,1)S(1)}, u32[]{:S(2)}, u32[]{:S(2)}) async-start(bf16[8,64,1024]{2,1,0:T(8,128)(2,1)} %broadcast_in_dim.58), calls=%async_computation.2 | async-start | bytes 2097152 | tf_op jit(solution)/shard_map/all_to_all | solution.py:95
  111.6 30.8 %copy-start.3 = (bf16[896,512]{1,0:T(8,128)(2,1)S(1)}, bf16[896,512]{1,0:T(8,128)(2,1)}, u32[]{:S(2)}) copy-start(bf16[896,512]{1,0:T(8,128)(2,1)} %get-tuple-element.13) | copy-start | bytes 2752516
  137.2 15.2 %copy-start.8 = (s32[2,64,1]{1,2,0:T(1,128)S(1)}, s32[2,64,1]{1,2,0:T(1,128)}, u32[]{:S(2)}) copy-start(s32[2,64,1]{1,2,0:T(1,128)} %param.8) | copy-start | bytes 1540
  137.2 5.2 %collective-permute-start.3 = (bf16[512,896]{1,0:T(8,128)(2,1)S(1)}, bf16[512,896]{1,0:T(8,128)(2,1)S(1)}, u32[]{:S(2)}, u32[]{:S(2)}) collective-permute-start(bf16[512,896]{1,0:T(8,128)(2,1)S(1)} %convolution_convert_fusion.1), channel_id=1, source_target_pairs={{0,1},{1,0},{2,3},{3,2},{4,5},{5,4},{6,7},{7,6},{8,9},{9,8},{10,11... | collective-permute-start | bytes 2752520 | tf_op jit(solution)/shard_map/ppermute | solution.py:101
  144.0 33.4 %all-to-all-start.3 = ((bf16[64,8,896]{2,1,0:T(8,128)(2,1)}), bf16[64,8,896]{2,1,0:T(8,128)(2,1)}, u32[]{:S(2)}, u32[]{:S(2)}) async-start(bf16[64,8,896]{2,1,0:T(8,128)(2,1)} %fusion.2), calls=%async_computation.3 | async-start | bytes 1835008 | tf_op jit(solution)/shard_map/all_to_all | solution.py:104
  152.4 4.0 %copy-start.5 = (bf16[512,896]{1,0:T(8,128)(2,1)S(1)}, bf16[512,896]{1,0:T(8,128)(2,1)}, u32[]{:S(2)}) copy-start(bf16[512,896]{1,0:T(8,128)(2,1)} %copy-done.4) | copy-start | bytes 2752516
  154.4 31.1 %collective-permute-start.5 = (bf16[448,512]{1,0:T(8,128)(2,1)S(1)}, bf16[448,512]{1,0:T(8,128)(2,1)}, u32[]{:S(2)}, u32[]{:S(2)}) collective-permute-start(bf16[448,512]{1,0:T(8,128)(2,1)S(1)} %slice.179), channel_id=1, source_target_pairs={{0,128},{64,192},{128,0},{192,64},{256,384},{320,448},{384,256},{4... | collective-permute-start | bytes 1376264 | tf_op jit(solution)/shard_map/ppermute | solution.py:117
  157.1 1.3 copy-start
  158.4 27.1 %collective-permute-start.6 = (bf16[448,512]{1,0:T(8,128)(2,1)S(1)}, bf16[448,512]{1,0:T(8,128)(2,1)S(1)}, u32[]{:S(2)}, u32[]{:S(2)}) collective-permute-start(bf16[448,512]{1,0:T(8,128)(2,1)S(1)} %slice.178), channel_id=1, source_target_pairs={{0,128},{64,192},{128,0},{192,64},{256,384},{320,448},{384,256},{4... | collective-permute-start | bytes 1376264 | tf_op jit(solution)/shard_map/ppermute | solution.py:117
  177.4 11.9 %copy-start.1 = (f32[896,512]{1,0:T(8,128)S(1)}, f32[896,512]{1,0:T(8,128)}, u32[]{:S(2)}) copy-start(f32[896,512]{1,0:T(8,128)} %copy-done) | copy-start | bytes 5505028
  179.2 10.1 %collective-permute-start.4 = (bf16[2,64,448]{2,1,0:T(8,128)(2,1)S(1)}, bf16[2,64,448]{2,1,0:T(8,128)(2,1)S(1)}, u32[]{:S(2)}, u32[]{:S(2)}) collective-permute-start(bf16[2,64,448]{2,1,0:T(8,128)(2,1)S(1)} %slice.106), channel_id=1, source_target_pairs={{0,128},{64,192},{128,0},{192,64},{256,384},{320,448},{384,256},{4... | collective-permute-start | bytes 344072 | tf_op jit(solution)/shard_map/ppermute | solution.py:119

commit v7 on v6

--- a/solution.py
+++ b/solution.py
@@ -110,18 +110,18 @@
     done = (jnp.stack([gate, ones]) * summed.reshape(2, token_count, wide)).astype(bf16)
 
     wholes = [
-        lax.dot_general(rows_of, columns_of, contract_first, preferred_element_type=f32)
+        lax.dot_general(
+            rows_of, columns_of, contract_first, preferred_element_type=f32
+        ).astype(bf16)
         for rows_of, columns_of in ((rows, given), (other_rows, kept))
     ]
-    came = [
-        lax.ppermute(whole[features:].astype(bf16), "dp", swap_side) for whole in wholes
-    ]
+    came = [lax.ppermute(whole[features:], "dp", swap_side) for whole in wholes]
     came_done = lax.ppermute(done[:, :, features:], "dp", swap_side)
-    came_done, came = lax.optimization_barrier((came_done, came))
+    done, came = lax.optimization_barrier((done, came))
     own_done = done[:, :, :features]
     is_mine = (jnp.arange(micro_count) == 1)[:, None, None] == on_second
     grad_first, grad_second = [
-        (whole[:features] + part.astype(f32)).astype(bf16)
+        (whole[:features].astype(f32) + part.astype(f32)).astype(bf16)
         for whole, part in zip(wholes, came)
     ]
     return (

time: 195 us -> 191 us (0.979)
  matrix products: 10.7 us -> 8.14 us
    all_to_all x1, waiting for transfers between devices: 15.7 us -> 18.3 us  [on_device(): lax.all_to_all(chip_sum.reshape(columns, capacity, wide), 'expert', 0, 0,...]
    ppermute x1, waiting for transfers between devices: 3.83 us -> 1.48 us  [on_device(): came_done = lax.ppermute(done[:, :, features:], 'dp', swap_side)]
where the time goes in v7:
time: 191 us; the launch traced here: 189 us
  waiting for transfers between devices  99.4 us (52%)
  starting transfers between devices  69.1 us (36%)
  matrix products  8.14 us (4%)
  other arithmetic  8.13 us (4%)
  local copies, waits for them, and re-layouts  3.11 us (2%)
    all_to_all x1, waiting for transfers between devices, on_device(): got = lax.all_to_all(parts, 'dp', 0, 0, axis_index_groups=peers, tiled=True)  27.1 us
    all_to_all x1, starting transfers between devices, on_device(): rows = lax.all_to_all(packed, 'expert', 0, 0, tiled=True)  25.2 us
    all_to_all x1, waiting for transfers between devices, on_device(): lax.all_to_all(share, 'dp', 0, 0, axis_index_groups=peers, tiled=True)  23.6 us
    ppermute x1, waiting for transfers between devices, on_device(): lax.ppermute(weights, 'dp', swap_side)  20.2 us
    all_to_all x1, waiting for transfers between devices, on_device(): lax.all_to_all(chip_sum.reshape(columns, capacity, wide), 'expert', 0, 0,...  18.3 us
    all_to_all x1, starting transfers between devices, on_device(): lax.all_to_all(chip_sum.reshape(columns, capacity, wide), 'expert', 0, 0,...  8.1 us
    all_to_all x1, starting transfers between devices, on_device(): got = lax.all_to_all(parts, 'dp', 0, 0, axis_index_groups=peers, tiled=True)  6.48 us
    ppermute x1, starting transfers between devices, on_device(): came_done = lax.ppermute(done[:, :, features:], 'dp', swap_side)  6.21 us
  transfers between devices with their start and end apart: 11, of which 8 were waited for; matrix products, arithmetic and copies ran while one was open for 5% of the time, Pallas kernels for 0%

profile of v7, /device:TPU:1, one launch (start us, length us, event | category | flops | bytes accessed | tf_op | source)
XLA Modules:
  0.0 188.8 jit_solution(12051170994151044139)
XLA Ops:
  0.6 1.0 broadcast_select_fusion.5
  1.6 0.0 copy-start.4
  1.6 0.0 copy-start.5
  1.7 4.1 %collective-permute-start = (bf16[2,64,448]{2,1,0:T(8,128)(2,1)S(1)}, bf16[2,64,448]{2,1,0:T(8,128)(2,1)S(1)}, u32[]{:S(2)}, u32[]{:S(2)}) collective-permute-start(bf16[2,64,448]{2,1,0:T(8,128)(2,1)S(1)} %pad_maximum_fusion.4), channel_id=1, source_target_pairs={{0,128},{64,192},{128,0},{192,64},{256,384},{320,448},{384,256},{4... | collective-permute-start | bytes 344072 | tf_op jit(solution)/shard_map/ppermute | solution.py:41
  5.8 0.7 broadcast_select_fusion.8
  6.5 0.1 mul.84
  6.6 0.7 fusion.53
  7.2 0.2 convert_reduce_fusion.1
  7.4 0.7 broadcast_add_fusion
  8.1 0.1 pad_add_fusion.1
  8.2 0.0 collective-permute-done
  8.2 1.4 fusion
  9.6 25.2 %all-to-all-start = ((bf16[64,8,896]{2,1,0:T(8,128)(2,1)}), bf16[64,8,896]{2,1,0:T(8,128)(2,1)S(1)}, u32[]{:S(2)}, u32[]{:S(2)}) async-start(bf16[64,8,896]{2,1,0:T(8,128)(2,1)} %fusion), calls=%async_computation | async-start | bytes 1835008 | tf_op jit(solution)/shard_map/all_to_all | solution.py:66
  34.8 0.0 copy-done.4
  34.8 0.0 copy-done.5
  34.8 0.1 bitcast_select_fusion.1
  34.9 0.1 pad_maximum_fusion.2
  35.0 3.1 %collective-permute-start.1 = (bf16[448,1024]{1,0:T(8,128)(2,1)S(1)}, bf16[448,1024]{1,0:T(8,128)(2,1)S(1)}, u32[]{:S(2)}, u32[]{:S(2)}) collective-permute-start(bf16[448,1024]{1,0:T(8,128)(2,1)S(1)} %pad_maximum_fusion.2), channel_id=1, source_target_pairs={{0,128},{64,192},{128,0},{192,64},{256,384},{320,448},{384,256},{4... | collective-permute-start | bytes 2752520 | tf_op jit(solution)/shard_map/ppermute | solution.py:47
  38.1 20.2 %collective-permute-done.1 = bf16[448,1024]{1,0:T(8,128)(2,1)S(1)} collective-permute-done((bf16[448,1024]{1,0:T(8,128)(2,1)S(1)}, bf16[448,1024]{1,0:T(8,128)(2,1)S(1)}, u32[]{:S(2)}, u32[]{:S(2)}) %collective-permute-start.1) | collective-permute-done | bytes 917536 | tf_op jit(solution)/shard_map/ppermute | solution.py:47
  58.4 0.2 pad_maximum_fusion
  58.5 5.1 %all-to-all-done = bf16[64,8,896]{2,1,0:T(8,128)(2,1)S(1)} async-done(((bf16[64,8,896]{2,1,0:T(8,128)(2,1)}), bf16[64,8,896]{2,1,0:T(8,128)(2,1)S(1)}, u32[]{:S(2)}, u32[]{:S(2)}) %all-to-all-start) | async-done | bytes 917536 | tf_op jit(solution)/shard_map/all_to_all | solution.py:66
  63.7 0.0 copy-start.1
  63.7 2.9 %collective-permute-start.2 = (bf16[512,896]{1,0:T(8,128)(2,1)S(1)}, bf16[512,896]{1,0:T(8,128)(2,1)S(1)}, u32[]{:S(2)}, u32[]{:S(2)}) collective-permute-start(bf16[512,896]{1,0:T(8,128)(2,1)S(1)} %bitcast.49), channel_id=1, source_target_pairs={{0,1},{1,0},{2,3},{3,2},{4,5},{5,4},{6,7},{7,6},{8,9},{9,8},{10,11... | collective-permute-start | bytes 2752520 | tf_op jit(solution)/shard_map/ppermute | solution.py:70
  66.6 0.7 convolution_convert_fusion.5
  67.3 1.4 collective-permute-done.2
  68.6 0.7 convolution_convert_fusion.4
  69.3 0.0 copy-done.1
  69.4 0.2 copy-done.7
  69.6 1.1 pad_maximum_fusion.1
  70.6 6.5 %all-to-all-start.1 = ((bf16[8,128,512]{2,1,0:T(8,128)(2,1)}), bf16[8,128,512]{2,1,0:T(8,128)(2,1)S(1)}, u32[]{:S(2)}, u32[]{:S(2)}) async-start(bf16[8,128,512]{2,1,0:T(8,128)(2,1)} %pad_maximum_fusion.1), calls=%async_computation.1 | async-start | bytes 2097152 | tf_op jit(solution)/shard_map/all_to_all | solution.py:81
  77.1 27.1 %all-to-all-done.1 = bf16[8,128,512]{2,1,0:T(8,128)(2,1)S(1)} async-done(((bf16[8,128,512]{2,1,0:T(8,128)(2,1)}), bf16[8,128,512]{2,1,0:T(8,128)(2,1)S(1)}, u32[]{:S(2)}, u32[]{:S(2)}) %all-to-all-start.1) | async-done | bytes 1048608 | tf_op jit(solution)/shard_map/all_to_all | solution.py:81
  104.3 0.1 convert_reduce_fusion
  104.4 0.1 select_convert_fusion.1
  104.5 1.1 broadcast_in_dim.58
  105.7 4.5 %all-to-all-start.2 = ((bf16[8,64,1024]{2,1,0:T(8,128)(2,1)}), bf16[8,64,1024]{2,1,0:T(8,128)(2,1)S(1)}, u32[]{:S(2)}, u32[]{:S(2)}) async-start(bf16[8,64,1024]{2,1,0:T(8,128)(2,1)} %broadcast_in_dim.58), calls=%async_computation.2 | async-start | bytes 2097152 | tf_op jit(solution)/shard_map/all_to_all | solution.py:95
  110.2 1.4 fusion.45
  111.6 23.6 %all-to-all-done.2 = bf16[8,64,1024]{2,1,0:T(8,128)(2,1)S(1)} async-done(((bf16[8,64,1024]{2,1,0:T(8,128)(2,1)}), bf16[8,64,1024]{2,1,0:T(8,128)(2,1)S(1)}, u32[]{:S(2)}, u32[]{:S(2)}) %all-to-all-start.2) | async-done | bytes 1048608 | tf_op jit(solution)/shard_map/all_to_all | solution.py:95
  135.2 1.9 %convolution_convert_fusion.3 = bf16[512,896]{1,0:T(8,128)(2,1)S(1)} fusion(bf16[896,512]{1,0:T(8,128)(2,1)} %get-tuple-element.14, bf16[512,1024]{1,0:T(8,128)(2,1)S(1)} %bitcast.45), kind=kOutput, calls=%fused_computation.6 | convolution fusion | flops 470220800 | bytes 2359296 | tf_op jit(solution)/shard_map/dot_general | solution.py:100
  137.2 0.0 copy-start.6
  137.2 0.0 copy-start.2
  137.2 3.2 %collective-permute-start.3 = (bf16[512,896]{1,0:T(8,128)(2,1)S(1)}, bf16[512,896]{1,0:T(8,128)(2,1)S(1)}, u32[]{:S(2)}, u32[]{:S(2)}) collective-permute-start(bf16[512,896]{1,0:T(8,128)(2,1)S(1)} %convolution_convert_fusion.3), channel_id=1, source_target_pairs={{0,1},{1,0},{2,3},{3,2},{4,5},{5,4},{6,7},{7,6},{8,9},{9,8},{10,11... | collective-permute-start | bytes 2752520 | tf_op jit(solution)/shard_map/ppermute | solution.py:101
  140.4 2.1 %collective-permute-done.3 = bf16[512,896]{1,0:T(8,128)(2,1)S(1)} collective-permute-done((bf16[512,896]{1,0:T(8,128)(2,1)S(1)}, bf16[512,896]{1,0:T(8,128)(2,1)S(1)}, u32[]{:S(2)}, u32[]{:S(2)}) %collective-permute-start.3) | collective-permute-done | bytes 917536 | tf_op jit(solution)/shard_map/ppermute | solution.py:101
  142.5 0.0 copy-done
  142.5 1.7 fusion.2
  144.2 8.1 %all-to-all-start.3 = ((bf16[64,8,896]{2,1,0:T(8,128)(2,1)}), bf16[64,8,896]{2,1,0:T(8,128)(2,1)S(1)}, u32[]{:S(2)}, u32[]{:S(2)}) async-start(bf16[64,8,896]{2,1,0:T(8,128)(2,1)} %fusion.2), calls=%async_computation.3 | async-start | bytes 1835008 | tf_op jit(solution)/shard_map/all_to_all | solution.py:104
  152.3 0.0 copy-done.6
  152.3 0.0 copy-done.2
  152.4 0.0 copy-start.8
  152.4 0.7 convolution_convert_fusion.2
  153.0 0.0 copy-start.3
  153.1 2.0 %collective-permute-start.4 = (bf16[448,512]{1,0:T(8,128)(2,1)S(1)}, bf16[448,512]{1,0:T(8,128)(2,1)}, u32[]{:S(2)}, u32[]{:S(2)}) collective-permute-start(bf16[448,512]{1,0:T(8,128)(2,1)S(1)} %slice.103), channel_id=1, source_target_pairs={{0,128},{64,192},{128,0},{192,64},{256,384},{320,448},{384,256},{4... | collective-permute-start | bytes 1376264 | tf_op jit(solution)/shard_map/ppermute | solution.py:118
  155.1 0.0 copy-done.8
  155.1 0.7 convolution_convert_fusion.1
  155.8 0.0 copy-done.3
  155.8 3.3 %collective-permute-start.5 = (bf16[448,512]{1,0:T(8,128)(2,1)S(1)}, bf16[448,512]{1,0:T(8,128)(2,1)S(1)}, u32[]{:S(2)}, u32[]{:S(2)}) collective-permute-start(bf16[448,512]{1,0:T(8,128)(2,1)S(1)} %slice.104), channel_id=1, source_target_pairs={{0,128},{64,192},{128,0},{192,64},{256,384},{320,448},{384,256},{4... | collective-permute-start | bytes 1376264 | tf_op jit(solution)/shard_map/ppermute | solution.py:118
  159.2 18.3 %all-to-all-done.3 = bf16[64,8,896]{2,1,0:T(8,128)(2,1)S(1)} async-done(((bf16[64,8,896]{2,1,0:T(8,128)(2,1)}), bf16[64,8,896]{2,1,0:T(8,128)(2,1)S(1)}, u32[]{:S(2)}, u32[]{:S(2)}) %all-to-all-start.3) | async-done | bytes 917536 | tf_op jit(solution)/shard_map/all_to_all | solution.py:104
  177.5 0.4 fusion.1
  177.8 0.1 slice.105
  177.9 6.2 %collective-permute-start.6 = (bf16[2,64,448]{2,1,0:T(8,128)(2,1)S(1)}, bf16[2,64,448]{2,1,0:T(8,128)(2,1)S(1)}, u32[]{:S(2)}, u32[]{:S(2)}) collective-permute-start(bf16[2,64,448]{2,1,0:T(8,128)(2,1)S(1)} %slice.105), channel_id=1, source_target_pairs={{0,128},{64,192},{128,0},{192,64},{256,384},{320,448},{384,256},{4... | collective-permute-start | bytes 344072 | tf_op jit(solution)/shard_map/ppermute | solution.py:119
  184.2 0.0 collective-permute-done.4
  184.2 0.0 collective-permute-done.5
  184.2 2.4 %select_bitcast_fusion = (bf16[512,448]{0,1:T(8,128)(2,1)}, bf16[448,512]{1,0:T(8,128)(2,1)}) fusion(pred[]{:T(512)S(6)} %eq.78, bf16[448,512]{1,0:T(8,128)(2,1)} %collective-permute-done.4, bf16[896,512]{1,0:T(8,128)(2,1)} %copy-done.3, bf16[448,512]{1,0:T(8,128)(2,1)S(1)} %collective-permute-done.5, bf16[896,512]{1,0:T(8,128)(2,1)S(1)} %convolution_convert_fusion.1), kind=kLoop, calls=%fused_computation.25 | loop fusion | flops 2293760 | bytes 2752513 | tf_op jit(solution)/shard_map/transpose | solution.py:131
  186.5 1.5 collective-permute-done.6
  188.0 0.8 broadcast_select_fusion.1
  (15 shorter events, 0.2 us)
Async XLA Ops:
  1.6 33.2 %copy-start.4 = (bf16[448,512]{1,0:T(8,128)(2,1)S(1)}, bf16[448,512]{1,0:T(8,128)(2,1)}, u32[]{:S(2)}) copy-start(bf16[448,512]{1,0:T(8,128)(2,1)} %param.10) | copy-start | bytes 1376260
  1.6 33.2 %copy-start.5 = (bf16[512,448]{0,1:T(8,128)(2,1)S(1)}, bf16[512,448]{0,1:T(8,128)(2,1)}, u32[]{:S(2)}) copy-start(bf16[512,448]{0,1:T(8,128)(2,1)} %param.11) | copy-start | bytes 1376260
  1.7 6.5 %collective-permute-start = (bf16[2,64,448]{2,1,0:T(8,128)(2,1)S(1)}, bf16[2,64,448]{2,1,0:T(8,128)(2,1)S(1)}, u32[]{:S(2)}, u32[]{:S(2)}) collective-permute-start(bf16[2,64,448]{2,1,0:T(8,128)(2,1)S(1)} %pad_maximum_fusion.4), channel_id=1, source_target_pairs={{0,128},{64,192},{128,0},{192,64},{256,384},{320,448},{384,256},{4... | collective-permute-start | bytes 344072 | tf_op jit(solution)/shard_map/ppermute | solution.py:41
  9.6 54.1 %all-to-all-start = ((bf16[64,8,896]{2,1,0:T(8,128)(2,1)}), bf16[64,8,896]{2,1,0:T(8,128)(2,1)S(1)}, u32[]{:S(2)}, u32[]{:S(2)}) async-start(bf16[64,8,896]{2,1,0:T(8,128)(2,1)} %fusion), calls=%async_computation | async-start | bytes 1835008 | tf_op jit(solution)/shard_map/all_to_all | solution.py:66
  35.0 23.4 %collective-permute-start.1 = (bf16[448,1024]{1,0:T(8,128)(2,1)S(1)}, bf16[448,1024]{1,0:T(8,128)(2,1)S(1)}, u32[]{:S(2)}, u32[]{:S(2)}) collective-permute-start(bf16[448,1024]{1,0:T(8,128)(2,1)S(1)} %pad_maximum_fusion.2), channel_id=1, source_target_pairs={{0,128},{64,192},{128,0},{192,64},{256,384},{320,448},{384,256},{4... | collective-permute-start | bytes 2752520 | tf_op jit(solution)/shard_map/ppermute | solution.py:47
  63.7 5.7 %copy-start.1 = (bf16[64,8,896]{2,1,0:T(8,128)(2,1)}, bf16[64,8,896]{2,1,0:T(8,128)(2,1)S(1)}, u32[]{:S(2)}) copy-start(bf16[64,8,896]{2,1,0:T(8,128)(2,1)S(1)} %all-to-all-done) | copy-start | bytes 2752516
  63.7 4.9 %collective-permute-start.2 = (bf16[512,896]{1,0:T(8,128)(2,1)S(1)}, bf16[512,896]{1,0:T(8,128)(2,1)S(1)}, u32[]{:S(2)}, u32[]{:S(2)}) collective-permute-start(bf16[512,896]{1,0:T(8,128)(2,1)S(1)} %bitcast.49), channel_id=1, source_target_pairs={{0,1},{1,0},{2,3},{3,2},{4,5},{5,4},{6,7},{7,6},{8,9},{9,8},{10,11... | collective-permute-start | bytes 2752520 | tf_op jit(solution)/shard_map/ppermute | solution.py:70
  68.6 0.9 copy-start.7
  70.6 33.6 %all-to-all-start.1 = ((bf16[8,128,512]{2,1,0:T(8,128)(2,1)}), bf16[8,128,512]{2,1,0:T(8,128)(2,1)S(1)}, u32[]{:S(2)}, u32[]{:S(2)}) async-start(bf16[8,128,512]{2,1,0:T(8,128)(2,1)} %pad_maximum_fusion.1), calls=%async_computation.1 | async-start | bytes 2097152 | tf_op jit(solution)/shard_map/all_to_all | solution.py:81
  105.7 29.6 %all-to-all-start.2 = ((bf16[8,64,1024]{2,1,0:T(8,128)(2,1)}), bf16[8,64,1024]{2,1,0:T(8,128)(2,1)S(1)}, u32[]{:S(2)}, u32[]{:S(2)}) async-start(bf16[8,64,1024]{2,1,0:T(8,128)(2,1)} %broadcast_in_dim.58), calls=%async_computation.2 | async-start | bytes 2097152 | tf_op jit(solution)/shard_map/all_to_all | solution.py:95
  111.6 30.9 %copy-start = (bf16[896,512]{1,0:T(8,128)(2,1)S(1)}, bf16[896,512]{1,0:T(8,128)(2,1)}, u32[]{:S(2)}) copy-start(bf16[896,512]{1,0:T(8,128)(2,1)} %get-tuple-element.13) | copy-start | bytes 2752516
  137.2 15.2 %copy-start.6 = (s32[2,64,1]{1,2,0:T(1,128)S(1)}, s32[2,64,1]{1,2,0:T(1,128)}, u32[]{:S(2)}) copy-start(s32[2,64,1]{1,2,0:T(1,128)} %param.8) | copy-start | bytes 1540
  137.2 15.2 %copy-start.2 = (bf16[64,8,896]{2,1,0:T(8,128)(2,1)S(1)}, bf16[64,8,896]{2,1,0:T(8,128)(2,1)}, u32[]{:S(2)}) copy-start(bf16[64,8,896]{2,1,0:T(8,128)(2,1)} %copy-done.1) | copy-start | bytes 2752516
  137.2 5.3 %collective-permute-start.3 = (bf16[512,896]{1,0:T(8,128)(2,1)S(1)}, bf16[512,896]{1,0:T(8,128)(2,1)S(1)}, u32[]{:S(2)}, u32[]{:S(2)}) collective-permute-start(bf16[512,896]{1,0:T(8,128)(2,1)S(1)} %convolution_convert_fusion.3), channel_id=1, source_target_pairs={{0,1},{1,0},{2,3},{3,2},{4,5},{5,4},{6,7},{7,6},{8,9},{9,8},{10,11... | collective-permute-start | bytes 2752520 | tf_op jit(solution)/shard_map/ppermute | solution.py:101
  144.2 33.2 %all-to-all-start.3 = ((bf16[64,8,896]{2,1,0:T(8,128)(2,1)}), bf16[64,8,896]{2,1,0:T(8,128)(2,1)S(1)}, u32[]{:S(2)}, u32[]{:S(2)}) async-start(bf16[64,8,896]{2,1,0:T(8,128)(2,1)} %fusion.2), calls=%async_computation.3 | async-start | bytes 1835008 | tf_op jit(solution)/shard_map/all_to_all | solution.py:104
  152.4 2.7 %copy-start.8 = (bf16[512,896]{1,0:T(8,128)(2,1)S(1)}, bf16[512,896]{1,0:T(8,128)(2,1)}, u32[]{:S(2)}) copy-start(bf16[512,896]{1,0:T(8,128)(2,1)} %copy-done.7) | copy-start | bytes 2752516
  153.0 2.7 %copy-start.3 = (bf16[896,512]{1,0:T(8,128)(2,1)}, bf16[896,512]{1,0:T(8,128)(2,1)S(1)}, u32[]{:S(2)}) copy-start(bf16[896,512]{1,0:T(8,128)(2,1)S(1)} %convolution_convert_fusion.2) | copy-start | bytes 2752516
  153.1 31.1 %collective-permute-start.4 = (bf16[448,512]{1,0:T(8,128)(2,1)S(1)}, bf16[448,512]{1,0:T(8,128)(2,1)}, u32[]{:S(2)}, u32[]{:S(2)}) collective-permute-start(bf16[448,512]{1,0:T(8,128)(2,1)S(1)} %slice.103), channel_id=1, source_target_pairs={{0,128},{64,192},{128,0},{192,64},{256,384},{320,448},{384,256},{4... | collective-permute-start | bytes 1376264 | tf_op jit(solution)/shard_map/ppermute | solution.py:118
  155.8 28.3 %collective-permute-start.5 = (bf16[448,512]{1,0:T(8,128)(2,1)S(1)}, bf16[448,512]{1,0:T(8,128)(2,1)S(1)}, u32[]{:S(2)}, u32[]{:S(2)}) collective-permute-start(bf16[448,512]{1,0:T(8,128)(2,1)S(1)} %slice.104), channel_id=1, source_target_pairs={{0,128},{64,192},{128,0},{192,64},{256,384},{320,448},{384,256},{4... | collective-permute-start | bytes 1376264 | tf_op jit(solution)/shard_map/ppermute | solution.py:118
  177.9 10.1 %collective-permute-start.6 = (bf16[2,64,448]{2,1,0:T(8,128)(2,1)S(1)}, bf16[2,64,448]{2,1,0:T(8,128)(2,1)S(1)}, u32[]{:S(2)}, u32[]{:S(2)}) collective-permute-start(bf16[2,64,448]{2,1,0:T(8,128)(2,1)S(1)} %slice.105), channel_id=1, source_target_pairs={{0,128},{64,192},{128,0},{192,64},{256,384},{320,448},{384,256},{4... | collective-permute-start | bytes 344072 | tf_op jit(solution)/shard_map/ppermute | solution.py:119

commit v8 on v7

--- a/solution.py
+++ b/solution.py
@@ -96,7 +96,6 @@
     full = full.reshape(-1, 2 * hidden_cols)
     kept, given = full[:, :hidden_cols], full[:, hidden_cols:]
 
-    first, second = lax.optimization_barrier((first, second))
     part = lax.dot_general(given, first, contract_last, preferred_element_type=f32)
     came_part = lax.ppermute(part.astype(bf16), "expert", swap_core)
     part = lax.dot_general(kept, second, contract_last, preferred_element_type=f32)

time: 191 us -> 189 us (0.990)
  blocking collectives: 0 us -> 26.8 us
  waiting for transfers between devices: 99.4 us -> 76 us
  local copies, waits for them, and re-layouts: 3.11 us -> 0.67 us
    all_to_all x0 -> x1, blocking collectives: none -> 26.8 us  [on_device(): lax.all_to_all(share, 'dp', 0, 0, axis_index_groups=peers, tiled=True)]
    all_to_all x1 -> x0, waiting for transfers between devices: 23.6 us -> none  [on_device(): lax.all_to_all(share, 'dp', 0, 0, axis_index_groups=peers, tiled=True)]
    all_to_all x1 -> x0, starting transfers between devices: 4.54 us -> none  [on_device(): lax.all_to_all(share, 'dp', 0, 0, axis_index_groups=peers, tiled=True)]
  transfers between devices with their start and end apart: 11 -> 10, of which waited for: 8 -> 7; matrix products, arithmetic and copies ran while one was open for 5% -> 4% of each run, Pallas kernels for 0% -> 0%
where the time goes in v8:
time: 189 us; the launch traced here: 188 us
  waiting for transfers between devices  76 us (40%)
  starting transfers between devices  68.5 us (36%)
  blocking collectives  26.8 us (14%)
  other arithmetic  8.11 us (4%)
  matrix products  6.95 us (4%)
    all_to_all x1, waiting for transfers between devices, on_device(): got = lax.all_to_all(parts, 'dp', 0, 0, axis_index_groups=peers, tiled=True)  27.1 us
    all_to_all x1, blocking collectives, on_device(): lax.all_to_all(share, 'dp', 0, 0, axis_index_groups=peers, tiled=True)  26.8 us
    all_to_all x1, starting transfers between devices, on_device(): rows = lax.all_to_all(packed, 'expert', 0, 0, tiled=True)  25.2 us
    ppermute x1, waiting for transfers between devices, on_device(): lax.ppermute(weights, 'dp', swap_side)  20.2 us
    all_to_all x1, waiting for transfers between devices, on_device(): lax.all_to_all(chip_sum.reshape(columns, capacity, wide), 'expert', 0, 0,...  19.1 us
    all_to_all x1, starting transfers between devices, on_device(): lax.all_to_all(chip_sum.reshape(columns, capacity, wide), 'expert', 0, 0,...  8.24 us
    ppermute x1, starting transfers between devices, on_device(): came_done = lax.ppermute(done[:, :, features:], 'dp', swap_side)  7.88 us
    ppermute x2, starting transfers between devices, on_device(): came = [lax.ppermute(whole[features:], 'dp', swap_side) for whole in wholes]  7.16 us
  transfers between devices with their start and end apart: 10, of which 7 were waited for; matrix products, arithmetic and copies ran while one was open for 4% of the time, Pallas kernels for 0%

profile of v8, /device:TPU:1, one launch (start us, length us, event | category | flops | bytes accessed | tf_op | source)
XLA Modules:
  0.0 188.0 jit_solution(11549898276709943452)
XLA Ops:
  0.6 1.0 broadcast_select_fusion.5
  1.6 0.0 copy-start.5
  1.6 0.0 copy-start.6
  1.7 4.1 %collective-permute-start = (bf16[2,64,448]{2,1,0:T(8,128)(2,1)S(1)}, bf16[2,64,448]{2,1,0:T(8,128)(2,1)S(1)}, u32[]{:S(2)}, u32[]{:S(2)}) collective-permute-start(bf16[2,64,448]{2,1,0:T(8,128)(2,1)S(1)} %pad_maximum_fusion.4), channel_id=1, source_target_pairs={{0,128},{64,192},{128,0},{192,64},{256,384},{320,448},{384,256},{4... | collective-permute-start | bytes 344072 | tf_op jit(solution)/shard_map/ppermute | solution.py:41
  5.8 0.7 broadcast_select_fusion.8
  6.5 0.1 mul.84
  6.6 0.7 fusion.52
  7.2 0.2 convert_reduce_fusion.1
  7.4 0.7 broadcast_add_fusion
  8.1 0.1 pad_add_fusion.1
  8.2 0.0 collective-permute-done
  8.2 1.4 fusion
  9.6 25.2 %all-to-all-start = ((bf16[64,8,896]{2,1,0:T(8,128)(2,1)}), bf16[64,8,896]{2,1,0:T(8,128)(2,1)S(1)}, u32[]{:S(2)}, u32[]{:S(2)}) async-start(bf16[64,8,896]{2,1,0:T(8,128)(2,1)} %fusion), calls=%async_computation | async-start | bytes 1835008 | tf_op jit(solution)/shard_map/all_to_all | solution.py:66
  34.8 0.0 copy-done.5
  34.8 0.0 copy-done.6
  34.8 0.1 bitcast_select_fusion.1
  34.9 0.1 pad_maximum_fusion.2
  35.0 3.1 %collective-permute-start.1 = (bf16[448,1024]{1,0:T(8,128)(2,1)S(1)}, bf16[448,1024]{1,0:T(8,128)(2,1)S(1)}, u32[]{:S(2)}, u32[]{:S(2)}) collective-permute-start(bf16[448,1024]{1,0:T(8,128)(2,1)S(1)} %pad_maximum_fusion.2), channel_id=1, source_target_pairs={{0,128},{64,192},{128,0},{192,64},{256,384},{320,448},{384,256},{4... | collective-permute-start | bytes 2752520 | tf_op jit(solution)/shard_map/ppermute | solution.py:47
  38.1 20.2 %collective-permute-done.1 = bf16[448,1024]{1,0:T(8,128)(2,1)S(1)} collective-permute-done((bf16[448,1024]{1,0:T(8,128)(2,1)S(1)}, bf16[448,1024]{1,0:T(8,128)(2,1)S(1)}, u32[]{:S(2)}, u32[]{:S(2)}) %collective-permute-start.1) | collective-permute-done | bytes 917536 | tf_op jit(solution)/shard_map/ppermute | solution.py:47
  58.4 0.2 pad_maximum_fusion
  58.5 5.1 %all-to-all-done = bf16[64,8,896]{2,1,0:T(8,128)(2,1)S(1)} async-done(((bf16[64,8,896]{2,1,0:T(8,128)(2,1)}), bf16[64,8,896]{2,1,0:T(8,128)(2,1)S(1)}, u32[]{:S(2)}, u32[]{:S(2)}) %all-to-all-start) | async-done | bytes 917536 | tf_op jit(solution)/shard_map/all_to_all | solution.py:66
  63.7 0.0 copy-start.2
  63.7 2.9 %collective-permute-start.2 = (bf16[512,896]{1,0:T(8,128)(2,1)S(1)}, bf16[512,896]{1,0:T(8,128)(2,1)S(1)}, u32[]{:S(2)}, u32[]{:S(2)}) collective-permute-start(bf16[512,896]{1,0:T(8,128)(2,1)S(1)} %bitcast.47), channel_id=1, source_target_pairs={{0,1},{1,0},{2,3},{3,2},{4,5},{5,4},{6,7},{7,6},{8,9},{9,8},{10,11... | collective-permute-start | bytes 2752520 | tf_op jit(solution)/shard_map/ppermute | solution.py:70
  66.5 0.7 convolution_convert_fusion.5
  67.3 1.4 collective-permute-done.2
  68.6 0.0 copy-start.8
  68.6 0.7 convolution_convert_fusion.4
  69.3 0.0 copy-done.2
  69.3 0.2 copy-done.8
  69.6 1.1 pad_maximum_fusion.1
  70.6 6.5 %all-to-all-start.1 = ((bf16[8,128,512]{2,1,0:T(8,128)(2,1)}), bf16[8,128,512]{2,1,0:T(8,128)(2,1)S(1)}, u32[]{:S(2)}, u32[]{:S(2)}) async-start(bf16[8,128,512]{2,1,0:T(8,128)(2,1)} %pad_maximum_fusion.1), calls=%async_computation.1 | async-start | bytes 2097152 | tf_op jit(solution)/shard_map/all_to_all | solution.py:81
  77.1 27.1 %all-to-all-done.1 = bf16[8,128,512]{2,1,0:T(8,128)(2,1)S(1)} async-done(((bf16[8,128,512]{2,1,0:T(8,128)(2,1)}), bf16[8,128,512]{2,1,0:T(8,128)(2,1)S(1)}, u32[]{:S(2)}, u32[]{:S(2)}) %all-to-all-start.1) | async-done | bytes 1048608 | tf_op jit(solution)/shard_map/all_to_all | solution.py:81
  104.2 0.1 convert_reduce_fusion
  104.4 0.1 select_convert_fusion.1
  104.5 0.1 broadcast_in_dim.58
  104.6 26.8 %all_to_all.20 = bf16[8,64,1024]{2,1,0:T(8,128)(2,1)S(1)} all-to-all(bf16[8,64,1024]{2,1,0:T(8,128)(2,1)S(1)} %broadcast_in_dim.58), channel_id=1, replica_groups={{0,64,256,320,512,576,768,832},{128,192,384,448,640,704,896,960},{1,65,..., dimensions={0} | all-to-all | bytes 2097152 | tf_op jit(solution)/shard_map/all_to_all | solution.py:95
  131.4 0.7 convolution_convert_fusion.3
  132.1 0.0 copy-start.7
  132.1 0.0 copy-start.3
  132.1 3.5 %collective-permute-start.3 = (bf16[512,896]{1,0:T(8,128)(2,1)S(1)}, bf16[512,896]{1,0:T(8,128)(2,1)S(1)}, u32[]{:S(2)}, u32[]{:S(2)}) collective-permute-start(bf16[512,896]{1,0:T(8,128)(2,1)S(1)} %convolution_convert_fusion.3), channel_id=1, source_target_pairs={{0,1},{1,0},{2,3},{3,2},{4,5},{5,4},{6,7},{7,6},{8,9},{9,8},{10,11... | collective-permute-start | bytes 2752520 | tf_op jit(solution)/shard_map/ppermute | solution.py:100
  135.7 2.1 %collective-permute-done.3 = bf16[512,896]{1,0:T(8,128)(2,1)S(1)} collective-permute-done((bf16[512,896]{1,0:T(8,128)(2,1)S(1)}, bf16[512,896]{1,0:T(8,128)(2,1)S(1)}, u32[]{:S(2)}, u32[]{:S(2)}) %collective-permute-start.3) | collective-permute-done | bytes 917536 | tf_op jit(solution)/shard_map/ppermute | solution.py:100
  137.7 0.0 copy-done
  137.7 1.7 fusion.2
  139.4 8.2 %all-to-all-start.3 = ((bf16[64,8,896]{2,1,0:T(8,128)(2,1)}), bf16[64,8,896]{2,1,0:T(8,128)(2,1)S(1)}, u32[]{:S(2)}, u32[]{:S(2)}) async-start(bf16[64,8,896]{2,1,0:T(8,128)(2,1)} %fusion.2), calls=%async_computation.3 | async-start | bytes 1835008 | tf_op jit(solution)/shard_map/all_to_all | solution.py:103
  147.7 0.0 copy-done.7
  147.7 0.0 copy-done.3
  147.7 0.0 copy-done.1
  147.7 0.0 copy-start.9
  147.7 0.7 convolution_convert_fusion.2
  148.4 0.0 copy-start.4
  148.5 5.2 %collective-permute-start.4 = (bf16[448,512]{1,0:T(8,128)(2,1)S(1)}, bf16[448,512]{1,0:T(8,128)(2,1)}, u32[]{:S(2)}, u32[]{:S(2)}) collective-permute-start(bf16[448,512]{1,0:T(8,128)(2,1)S(1)} %slice.103), channel_id=1, source_target_pairs={{0,128},{64,192},{128,0},{192,64},{256,384},{320,448},{384,256},{4... | collective-permute-start | bytes 1376264 | tf_op jit(solution)/shard_map/ppermute | solution.py:117
  153.7 0.0 copy-done.9
  153.7 0.7 convolution_convert_fusion.1
  154.4 0.0 copy-done.4
  154.4 1.9 %collective-permute-start.5 = (bf16[448,512]{1,0:T(8,128)(2,1)S(1)}, bf16[448,512]{1,0:T(8,128)(2,1)S(1)}, u32[]{:S(2)}, u32[]{:S(2)}) collective-permute-start(bf16[448,512]{1,0:T(8,128)(2,1)S(1)} %slice.104), channel_id=1, source_target_pairs={{0,128},{64,192},{128,0},{192,64},{256,384},{320,448},{384,256},{4... | collective-permute-start | bytes 1376264 | tf_op jit(solution)/shard_map/ppermute | solution.py:117
  156.4 19.1 %all-to-all-done.3 = bf16[64,8,896]{2,1,0:T(8,128)(2,1)S(1)} async-done(((bf16[64,8,896]{2,1,0:T(8,128)(2,1)}), bf16[64,8,896]{2,1,0:T(8,128)(2,1)S(1)}, u32[]{:S(2)}, u32[]{:S(2)}) %all-to-all-start.3) | async-done | bytes 917536 | tf_op jit(solution)/shard_map/all_to_all | solution.py:103
  175.5 0.4 fusion.1
  175.8 0.1 slice.105
  175.9 7.9 %collective-permute-start.6 = (bf16[2,64,448]{2,1,0:T(8,128)(2,1)S(1)}, bf16[2,64,448]{2,1,0:T(8,128)(2,1)S(1)}, u32[]{:S(2)}, u32[]{:S(2)}) collective-permute-start(bf16[2,64,448]{2,1,0:T(8,128)(2,1)S(1)} %slice.105), channel_id=1, source_target_pairs={{0,128},{64,192},{128,0},{192,64},{256,384},{320,448},{384,256},{4... | collective-permute-start | bytes 344072 | tf_op jit(solution)/shard_map/ppermute | solution.py:118
  183.8 0.0 collective-permute-done.4
  183.8 0.0 collective-permute-done.5
  183.8 2.4 %select_bitcast_fusion = (bf16[512,448]{0,1:T(8,128)(2,1)}, bf16[448,512]{1,0:T(8,128)(2,1)}) fusion(pred[]{:T(512)S(6)} %eq.78, bf16[448,512]{1,0:T(8,128)(2,1)} %collective-permute-done.4, bf16[896,512]{1,0:T(8,128)(2,1)} %copy-done.4, bf16[448,512]{1,0:T(8,128)(2,1)S(1)} %collective-permute-done.5, bf16[896,512]{1,0:T(8,128)(2,1)S(1)} %convolution_convert_fusion.1), kind=kLoop, calls=%fused_computation.29 | loop fusion | flops 2293760 | bytes 2752513 | tf_op jit(solution)/shard_map/transpose | solution.py:130
  186.2 1.0 collective-permute-done.6
  187.2 0.8 broadcast_select_fusion.1
  (15 shorter events, 0.2 us)
Async XLA Ops:
  1.6 33.2 %copy-start.5 = (bf16[448,512]{1,0:T(8,128)(2,1)S(1)}, bf16[448,512]{1,0:T(8,128)(2,1)}, u32[]{:S(2)}) copy-start(bf16[448,512]{1,0:T(8,128)(2,1)} %param.10) | copy-start | bytes 1376260
  1.6 33.2 %copy-start.6 = (bf16[512,448]{0,1:T(8,128)(2,1)S(1)}, bf16[512,448]{0,1:T(8,128)(2,1)}, u32[]{:S(2)}) copy-start(bf16[512,448]{0,1:T(8,128)(2,1)} %param.11) | copy-start | bytes 1376260
  1.7 6.5 %collective-permute-start = (bf16[2,64,448]{2,1,0:T(8,128)(2,1)S(1)}, bf16[2,64,448]{2,1,0:T(8,128)(2,1)S(1)}, u32[]{:S(2)}, u32[]{:S(2)}) collective-permute-start(bf16[2,64,448]{2,1,0:T(8,128)(2,1)S(1)} %pad_maximum_fusion.4), channel_id=1, source_target_pairs={{0,128},{64,192},{128,0},{192,64},{256,384},{320,448},{384,256},{4... | collective-permute-start | bytes 344072 | tf_op jit(solution)/shard_map/ppermute | solution.py:41
  9.6 54.1 %all-to-all-start = ((bf16[64,8,896]{2,1,0:T(8,128)(2,1)}), bf16[64,8,896]{2,1,0:T(8,128)(2,1)S(1)}, u32[]{:S(2)}, u32[]{:S(2)}) async-start(bf16[64,8,896]{2,1,0:T(8,128)(2,1)} %fusion), calls=%async_computation | async-start | bytes 1835008 | tf_op jit(solution)/shard_map/all_to_all | solution.py:66
  35.0 23.4 %collective-permute-start.1 = (bf16[448,1024]{1,0:T(8,128)(2,1)S(1)}, bf16[448,1024]{1,0:T(8,128)(2,1)S(1)}, u32[]{:S(2)}, u32[]{:S(2)}) collective-permute-start(bf16[448,1024]{1,0:T(8,128)(2,1)S(1)} %pad_maximum_fusion.2), channel_id=1, source_target_pairs={{0,128},{64,192},{128,0},{192,64},{256,384},{320,448},{384,256},{4... | collective-permute-start | bytes 2752520 | tf_op jit(solution)/shard_map/ppermute | solution.py:47
  63.7 5.7 %copy-start.2 = (bf16[64,8,896]{2,1,0:T(8,128)(2,1)}, bf16[64,8,896]{2,1,0:T(8,128)(2,1)S(1)}, u32[]{:S(2)}) copy-start(bf16[64,8,896]{2,1,0:T(8,128)(2,1)S(1)} %all-to-all-done) | copy-start | bytes 2752516
  63.7 4.9 %collective-permute-start.2 = (bf16[512,896]{1,0:T(8,128)(2,1)S(1)}, bf16[512,896]{1,0:T(8,128)(2,1)S(1)}, u32[]{:S(2)}, u32[]{:S(2)}) collective-permute-start(bf16[512,896]{1,0:T(8,128)(2,1)S(1)} %bitcast.47), channel_id=1, source_target_pairs={{0,1},{1,0},{2,3},{3,2},{4,5},{5,4},{6,7},{7,6},{8,9},{9,8},{10,11... | collective-permute-start | bytes 2752520 | tf_op jit(solution)/shard_map/ppermute | solution.py:70
  68.6 0.9 copy-start.8
  70.6 33.6 %all-to-all-start.1 = ((bf16[8,128,512]{2,1,0:T(8,128)(2,1)}), bf16[8,128,512]{2,1,0:T(8,128)(2,1)S(1)}, u32[]{:S(2)}, u32[]{:S(2)}) async-start(bf16[8,128,512]{2,1,0:T(8,128)(2,1)} %pad_maximum_fusion.1), calls=%async_computation.1 | async-start | bytes 2097152 | tf_op jit(solution)/shard_map/all_to_all | solution.py:81
  131.4 6.4 %copy-start = (bf16[8,64,1024]{2,1,0:T(8,128)(2,1)}, bf16[8,64,1024]{2,1,0:T(8,128)(2,1)S(1)}, u32[]{:S(2)}) copy-start(bf16[8,64,1024]{2,1,0:T(8,128)(2,1)S(1)} %all_to_all.20) | copy-start | bytes 3145732
  132.1 15.6 %copy-start.7 = (s32[2,64,1]{1,2,0:T(1,128)S(1)}, s32[2,64,1]{1,2,0:T(1,128)}, u32[]{:S(2)}) copy-start(s32[2,64,1]{1,2,0:T(1,128)} %param.8) | copy-start | bytes 1540
  132.1 15.6 %copy-start.3 = (bf16[64,8,896]{2,1,0:T(8,128)(2,1)S(1)}, bf16[64,8,896]{2,1,0:T(8,128)(2,1)}, u32[]{:S(2)}) copy-start(bf16[64,8,896]{2,1,0:T(8,128)(2,1)} %copy-done.2) | copy-start | bytes 2752516
  132.1 5.6 %collective-permute-start.3 = (bf16[512,896]{1,0:T(8,128)(2,1)S(1)}, bf16[512,896]{1,0:T(8,128)(2,1)S(1)}, u32[]{:S(2)}, u32[]{:S(2)}) collective-permute-start(bf16[512,896]{1,0:T(8,128)(2,1)S(1)} %convolution_convert_fusion.3), channel_id=1, source_target_pairs={{0,1},{1,0},{2,3},{3,2},{4,5},{5,4},{6,7},{7,6},{8,9},{9,8},{10,11... | collective-permute-start | bytes 2752520 | tf_op jit(solution)/shard_map/ppermute | solution.py:100
  139.4 8.3 %copy-start.1 = (bf16[8,64,1024]{2,1,0:T(8,128)(2,1)S(1)}, bf16[8,64,1024]{2,1,0:T(8,128)(2,1)}, u32[]{:S(2)}) copy-start(bf16[8,64,1024]{2,1,0:T(8,128)(2,1)} %copy-done) | copy-start | bytes 3145732
  139.4 36.0 %all-to-all-start.3 = ((bf16[64,8,896]{2,1,0:T(8,128)(2,1)}), bf16[64,8,896]{2,1,0:T(8,128)(2,1)S(1)}, u32[]{:S(2)}, u32[]{:S(2)}) async-start(bf16[64,8,896]{2,1,0:T(8,128)(2,1)} %fusion.2), calls=%async_computation.3 | async-start | bytes 1835008 | tf_op jit(solution)/shard_map/all_to_all | solution.py:103
  147.7 6.0 %copy-start.9 = (bf16[512,896]{1,0:T(8,128)(2,1)S(1)}, bf16[512,896]{1,0:T(8,128)(2,1)}, u32[]{:S(2)}) copy-start(bf16[512,896]{1,0:T(8,128)(2,1)} %copy-done.8) | copy-start | bytes 2752516
  148.4 6.0 %copy-start.4 = (bf16[896,512]{1,0:T(8,128)(2,1)}, bf16[896,512]{1,0:T(8,128)(2,1)S(1)}, u32[]{:S(2)}) copy-start(bf16[896,512]{1,0:T(8,128)(2,1)S(1)} %convolution_convert_fusion.2) | copy-start | bytes 2752516
  148.5 35.4 %collective-permute-start.4 = (bf16[448,512]{1,0:T(8,128)(2,1)S(1)}, bf16[448,512]{1,0:T(8,128)(2,1)}, u32[]{:S(2)}, u32[]{:S(2)}) collective-permute-start(bf16[448,512]{1,0:T(8,128)(2,1)S(1)} %slice.103), channel_id=1, source_target_pairs={{0,128},{64,192},{128,0},{192,64},{256,384},{320,448},{384,256},{4... | collective-permute-start | bytes 1376264 | tf_op jit(solution)/shard_map/ppermute | solution.py:117
  154.4 29.4 %collective-permute-start.5 = (bf16[448,512]{1,0:T(8,128)(2,1)S(1)}, bf16[448,512]{1,0:T(8,128)(2,1)S(1)}, u32[]{:S(2)}, u32[]{:S(2)}) collective-permute-start(bf16[448,512]{1,0:T(8,128)(2,1)S(1)} %slice.104), channel_id=1, source_target_pairs={{0,128},{64,192},{128,0},{192,64},{256,384},{320,448},{384,256},{4... | collective-permute-start | bytes 1376264 | tf_op jit(solution)/shard_map/ppermute | solution.py:117
  175.9 11.3 %collective-permute-start.6 = (bf16[2,64,448]{2,1,0:T(8,128)(2,1)S(1)}, bf16[2,64,448]{2,1,0:T(8,128)(2,1)S(1)}, u32[]{:S(2)}, u32[]{:S(2)}) collective-permute-start(bf16[2,64,448]{2,1,0:T(8,128)(2,1)S(1)} %slice.105), channel_id=1, source_target_pairs={{0,128},{64,192},{128,0},{192,64},{256,384},{320,448},{384,256},{4... | collective-permute-start | bytes 344072 | tf_op jit(solution)/shard_map/ppermute | solution.py:118

commit v9 on v8

--- a/solution.py
+++ b/solution.py
@@ -81,13 +81,12 @@
     got = lax.all_to_all(parts, "dp", 0, 0, axis_index_groups=peers, tiled=True)
     total = jnp.sum(got.astype(f32), axis=0)
     left, right = total[: total.shape[0] // 2], total[total.shape[0] // 2 :]
-    on_first = (lax.axis_index("expert") & 1) < 1
-    pre, back = jnp.where(on_first, left, right), jnp.where(on_first, right, left)
+    pre, back = jnp.where(first_core, left, right), jnp.where(first_core, right, left)
     hidden, preact_grad = jax.nn.silu(pre), back * silu_grad(pre)
     share = jnp.concatenate(
         [
-            jnp.where(on_first, hidden, preact_grad).astype(bf16),
-            jnp.where(on_first, preact_grad, hidden).astype(bf16),
+            jnp.where(first_core, hidden, preact_grad).astype(bf16),
+            jnp.where(first_core, preact_grad, hidden).astype(bf16),
         ],
         axis=1,
     )

time: 189 us -> 186 us (0.984)
  the two profiles are of different devices: /device:TPU:1 before, /device:TPU:16 now
where the time goes in v9:
time: 186 us
  blocking collectives  66.8 us (36%)
  waiting for transfers between devices  52.4 us (28%)
  starting transfers between devices  49.3 us (27%)
  matrix products  8.18 us (4%)
  other arithmetic  7.12 us (4%)
    all_to_all x1, blocking collectives, on_device(): got = lax.all_to_all(parts, 'dp', 0, 0, axis_index_groups=peers, tiled=True)  37.9 us
    all_to_all x1, blocking collectives, on_device(): lax.all_to_all(share, 'dp', 0, 0, axis_index_groups=peers, tiled=True)  28.9 us
    all_to_all x1, starting transfers between devices, on_device(): rows = lax.all_to_all(packed, 'expert', 0, 0, tiled=True)  22.5 us
    all_to_all x1, waiting for transfers between devices, on_device(): lax.all_to_all(chip_sum.reshape(columns, capacity, wide), 'expert', 0, 0,...  21.5 us
    ppermute x1, waiting for transfers between devices, on_device(): lax.ppermute(weights, 'dp', swap_side)  20.8 us
    all_to_all x1, starting transfers between devices, on_device(): lax.all_to_all(chip_sum.reshape(columns, capacity, wide), 'expert', 0, 0,...  8.24 us
    ppermute x2, starting transfers between devices, on_device(): came = [lax.ppermute(whole[features:], 'dp', swap_side) for whole in wholes]  5.85 us
  transfers between devices with their start and end apart: 9, of which 7 were waited for; matrix products, arithmetic and copies ran while one was open for 5% of the time, Pallas kernels for 0%

profile of v9, /device:TPU:16, one launch (start us, length us, event | category | flops | bytes accessed | tf_op | source)
XLA Modules:
  0.0 185.5 jit_solution(16382075072133636123)
XLA Ops:
  0.6 1.0 broadcast_select_fusion.5
  1.6 0.0 copy-start.2
  1.6 0.0 copy-start.3
  1.7 3.5 %collective-permute-start = (bf16[2,64,448]{2,1,0:T(8,128)(2,1)S(1)}, bf16[2,64,448]{2,1,0:T(8,128)(2,1)S(1)}, u32[]{:S(2)}, u32[]{:S(2)}) collective-permute-start(bf16[2,64,448]{2,1,0:T(8,128)(2,1)S(1)} %pad_maximum_fusion.4), channel_id=1, source_target_pairs={{0,128},{64,192},{128,0},{192,64},{256,384},{320,448},{384,256},{4... | collective-permute-start | bytes 344072 | tf_op jit(solution)/shard_map/ppermute | solution.py:41
  5.2 0.7 broadcast_select_fusion.8
  5.9 0.1 mul.84
  6.0 0.7 fusion.52
  6.7 0.2 convert_reduce_fusion.1
  6.9 0.7 broadcast_add_fusion
  7.5 0.1 pad_add_fusion.1
  7.6 1.3 collective-permute-done
  8.9 1.4 fusion
  10.3 22.5 %all-to-all-start = ((bf16[64,8,896]{2,1,0:T(8,128)(2,1)}), bf16[64,8,896]{2,1,0:T(8,128)(2,1)S(1)}, u32[]{:S(2)}, u32[]{:S(2)}) async-start(bf16[64,8,896]{2,1,0:T(8,128)(2,1)} %fusion), calls=%async_computation | async-start | bytes 1835008 | tf_op jit(solution)/shard_map/all_to_all | solution.py:66
  32.8 0.0 copy-done.2
  32.8 0.0 copy-done.3
  32.8 0.1 bitcast_select_fusion.1
  32.9 0.1 pad_maximum_fusion.2
  33.0 3.4 %collective-permute-start.1 = (bf16[448,1024]{1,0:T(8,128)(2,1)S(1)}, bf16[448,1024]{1,0:T(8,128)(2,1)S(1)}, u32[]{:S(2)}, u32[]{:S(2)}) collective-permute-start(bf16[448,1024]{1,0:T(8,128)(2,1)S(1)} %pad_maximum_fusion.2), channel_id=1, source_target_pairs={{0,128},{64,192},{128,0},{192,64},{256,384},{320,448},{384,256},{4... | collective-permute-start | bytes 2752520 | tf_op jit(solution)/shard_map/ppermute | solution.py:47
  36.5 20.8 %collective-permute-done.1 = bf16[448,1024]{1,0:T(8,128)(2,1)S(1)} collective-permute-done((bf16[448,1024]{1,0:T(8,128)(2,1)S(1)}, bf16[448,1024]{1,0:T(8,128)(2,1)S(1)}, u32[]{:S(2)}, u32[]{:S(2)}) %collective-permute-start.1) | collective-permute-done | bytes 917536 | tf_op jit(solution)/shard_map/ppermute | solution.py:47
  57.3 0.2 pad_maximum_fusion
  57.4 2.0 %all-to-all-done = bf16[64,8,896]{2,1,0:T(8,128)(2,1)S(1)} async-done(((bf16[64,8,896]{2,1,0:T(8,128)(2,1)}), bf16[64,8,896]{2,1,0:T(8,128)(2,1)S(1)}, u32[]{:S(2)}, u32[]{:S(2)}) %all-to-all-start) | async-done | bytes 917536 | tf_op jit(solution)/shard_map/all_to_all | solution.py:66
  59.5 0.0 copy-start
  59.5 1.9 %collective-permute-start.2 = (bf16[512,896]{1,0:T(8,128)(2,1)S(1)}, bf16[512,896]{1,0:T(8,128)(2,1)S(1)}, u32[]{:S(2)}, u32[]{:S(2)}) collective-permute-start(bf16[512,896]{1,0:T(8,128)(2,1)S(1)} %bitcast.47), channel_id=1, source_target_pairs={{0,1},{1,0},{2,3},{3,2},{4,5},{5,4},{6,7},{7,6},{8,9},{9,8},{10,11... | collective-permute-start | bytes 2752520 | tf_op jit(solution)/shard_map/ppermute | solution.py:70
  61.4 0.7 convolution_convert_fusion.5
  62.1 1.7 collective-permute-done.2
  63.8 0.0 copy-start.5
  63.8 0.7 convolution_convert_fusion.4
  64.5 0.0 copy-done
  64.5 0.2 copy-done.5
  64.8 0.1 pad_maximum_fusion.1
  64.8 37.9 %all_to_all.20 = bf16[8,128,512]{2,1,0:T(8,128)(2,1)S(1)} all-to-all(bf16[8,128,512]{2,1,0:T(8,128)(2,1)S(1)} %pad_maximum_fusion.1), channel_id=1, replica_groups={{0,64,256,320,512,576,768,832},{128,192,384,448,640,704,896,960},{1,65,..., dimensions={0} | all-to-all | bytes 2097152 | tf_op jit(solution)/shard_map/all_to_all | solution.py:81
  102.8 0.1 convert_reduce_fusion
  102.9 0.1 select_convert_fusion.1
  103.0 0.1 broadcast_in_dim.58
  103.1 28.9 %all_to_all.21 = bf16[8,64,1024]{2,1,0:T(8,128)(2,1)S(1)} all-to-all(bf16[8,64,1024]{2,1,0:T(8,128)(2,1)S(1)} %broadcast_in_dim.58), channel_id=1, replica_groups={{0,64,256,320,512,576,768,832},{128,192,384,448,640,704,896,960},{1,65,..., dimensions={0} | all-to-all | bytes 2097152 | tf_op jit(solution)/shard_map/all_to_all | solution.py:94
  132.1 0.7 convolution_convert_fusion.3
  132.8 0.0 copy-start.4
  132.8 1.9 %collective-permute-start.3 = (bf16[512,896]{1,0:T(8,128)(2,1)S(1)}, bf16[512,896]{1,0:T(8,128)(2,1)S(1)}, u32[]{:S(2)}, u32[]{:S(2)}) collective-permute-start(bf16[512,896]{1,0:T(8,128)(2,1)S(1)} %convolution_convert_fusion.3), channel_id=1, source_target_pairs={{0,1},{1,0},{2,3},{3,2},{4,5},{5,4},{6,7},{7,6},{8,9},{9,8},{10,11... | collective-permute-start | bytes 2752520 | tf_op jit(solution)/shard_map/ppermute | solution.py:99
  134.8 2.4 %collective-permute-done.3 = bf16[512,896]{1,0:T(8,128)(2,1)S(1)} collective-permute-done((bf16[512,896]{1,0:T(8,128)(2,1)S(1)}, bf16[512,896]{1,0:T(8,128)(2,1)S(1)}, u32[]{:S(2)}, u32[]{:S(2)}) %collective-permute-start.3) | collective-permute-done | bytes 917536 | tf_op jit(solution)/shard_map/ppermute | solution.py:99
  137.2 1.7 fusion.2
  138.9 8.2 %all-to-all-start.3 = ((bf16[64,8,896]{2,1,0:T(8,128)(2,1)}), bf16[64,8,896]{2,1,0:T(8,128)(2,1)S(1)}, u32[]{:S(2)}, u32[]{:S(2)}) async-start(bf16[64,8,896]{2,1,0:T(8,128)(2,1)} %fusion.2), calls=%async_computation.3 | async-start | bytes 1835008 | tf_op jit(solution)/shard_map/all_to_all | solution.py:102
  147.1 0.0 copy-done.4
  147.2 0.0 copy-start.6
  147.2 1.9 %convolution_convert_fusion.2 = bf16[896,512]{1,0:T(8,128)(2,1)S(1)} fusion(bf16[512,896]{1,0:T(8,128)(2,1)} %bitcast.49, bf16[512,1024]{1,0:T(8,128)(2,1)S(1)} %bitcast.45), kind=kOutput, calls=%fused_computation.5 | convolution fusion | flops 470220800 | bytes 2359296 | tf_op jit(solution)/shard_map/dot_general | solution.py:111
  149.1 1.9 %collective-permute-start.4 = (bf16[448,512]{1,0:T(8,128)(2,1)S(1)}, bf16[448,512]{1,0:T(8,128)(2,1)}, u32[]{:S(2)}, u32[]{:S(2)}) collective-permute-start(bf16[448,512]{1,0:T(8,128)(2,1)S(1)} %slice.103), channel_id=1, source_target_pairs={{0,128},{64,192},{128,0},{192,64},{256,384},{320,448},{384,256},{4... | collective-permute-start | bytes 1376264 | tf_op jit(solution)/shard_map/ppermute | solution.py:116
  151.1 0.0 copy-done.6
  151.1 0.7 convolution_convert_fusion.1
  151.7 0.0 copy-start.1
  151.8 3.9 %collective-permute-start.5 = (bf16[448,512]{1,0:T(8,128)(2,1)S(1)}, bf16[448,512]{1,0:T(8,128)(2,1)S(1)}, u32[]{:S(2)}, u32[]{:S(2)}) collective-permute-start(bf16[448,512]{1,0:T(8,128)(2,1)S(1)} %slice.104), channel_id=1, source_target_pairs={{0,128},{64,192},{128,0},{192,64},{256,384},{320,448},{384,256},{4... | collective-permute-start | bytes 1376264 | tf_op jit(solution)/shard_map/ppermute | solution.py:116
  155.7 0.0 copy-done.1
  155.8 21.5 %all-to-all-done.3 = bf16[64,8,896]{2,1,0:T(8,128)(2,1)S(1)} async-done(((bf16[64,8,896]{2,1,0:T(8,128)(2,1)}), bf16[64,8,896]{2,1,0:T(8,128)(2,1)S(1)}, u32[]{:S(2)}, u32[]{:S(2)}) %all-to-all-start.3) | async-done | bytes 917536 | tf_op jit(solution)/shard_map/all_to_all | solution.py:102
  177.3 0.4 fusion.1
  177.6 0.1 slice.105
  177.7 1.9 %collective-permute-start.6 = (bf16[2,64,448]{2,1,0:T(8,128)(2,1)S(1)}, bf16[2,64,448]{2,1,0:T(8,128)(2,1)S(1)}, u32[]{:S(2)}, u32[]{:S(2)}) collective-permute-start(bf16[2,64,448]{2,1,0:T(8,128)(2,1)S(1)} %slice.105), channel_id=1, source_target_pairs={{0,128},{64,192},{128,0},{192,64},{256,384},{320,448},{384,256},{4... | collective-permute-start | bytes 344072 | tf_op jit(solution)/shard_map/ppermute | solution.py:117
  179.7 0.0 collective-permute-done.4
  179.7 0.0 collective-permute-done.5
  179.7 2.4 %select_bitcast_fusion = (bf16[512,448]{0,1:T(8,128)(2,1)}, bf16[448,512]{1,0:T(8,128)(2,1)}) fusion(pred[]{:T(512)S(6)} %eq.75, bf16[448,512]{1,0:T(8,128)(2,1)} %collective-permute-done.4, bf16[896,512]{1,0:T(8,128)(2,1)S(1)} %convolution_convert_fusion.2, bf16[448,512]{1,0:T(8,128)(2,1)S(1)} %collective-permute-done.5, bf16[896,512]{1,0:T(8,128)(2,1)} %copy-done.1), kind=kLoop, calls=%fused_computation.29 | loop fusion | flops 2293760 | bytes 2752513 | tf_op jit(solution)/shard_map/transpose | solution.py:129
  182.1 2.6 %collective-permute-done.6 = bf16[2,64,448]{2,1,0:T(8,128)(2,1)S(1)} collective-permute-done((bf16[2,64,448]{2,1,0:T(8,128)(2,1)S(1)}, bf16[2,64,448]{2,1,0:T(8,128)(2,1)S(1)}, u32[]{:S(2)}, u32[]{:S(2)}) %collective-permute-start.6) | collective-permute-done | bytes 114720 | tf_op jit(solution)/shard_map/ppermute | solution.py:117
  184.7 0.8 broadcast_select_fusion.1
  (13 shorter events, 0.2 us)
Async XLA Ops:
  1.6 31.2 %copy-start.2 = (bf16[448,512]{1,0:T(8,128)(2,1)S(1)}, bf16[448,512]{1,0:T(8,128)(2,1)}, u32[]{:S(2)}) copy-start(bf16[448,512]{1,0:T(8,128)(2,1)} %param.10) | copy-start | bytes 1376260
  1.6 31.2 %copy-start.3 = (bf16[512,448]{0,1:T(8,128)(2,1)S(1)}, bf16[512,448]{0,1:T(8,128)(2,1)}, u32[]{:S(2)}) copy-start(bf16[512,448]{0,1:T(8,128)(2,1)} %param.11) | copy-start | bytes 1376260
  1.7 7.3 %collective-permute-start = (bf16[2,64,448]{2,1,0:T(8,128)(2,1)S(1)}, bf16[2,64,448]{2,1,0:T(8,128)(2,1)S(1)}, u32[]{:S(2)}, u32[]{:S(2)}) collective-permute-start(bf16[2,64,448]{2,1,0:T(8,128)(2,1)S(1)} %pad_maximum_fusion.4), channel_id=1, source_target_pairs={{0,128},{64,192},{128,0},{192,64},{256,384},{320,448},{384,256},{4... | collective-permute-start | bytes 344072 | tf_op jit(solution)/shard_map/ppermute | solution.py:41
  10.3 49.1 %all-to-all-start = ((bf16[64,8,896]{2,1,0:T(8,128)(2,1)}), bf16[64,8,896]{2,1,0:T(8,128)(2,1)S(1)}, u32[]{:S(2)}, u32[]{:S(2)}) async-start(bf16[64,8,896]{2,1,0:T(8,128)(2,1)} %fusion), calls=%async_computation | async-start | bytes 1835008 | tf_op jit(solution)/shard_map/all_to_all | solution.py:66
  33.0 24.2 %collective-permute-start.1 = (bf16[448,1024]{1,0:T(8,128)(2,1)S(1)}, bf16[448,1024]{1,0:T(8,128)(2,1)S(1)}, u32[]{:S(2)}, u32[]{:S(2)}) collective-permute-start(bf16[448,1024]{1,0:T(8,128)(2,1)S(1)} %pad_maximum_fusion.2), channel_id=1, source_target_pairs={{0,128},{64,192},{128,0},{192,64},{256,384},{320,448},{384,256},{4... | collective-permute-start | bytes 2752520 | tf_op jit(solution)/shard_map/ppermute | solution.py:47
  59.5 5.1 %copy-start = (bf16[64,8,896]{2,1,0:T(8,128)(2,1)}, bf16[64,8,896]{2,1,0:T(8,128)(2,1)S(1)}, u32[]{:S(2)}) copy-start(bf16[64,8,896]{2,1,0:T(8,128)(2,1)S(1)} %all-to-all-done) | copy-start | bytes 2752516
  59.5 4.4 %collective-permute-start.2 = (bf16[512,896]{1,0:T(8,128)(2,1)S(1)}, bf16[512,896]{1,0:T(8,128)(2,1)S(1)}, u32[]{:S(2)}, u32[]{:S(2)}) collective-permute-start(bf16[512,896]{1,0:T(8,128)(2,1)S(1)} %bitcast.47), channel_id=1, source_target_pairs={{0,1},{1,0},{2,3},{3,2},{4,5},{5,4},{6,7},{7,6},{8,9},{9,8},{10,11... | collective-permute-start | bytes 2752520 | tf_op jit(solution)/shard_map/ppermute | solution.py:70
  63.8 1.0 copy-start.5
  132.8 14.3 %copy-start.4 = (s32[2,64,1]{1,2,0:T(1,128)S(1)}, s32[2,64,1]{1,2,0:T(1,128)}, u32[]{:S(2)}) copy-start(s32[2,64,1]{1,2,0:T(1,128)} %param.8) | copy-start | bytes 1540
  132.8 4.4 %collective-permute-start.3 = (bf16[512,896]{1,0:T(8,128)(2,1)S(1)}, bf16[512,896]{1,0:T(8,128)(2,1)S(1)}, u32[]{:S(2)}, u32[]{:S(2)}) collective-permute-start(bf16[512,896]{1,0:T(8,128)(2,1)S(1)} %convolution_convert_fusion.3), channel_id=1, source_target_pairs={{0,1},{1,0},{2,3},{3,2},{4,5},{5,4},{6,7},{7,6},{8,9},{9,8},{10,11... | collective-permute-start | bytes 2752520 | tf_op jit(solution)/shard_map/ppermute | solution.py:99
  138.9 38.4 %all-to-all-start.3 = ((bf16[64,8,896]{2,1,0:T(8,128)(2,1)}), bf16[64,8,896]{2,1,0:T(8,128)(2,1)S(1)}, u32[]{:S(2)}, u32[]{:S(2)}) async-start(bf16[64,8,896]{2,1,0:T(8,128)(2,1)} %fusion.2), calls=%async_computation.3 | async-start | bytes 1835008 | tf_op jit(solution)/shard_map/all_to_all | solution.py:102
  147.2 3.9 %copy-start.6 = (bf16[512,896]{1,0:T(8,128)(2,1)S(1)}, bf16[512,896]{1,0:T(8,128)(2,1)}, u32[]{:S(2)}) copy-start(bf16[512,896]{1,0:T(8,128)(2,1)} %copy-done.5) | copy-start | bytes 2752516
  149.1 30.5 %collective-permute-start.4 = (bf16[448,512]{1,0:T(8,128)(2,1)S(1)}, bf16[448,512]{1,0:T(8,128)(2,1)}, u32[]{:S(2)}, u32[]{:S(2)}) collective-permute-start(bf16[448,512]{1,0:T(8,128)(2,1)S(1)} %slice.103), channel_id=1, source_target_pairs={{0,128},{64,192},{128,0},{192,64},{256,384},{320,448},{384,256},{4... | collective-permute-start | bytes 1376264 | tf_op jit(solution)/shard_map/ppermute | solution.py:116
  151.7 4.0 %copy-start.1 = (bf16[896,512]{1,0:T(8,128)(2,1)}, bf16[896,512]{1,0:T(8,128)(2,1)S(1)}, u32[]{:S(2)}) copy-start(bf16[896,512]{1,0:T(8,128)(2,1)S(1)} %convolution_convert_fusion.1) | copy-start | bytes 2752516
  151.8 27.9 %collective-permute-start.5 = (bf16[448,512]{1,0:T(8,128)(2,1)S(1)}, bf16[448,512]{1,0:T(8,128)(2,1)S(1)}, u32[]{:S(2)}, u32[]{:S(2)}) collective-permute-start(bf16[448,512]{1,0:T(8,128)(2,1)S(1)} %slice.104), channel_id=1, source_target_pairs={{0,128},{64,192},{128,0},{192,64},{256,384},{320,448},{384,256},{4... | collective-permute-start | bytes 1376264 | tf_op jit(solution)/shard_map/ppermute | solution.py:116
  177.7 7.0 %collective-permute-start.6 = (bf16[2,64,448]{2,1,0:T(8,128)(2,1)S(1)}, bf16[2,64,448]{2,1,0:T(8,128)(2,1)S(1)}, u32[]{:S(2)}, u32[]{:S(2)}) collective-permute-start(bf16[2,64,448]{2,1,0:T(8,128)(2,1)S(1)} %slice.105), channel_id=1, source_target_pairs={{0,128},{64,192},{128,0},{192,64},{256,384},{320,448},{384,256},{4... | collective-permute-start | bytes 344072 | tf_op jit(solution)/shard_map/ppermute | solution.py:117
